TPU v7x, 256 devices: a whole 4x4x8 slice. The times are simulated.
256 devices in a mesh: lat: 32 (over y_hi, z, core), seg: 8 (over y_lo, x).
Axes of the slice: x: 4, y: 4 (y_hi: 2, y_lo: 2; y = y_hi * 2 + y_lo), z: 8, core: 2. Of those that a mesh axis runs over, the one named last changes fastest.
Arguments:
- atmosphere: float32 [384, 96, 768], P('lat', 'seg'), may hold values from -6 to 6
- cloud_state: float32 [32, 96, 49152], P('lat', None, 'seg'), may hold values from -6 to 6
- channel_lat: int32 [32], P('lat'), may hold values from 0 to 383, as said below
- cell_column: int32 [32, 49152], P('lat', 'seg'), may hold values from 0 to 95, as said below
- channel_wind: float32 [32, 96], P('lat'), may hold values from -0.45 to 0.45
- diffusivity: float32 [96], replicated, may hold values from 0.03 to 0.25
- mixing: float32 [96, 96], replicated, may hold values from -0.625 to 0.625
Outputs:
- next_atmosphere: float32 [384, 96, 768], P('lat', 'seg')
- next_clouds: float32 [32, 96, 49152], P('lat', None, 'seg')
Inputs may be any that keep to these rules, and one draw needn't show every extreme that they name: channel_lat[c] lies in the latitude rows c * 12 to (c + 1) * 12 - 1. `cell_column`: within each segment of 6144 cells of a channel, column numbers never fall and every column holds between half of 64 and three halves of 64 cells; both bounds are reached in every segment.
All inputs are finite; a program needn't handle non-finite values.
Results may differ from a plain program's by a relative error of at most 0.0003.
Values sent between devices are 32-bit elements; how exact they have to be, the bound alone decides.
No kernel may reach another device: no remote copies, remote signals or barrier semaphores. Data moves between devices by JAX's collectives and lax.ppermute only.
A program may use at most 64 MiB of HBM per device.

v0:
```python
import math

import jax
import jax.numpy as jnp
from jax import lax
from jax.sharding import PartitionSpec as P

M = 256
NT = 256
STEPS = 2
SUBSTEPS = 3


RELAXATION = 0.5
MIXING_RATE = 0.3
DAMPING = 0.2
COUPLING = 2.0
HIGHEST = lax.Precision.HIGHEST


def padded_2(block, sides, width):
    for axis, dim in sides:
        count = lax.axis_size(axis)
        forward = [(i, i + 1) for i in range(count - 1)]
        forward.append((count - 1, 0))
        backward = [(target, source) for source, target in forward]
        low = lax.ppermute(
            lax.slice_in_dim(block, block.shape[dim] - width, None, axis=dim), axis, forward
        )
        high = lax.ppermute(lax.slice_in_dim(block, 0, width, axis=dim), axis, backward)
        block = jnp.concatenate([low, block, high], axis=dim)
    return block


def fourier_tables(wavenumbers, longitudes):
    positions = jnp.arange(longitudes, dtype=jnp.int32)
    phase_turns = positions[:, None] * wavenumbers[None, :] % longitudes
    angles = phase_turns.astype(jnp.float32) * (2.0 * math.pi / longitudes)
    waves_pair = jnp.stack((jnp.cos(angles), jnp.sin(angles)), axis=2)
    weights = jnp.where(wavenumbers == 0, 1.0, 2.0).astype(jnp.float32)
    return (waves_pair / longitudes, waves_pair * weights[None, :, None])


def meridian_tables(latitudes, degrees, lat_total):
    phase_turns = degrees[:, None] * (2 * latitudes[None, :] + 1) % (4 * lat_total)
    angles = phase_turns.astype(jnp.float32) * (math.pi / (2.0 * lat_total))
    basis = jnp.cos(angles)
    weights = jnp.where(degrees == 0, 1.0, 2.0).astype(jnp.float32) / lat_total
    return (basis * weights[:, None], jnp.transpose(basis))


def implicit_solve(spectrum, wavenumbers):
    degree_total = spectrum.shape[0]
    degrees = jnp.arange(degree_total, dtype=jnp.int32)
    wave_values = wavenumbers.astype(jnp.float32)
    degree_values = degrees.astype(jnp.float32)
    size_ratio = (
        wave_values[None, :] * wave_values[None, :]
        + degree_values[:, None] * degree_values[:, None]
    ) / (degree_total * degree_total)
    damping_factor = (1.0 + size_ratio * size_ratio)[:, :, None, None]
    coupling_factor = (COUPLING * size_ratio)[:, :, None, None]
    determinant = damping_factor * damping_factor + coupling_factor * coupling_factor
    retained = (wavenumbers[None, :] + degrees[:, None] < degree_total).astype(jnp.float32)[
        :, :, None, None, None
    ]
    shape_full = spectrum.shape
    components = spectrum.reshape(
        shape_full[0], shape_full[1], shape_full[2], shape_full[3] // 3, 3
    )
    vorticity = components[..., 0] / damping_factor
    divergence = (
        damping_factor * components[..., 1] + coupling_factor * components[..., 2]
    ) / determinant
    geopotential = (
        damping_factor * components[..., 2] - coupling_factor * components[..., 1]
    ) / determinant
    return (jnp.stack((vorticity, divergence, geopotential), axis=4) * retained).reshape(shape_full)


def advance(padded, forcing, diffusivity, channel_wind, mixing):
    center = padded[:, :, 1:-1]
    right_cell = padded[:, :, 2:]
    left_cell = padded[:, :, :-2]
    mixed_levels = jnp.einsum("kl,clx->ckx", mixing, center, precision=HIGHEST)
    return (
        center
        + diffusivity[None, :, None] * (right_cell - 2.0 * center + left_cell)
        - 0.5 * channel_wind[:, :, None] * (right_cell - left_cell)
        + MIXING_RATE * mixed_levels
        + forcing
        - DAMPING * jnp.tanh(center)
    )


def shards(atmosphere, cloud_state, channel_lat, cell_column, channel_wind, diffusivity, mixing):
    lat_dev = atmosphere.shape[0]
    pairs_here = atmosphere.shape[1]
    longitudes = atmosphere.shape[2]
    lat_count = lax.axis_size("lat")
    seg_count = lax.axis_size("seg")
    lat_index = lax.axis_index("lat")
    lat_total = lat_dev * lat_count
    columns = longitudes // seg_count
    owned_count = M // lat_count
    degrees = jnp.arange(NT, dtype=jnp.int32)
    forward, inverse = fourier_tables(jnp.arange(M, dtype=jnp.int32), longitudes)
    forward_flat = forward.reshape(longitudes, M * 2)
    inverse_flat = inverse.reshape(longitudes, M * 2)
    owned_waves = lat_index * owned_count + jnp.arange(owned_count, dtype=jnp.int32)
    offsets = channel_lat - lat_index * lat_dev
    onehot = (
        cell_column[:, :, None] == jnp.arange(columns, dtype=jnp.int32)[None, None, :]
    ).astype(jnp.float32)
    counts = jnp.sum(onehot, axis=1)
    to_spec, from_spec = meridian_tables(jnp.arange(lat_total, dtype=jnp.int32), degrees, lat_total)

    def column_mean(values):
        return jnp.einsum("ckx,cxn->ckn", values, onehot, precision=HIGHEST) / counts[:, None, :]

    clouds = cloud_state
    for model_step in range(STEPS):
        channel_rows = jnp.take(atmosphere, offsets, axis=0)
        profile = lax.all_to_all(channel_rows, "seg", split_axis=2, concat_axis=1, tiled=True)
        start_mean = column_mean(clouds)
        forcing = jnp.einsum(
            "ckn,cxn->ckx", RELAXATION * (profile - start_mean), onehot, precision=HIGHEST
        )
        for substep in range(SUBSTEPS):
            padded = padded_2(clouds, (("seg", 2),), 1)
            clouds = advance(padded, forcing, diffusivity, channel_wind, mixing)
        tendency = column_mean(clouds) - start_mean
        returned = lax.all_to_all(tendency, "seg", split_axis=1, concat_axis=2, tiled=True)
        atmosphere = atmosphere.at[offsets].add(returned)
        coeff_rows = jnp.einsum("jkx,xn->jnk", atmosphere, forward_flat, precision=HIGHEST)
        coeff_flat = coeff_rows.reshape(lat_dev, M * 2 * pairs_here)
        gathered = lax.all_to_all(coeff_flat, "lat", split_axis=1, concat_axis=0, tiled=True)
        spectrum = jnp.dot(to_spec, gathered, precision=HIGHEST)
        spectrum = implicit_solve(spectrum.reshape(NT, owned_count, 2, pairs_here), owned_waves)
        back_rows = jnp.dot(
            from_spec, spectrum.reshape(NT, owned_count * 2 * pairs_here), precision=HIGHEST
        )
        restored = lax.all_to_all(back_rows, "lat", split_axis=0, concat_axis=1, tiled=True)
        atmosphere = jnp.einsum(
            "jnk,xn->jkx",
            restored.reshape(lat_dev, M * 2, pairs_here),
            inverse_flat,
            precision=HIGHEST,
        )
    return (atmosphere, clouds)


def solution(mesh):
    placed = (
        P("lat", "seg", None),
        P("lat", None, "seg"),
        P("lat"),
        P("lat", "seg"),
        P("lat", None),
        P(),
        P(),
    )
    return jax.shard_map(
        shards,
        mesh=mesh,
        in_specs=placed,
        out_specs=(P("lat", "seg", None), P("lat", None, "seg")),
        check_vma=False,
    )
```

profile of v0, /device:TPU:32, one launch (start us, length us, event | category | flops | bytes accessed | tf_op | source)
XLA Modules:
  0.0 305.0 jit_solution(11302446731528107870)
XLA Ops:
  4.5 2.5 reduce.11
  8.0 5.3 %all-to-all-start = ((f32[8,1,1152]{2,1,0:T(1,128)}), f32[8,1,1152]{2,1,0:T(1,128)S(1)}, u32[]{:S(2)}, u32[]{:S(2)}) async-start(f32[8,1,1152]{2,1,0:T(1,128)} %reshape.716), calls=%async_computation | async-start | bytes 73728 | tf_op jit(solution)/shard_map/all_to_all | solution.py:124
  13.4 4.1 %collective-permute-start = (f32[1,96,1]{2,1,0:T(8,128)S(1)}, f32[1,96,1]{2,1,0:T(8,128)}, u32[]{:S(2)}, u32[]{:S(2)}) collective-permute-start(f32[1,96,1]{2,1,0:T(8,128)S(1)} %get-tuple-element.48), channel_id=1, source_target_pairs={{1,0},{2,1},{3,2},{4,3},{5,4},{6,5},{7,6},{0,7},{9,8},{10,9},{11,1... | collective-permute-start | bytes 1160 | tf_op jit(solution)/shard_map/ppermute | solution.py:30
  18.0 3.2 %fusion.89 = (f32[768,256,1]{1,0,2:T(8,128)S(1)}, f32[768,256,1]{1,0,2:T(8,128)S(1)}) fusion(), kind=kLoop, calls=%fused_computation.79 | loop fusion | flops 1769472 | bytes 1572864 | tf_op jit(solution)/shard_map/sin | solution.py:39
  27.4 2.3 convolution_bitcast_fusion.1
  29.7 4.3 %multiply_subtract_fusion.5 = f32[1,96,6144]{2,1,0:T(8,128)S(1)} fusion(f32[1,96,6144]{2,1,0:T(8,128)S(1)} %copy-done.5, f32[1,96,6144]{2,1,0:T(8,128)S(1)} %convolution_bitcast_fusion.1, f32[1,96,1]{2,1,0:T(8,128)} %collective-permute-done.1, f32[1,96,1]{2,1,0:T(8,128)} %collective-permute-done, f32[96,96]{1,0:T(8,128)S(1)} %copy-done, ...), kind=kOutput, calls=%fused_computation.44 | convolution fusion | flops 688324608 | bytes 7116288 | tf_op jit(solution)/shard_map/kl,clx->ckx/dot_general | solution.py:85
  34.1 4.3 %collective-permute-start.2 = (f32[1,96,1]{2,1,0:T(8,128)S(1)}, f32[1,96,1]{2,1,0:T(8,128)S(1)}, u32[]{:S(2)}, u32[]{:S(2)}) collective-permute-start(f32[1,96,1]{2,1,0:T(8,128)S(1)} %get-tuple-element.46), channel_id=1, source_target_pairs={{1,0},{2,1},{3,2},{4,3},{5,4},{6,5},{7,6},{0,7},{9,8},{10,9},{11,1... | collective-permute-start | bytes 1160 | tf_op jit(solution)/shard_map/ppermute | solution.py:30
  38.4 2.3 fusion.94
  40.7 3.9 %collective-permute-done.3 = f32[1,96,1]{2,1,0:T(8,128)S(1)} collective-permute-done((f32[1,96,1]{2,1,0:T(8,128)S(1)}, f32[1,96,1]{2,1,0:T(8,128)S(1)}, u32[]{:S(2)}, u32[]{:S(2)}) %collective-permute-start.3) | collective-permute-done | bytes 416 | tf_op jit(solution)/shard_map/ppermute | solution.py:27
  44.6 3.3 %multiply_subtract_fusion.4 = f32[1,96,6144]{2,1,0:T(8,128)S(1)} fusion(f32[1,96,6144]{2,1,0:T(8,128)S(1)} %multiply_subtract_fusion.5, f32[1,96,6144]{2,1,0:T(8,128)S(1)} %convolution_bitcast_fusion.1, f32[1,96,1]{2,1,0:T(8,128)S(1)} %collective-permute-done.3, f32[1,96,1]{2,1,0:T(8,128)S(1)} %collective-permute-done.2, f32[96,96]{1,0:T(8,128)S(1)} %copy-done, ...), kind=kOutput, calls=%fused_computation.43 | convolution fusion | flops 688324608 | bytes 7116288 | tf_op jit(solution)/shard_map/kl,clx->ckx/dot_general | solution.py:85
  52.1 2.4 collective-permute-done.5
  54.5 8.2 %multiply_subtract_fusion.3 = f32[1,96,6144]{2,1,0:T(8,128)S(1)} fusion(f32[1,96,6144]{2,1,0:T(8,128)} %copy-done.13, f32[1,96,6144]{2,1,0:T(8,128)} %copy-done.9, f32[1,96,1]{2,1,0:T(8,128)S(1)} %collective-permute-done.5, f32[1,96,1]{2,1,0:T(8,128)S(1)} %collective-permute-done.4, f32[96,96]{1,0:T(8,128)S(1)} %copy-done, f32[96]{0:T(128)S(1)} %multiply_bitcast_fusion, ...), kind=kOutput, calls=%fused_computation.42 | convolution fusion | flops 688324608 | bytes 7116288 | tf_op jit(solution)/shard_map/kl,clx->ckx/dot_general | solution.py:85
  66.4 3.6 %all-to-all-start.1 = ((f32[1,96,96]{2,0,1:T(1,128)}), f32[1,96,96]{2,0,1:T(1,128)S(1)}, u32[]{:S(2)}, u32[]{:S(2)}) async-start(f32[1,96,96]{2,0,1:T(1,128)} %copy.126), calls=%async_computation.1 | async-start | bytes 98304 | tf_op jit(solution)/shard_map/all_to_all | solution.py:133
  70.0 2.2 copy.121
  72.2 2.4 div.102
  76.3 2.1 fusion.126
  78.3 3.6 %fusion.37 = f32[12,512,12]{1,2,0:T(8,128)} fusion(f32[12,12,768]{2,1,0:T(8,128)} %fusion.126, f32[768,512]{0,1:T(8,128)S(1)} %div.102), kind=kOutput, calls=%fused_computation.63 | convolution fusion | flops 679477248 | bytes 2310144 | tf_op jit(solution)/shard_map/jkx,xn->jnk/dot_general | solution.py:135
  81.9 3.1 %copy.130 = f32[12,512,12]{2,1,0:T(8,128)} copy(f32[12,512,12]{1,2,0:T(8,128)} %fusion.37) | data formatting | bytes 589824 | tf_op jit(solution)/shard_map/jkx,xn->jnk/transpose | solution.py:135
  85.0 3.7 %all_to_all.103 = f32[12,32,192]{2,1,0:T(8,128)} reshape(f32[12,512,12]{2,1,0:T(8,128)} %copy.130) | data formatting | bytes 589824 | tf_op jit(solution)/shard_map/all_to_all | solution.py:137
  90.7 11.1 %all-to-all-start.2 = ((f32[12,32,192]{2,0,1:T(8,128)}), f32[12,32,192]{2,0,1:T(8,128)}, u32[]{:S(2)}, u32[]{:S(2)}) async-start(f32[12,32,192]{2,0,1:T(8,128)} %copy.131), calls=%async_computation.2 | async-start | bytes 1048576 | tf_op jit(solution)/shard_map/all_to_all | solution.py:137
  103.9 17.3 %all-to-all-done.2 = f32[12,32,192]{2,0,1:T(8,128)} async-done(((f32[12,32,192]{2,0,1:T(8,128)}), f32[12,32,192]{2,0,1:T(8,128)}, u32[]{:S(2)}, u32[]{:S(2)}) %all-to-all-start.2) | async-done | bytes 294944 | tf_op jit(solution)/shard_map/all_to_all | solution.py:137
  125.0 3.2 %fusion.104 = f32[256,8,2,4,3]{0,1,4,3,2:T(8,128)S(1)} fusion(f32[8,2,4,3,384]{4,3,2,1,0:T(4,128)} %dot_general.79, f32[256]{0:T(256)} %get-tuple-element.62, s32[384]{0:T(512)S(1)} %multiply_add_fusion.1), kind=kOutput, calls=%fused_computation.97 | convolution fusion | flops 227475456 | bytes 494080 | tf_op jit(solution)/shard_map/dot_general | solution.py:138
  131.9 5.7 %all-to-all-start.3 = ((f32[32,12,192]{2,1,0:T(8,128)}), f32[32,12,192]{2,1,0:T(8,128)}, u32[]{:S(2)}, u32[]{:S(2)}) async-start(f32[32,12,192]{2,1,0:T(8,128)} %copy.136), calls=%async_computation.3 | async-start | bytes 1048576 | tf_op jit(solution)/shard_map/all_to_all | solution.py:143
  137.6 2.2 copy.138
  139.8 2.4 mul.577
  142.2 14.7 %all-to-all-done.3 = f32[32,12,192]{2,1,0:T(8,128)} async-done(((f32[32,12,192]{2,1,0:T(8,128)}), f32[32,12,192]{2,1,0:T(8,128)}, u32[]{:S(2)}, u32[]{:S(2)}) %all-to-all-start.3) | async-done | bytes 294944 | tf_op jit(solution)/shard_map/all_to_all | solution.py:143
  158.9 3.9 %reshape.660 = f32[12,512,12]{2,1,0:T(8,128)} reshape(f32[12,32,192]{2,1,0:T(8,128)} %copy.137) | data formatting | bytes 589824 | tf_op jit(solution)/shard_map/reshape | solution.py:146
  162.7 7.2 %fusion.24 = f32[12,12,768]{2,1,0:T(8,128)S(1)} fusion(f32[12,512,12]{2,1,0:T(8,128)} %reshape.660, f32[768,512]{0,1:T(8,128)S(1)} %mul.577), kind=kOutput, calls=%fused_computation.52 | convolution fusion | flops 679477248 | bytes 2310144 | tf_op jit(solution)/shard_map/jnk,xn->jkx/dot_general | solution.py:144
  171.7 3.3 %reduce.13 = f32[768,12]{1,0:T(8,128)} reduce(f32[768,1,12]{2,1,0:T(1,128)} %bitcast.202, f32[]{:T(128)} %broadcast.592), dimensions={1}, to_apply=%bitcast.181.reduce_sub_computation | reduce | bytes 73732
  176.9 3.4 %all-to-all-start.4 = ((f32[8,1,1152]{2,1,0:T(1,128)}), f32[8,1,1152]{2,1,0:T(1,128)S(1)}, u32[]{:S(2)}, u32[]{:S(2)}) async-start(f32[8,1,1152]{2,1,0:T(1,128)} %reshape.718), calls=%async_computation.4 | async-start | bytes 73728 | tf_op jit(solution)/shard_map/all_to_all | solution.py:124
  181.3 4.2 %collective-permute-start.6 = (f32[1,96,1]{2,1,0:T(8,128)S(1)}, f32[1,96,1]{2,1,0:T(8,128)}, u32[]{:S(2)}, u32[]{:S(2)}) collective-permute-start(f32[1,96,1]{2,1,0:T(8,128)S(1)} %get-tuple-element.42), channel_id=1, source_target_pairs={{1,0},{2,1},{3,2},{4,3},{5,4},{6,5},{7,6},{0,7},{9,8},{10,9},{11,1... | collective-permute-start | bytes 1160 | tf_op jit(solution)/shard_map/ppermute | solution.py:30
  190.0 2.3 convolution_bitcast_fusion
  192.3 4.2 %multiply_subtract_fusion.2 = f32[1,96,6144]{2,1,0:T(8,128)S(1)} fusion(f32[1,96,6144]{2,1,0:T(8,128)S(1)} %copy-done.7, f32[1,96,6144]{2,1,0:T(8,128)S(1)} %convolution_bitcast_fusion, f32[1,96,1]{2,1,0:T(8,128)} %collective-permute-done.7, f32[1,96,1]{2,1,0:T(8,128)} %collective-permute-done.6, f32[96,96]{1,0:T(8,128)S(1)} %copy-done, ...), kind=kOutput, calls=%fused_computation.41 | convolution fusion | flops 688324608 | bytes 7116288 | tf_op jit(solution)/shard_map/kl,clx->ckx/dot_general | solution.py:85
  196.6 3.1 %collective-permute-start.8 = (f32[1,96,1]{2,1,0:T(8,128)S(1)}, f32[1,96,1]{2,1,0:T(8,128)S(1)}, u32[]{:S(2)}, u32[]{:S(2)}) collective-permute-start(f32[1,96,1]{2,1,0:T(8,128)S(1)} %get-tuple-element.40), channel_id=1, source_target_pairs={{1,0},{2,1},{3,2},{4,3},{5,4},{6,5},{7,6},{0,7},{9,8},{10,9},{11,1... | collective-permute-start | bytes 1160 | tf_op jit(solution)/shard_map/ppermute | solution.py:30
  201.4 4.4 %collective-permute-done.9 = f32[1,96,1]{2,1,0:T(8,128)S(1)} collective-permute-done((f32[1,96,1]{2,1,0:T(8,128)S(1)}, f32[1,96,1]{2,1,0:T(8,128)S(1)}, u32[]{:S(2)}, u32[]{:S(2)}) %collective-permute-start.9) | collective-permute-done | bytes 416 | tf_op jit(solution)/shard_map/ppermute | solution.py:27
  205.9 3.3 %multiply_subtract_fusion.1 = f32[1,96,6144]{2,1,0:T(8,128)S(1)} fusion(f32[1,96,6144]{2,1,0:T(8,128)S(1)} %multiply_subtract_fusion.2, f32[1,96,6144]{2,1,0:T(8,128)S(1)} %convolution_bitcast_fusion, f32[1,96,1]{2,1,0:T(8,128)S(1)} %collective-permute-done.9, f32[1,96,1]{2,1,0:T(8,128)S(1)} %collective-permute-done.8, f32[96,96]{1,0:T(8,128)S(1)} %copy-done, ...), kind=kOutput, calls=%fused_computation.40 | convolution fusion | flops 688324608 | bytes 7116288 | tf_op jit(solution)/shard_map/kl,clx->ckx/dot_general | solution.py:85
  209.4 2.2 collective-permute-start.11
  213.4 2.4 collective-permute-done.11
  215.8 3.3 %multiply_subtract_fusion = f32[1,96,6144]{2,1,0:T(8,128)S(1)} fusion(f32[1,96,6144]{2,1,0:T(8,128)S(1)} %multiply_subtract_fusion.1, f32[1,96,6144]{2,1,0:T(8,128)S(1)} %convolution_bitcast_fusion, f32[1,96,1]{2,1,0:T(8,128)S(1)} %collective-permute-done.11, f32[1,96,1]{2,1,0:T(8,128)S(1)} %collective-permute-done.10, f32[96,96]{1,0:T(8,128)S(1)} %copy-done, ...), kind=kOutput, calls=%fused_computation.39 | convolution fusion | flops 688324608 | bytes 7116288 | tf_op jit(solution)/shard_map/kl,clx->ckx/dot_general | solution.py:85
  222.3 8.7 %all_to_all.130 = f32[1,96,96]{2,0,1:T(1,128)S(1)} all-to-all(f32[1,96,96]{2,0,1:T(1,128)S(1)} %copy.146), channel_id=1, replica_groups=mesh['lat'=32,'seg'=8] {'seg'}, dimensions={1} | all-to-all | bytes 73728 | tf_op jit(solution)/shard_map/all_to_all | solution.py:133
  233.1 3.6 %fusion.34 = f32[12,512,12]{1,2,0:T(8,128)} fusion(f32[12,12,768]{2,1,0:T(8,128)} %fusion.127, f32[768,512]{0,1:T(8,128)S(1)} %div.102), kind=kOutput, calls=%fused_computation.62 | convolution fusion | flops 679477248 | bytes 2310144 | tf_op jit(solution)/shard_map/jkx,xn->jnk/dot_general | solution.py:135
  236.6 3.1 %copy.150 = f32[12,512,12]{2,1,0:T(8,128)} copy(f32[12,512,12]{1,2,0:T(8,128)} %fusion.34) | data formatting | bytes 589824 | tf_op jit(solution)/shard_map/jkx,xn->jnk/transpose | solution.py:135
  239.7 3.0 all_to_all.116
  243.0 23.3 %all_to_all.131 = f32[12,32,192]{2,0,1:T(8,128)S(1)} all-to-all(f32[12,32,192]{2,0,1:T(8,128)S(1)} %copy.151), channel_id=1, replica_groups=mesh['lat'=32,'seg'=8] {'lat'}, dimensions={1} | all-to-all | bytes 589824 | tf_op jit(solution)/shard_map/all_to_all | solution.py:137
  266.6 2.2 fusion.102
  270.0 23.0 %all_to_all.132 = f32[32,12,192]{2,1,0:T(8,128)S(1)} all-to-all(f32[32,12,192]{2,1,0:T(8,128)S(1)} %copy.156), channel_id=1, replica_groups=mesh['lat'=32,'seg'=8] {'lat'}, dimensions={0} | all-to-all | bytes 589824 | tf_op jit(solution)/shard_map/all_to_all | solution.py:143
  293.3 3.5 %reshape.665 = f32[12,512,12]{2,1,0:T(8,128)} reshape(f32[12,32,192]{2,1,0:T(8,128)S(1)} %copy.157) | data formatting | bytes 589824 | tf_op jit(solution)/shard_map/reshape | solution.py:146
  296.8 8.0 %fusion.22 = f32[12,12,768]{2,1,0:T(8,128)} fusion(f32[12,512,12]{2,1,0:T(8,128)} %reshape.665, f32[768,512]{0,1:T(8,128)S(1)} %mul.577), kind=kOutput, calls=%fused_computation.50 | convolution fusion | flops 679477248 | bytes 2310144 | tf_op jit(solution)/shard_map/jnk,xn->jkx/dot_general | solution.py:144
  (131 shorter events, 54.1 us)
Async XLA Ops:
  0.6 29.1 %copy-start = (f32[96,96]{1,0:T(8,128)S(1)}, f32[96,96]{1,0:T(8,128)}, u32[]{:S(2)}) copy-start(f32[96,96]{1,0:T(8,128)} %param.19) | copy-start | bytes 110596
  0.6 12.6 %copy-start.4 = (f32[1,96,6144]{2,1,0:T(8,128)S(1)}, f32[1,96,6144]{2,1,0:T(8,128)}, u32[]{:S(2)}) copy-start(f32[1,96,6144]{2,1,0:T(8,128)} %param.14) | copy-start | bytes 7077892
  1.9 21.8 %copy-start.2 = (f32[12,12,768]{2,1,0:T(8,128)}, f32[12,12,768]{2,1,0:T(8,128)S(1)}, u32[]{:S(2)}) copy-start(f32[12,12,768]{2,1,0:T(8,128)S(1)} %copy.187) | copy-start | bytes 1327108
  1.9 19.9 %copy-start.10 = (s32[1,6144]{1,0:T(1,128)S(1)}, s32[1,6144]{1,0:T(1,128)}, u32[]{:S(2)}) copy-start(s32[1,6144]{1,0:T(1,128)} %param.16) | copy-start | bytes 73732
  7.0 16.7 %copy-start.16 = (f32[1,96]{1,0:T(1,128)S(1)}, f32[1,96]{1,0:T(1,128)}, u32[]{:S(2)}) copy-start(f32[1,96]{1,0:T(1,128)} %param.17) | copy-start | bytes 1156
  8.0 16.1 %all-to-all-start = ((f32[8,1,1152]{2,1,0:T(1,128)}), f32[8,1,1152]{2,1,0:T(1,128)S(1)}, u32[]{:S(2)}, u32[]{:S(2)}) async-start(f32[8,1,1152]{2,1,0:T(1,128)} %reshape.716), calls=%async_computation | async-start | bytes 73728 | tf_op jit(solution)/shard_map/all_to_all | solution.py:124
  13.4 16.3 %collective-permute-start = (f32[1,96,1]{2,1,0:T(8,128)S(1)}, f32[1,96,1]{2,1,0:T(8,128)}, u32[]{:S(2)}, u32[]{:S(2)}) collective-permute-start(f32[1,96,1]{2,1,0:T(8,128)S(1)} %get-tuple-element.48), channel_id=1, source_target_pairs={{1,0},{2,1},{3,2},{4,3},{5,4},{6,5},{7,6},{0,7},{9,8},{10,9},{11,1... | collective-permute-start | bytes 1160 | tf_op jit(solution)/shard_map/ppermute | solution.py:30
  17.5 12.2 %collective-permute-start.1 = (f32[1,96,1]{2,1,0:T(8,128)S(1)}, f32[1,96,1]{2,1,0:T(8,128)}, u32[]{:S(2)}, u32[]{:S(2)}) collective-permute-start(f32[1,96,1]{2,1,0:T(8,128)S(1)} %get-tuple-element.49), channel_id=1, source_target_pairs={{0,1},{1,2},{2,3},{3,4},{4,5},{5,6},{6,7},{7,0},{8,9},{9,10},{10,1... | collective-permute-start | bytes 1160 | tf_op jit(solution)/shard_map/ppermute | solution.py:27
  23.7 30.8 %copy-start.19 = (f32[96]{0:T(128)}, f32[96]{0:T(128)S(1)}, u32[]{:S(2)}) copy-start(f32[96]{0:T(128)S(1)} %multiply_bitcast_fusion) | copy-start | bytes 1156
  24.0 5.7 %copy-start.17 = (f32[96]{0:T(128)S(1)}, f32[96]{0:T(128)}, u32[]{:S(2)}) copy-start(f32[96]{0:T(128)} %param.18) | copy-start | bytes 1156
  27.4 2.3 copy-start.5
  29.7 14.9 %copy-start.9 = (f32[1,96,6144]{2,1,0:T(8,128)}, f32[1,96,6144]{2,1,0:T(8,128)S(1)}, u32[]{:S(2)}) copy-start(f32[1,96,6144]{2,1,0:T(8,128)S(1)} %convolution_bitcast_fusion.1) | copy-start | bytes 7077892
  34.1 6.6 %collective-permute-start.2 = (f32[1,96,1]{2,1,0:T(8,128)S(1)}, f32[1,96,1]{2,1,0:T(8,128)S(1)}, u32[]{:S(2)}, u32[]{:S(2)}) collective-permute-start(f32[1,96,1]{2,1,0:T(8,128)S(1)} %get-tuple-element.46), channel_id=1, source_target_pairs={{1,0},{2,1},{3,2},{4,3},{5,4},{6,5},{7,6},{0,7},{9,8},{10,9},{11,1... | collective-permute-start | bytes 1160 | tf_op jit(solution)/shard_map/ppermute | solution.py:30
  38.4 6.2 %collective-permute-start.3 = (f32[1,96,1]{2,1,0:T(8,128)S(1)}, f32[1,96,1]{2,1,0:T(8,128)S(1)}, u32[]{:S(2)}, u32[]{:S(2)}) collective-permute-start(f32[1,96,1]{2,1,0:T(8,128)S(1)} %get-tuple-element.47), channel_id=1, source_target_pairs={{0,1},{1,2},{2,3},{3,4},{4,5},{5,6},{6,7},{7,0},{8,9},{9,10},{10,1... | collective-permute-start | bytes 1160 | tf_op jit(solution)/shard_map/ppermute | solution.py:27
  40.7 9.4 %copy-start.15 = (s32[3]{0:T(128)S(1)}, s32[3]{0:T(128)}, u32[]{:S(2)}) copy-start(s32[3]{0:T(128)} %constant.118.clone.1) | copy-start | bytes 40
  47.9 2.1 copy-start.13
  48.0 4.1 %collective-permute-start.4 = (f32[1,96,1]{2,1,0:T(8,128)S(1)}, f32[1,96,1]{2,1,0:T(8,128)S(1)}, u32[]{:S(2)}, u32[]{:S(2)}) collective-permute-start(f32[1,96,1]{2,1,0:T(8,128)S(1)} %get-tuple-element.44), channel_id=1, source_target_pairs={{1,0},{2,1},{3,2},{4,3},{5,4},{6,5},{7,6},{0,7},{9,8},{10,9},{11,1... | collective-permute-start | bytes 1160 | tf_op jit(solution)/shard_map/ppermute | solution.py:30
  48.3 6.2 %collective-permute-start.5 = (f32[1,96,1]{2,1,0:T(8,128)S(1)}, f32[1,96,1]{2,1,0:T(8,128)S(1)}, u32[]{:S(2)}, u32[]{:S(2)}) collective-permute-start(f32[1,96,1]{2,1,0:T(8,128)S(1)} %get-tuple-element.45), channel_id=1, source_target_pairs={{0,1},{1,2},{2,3},{3,4},{4,5},{5,6},{6,7},{7,0},{8,9},{9,10},{10,1... | collective-permute-start | bytes 1160 | tf_op jit(solution)/shard_map/ppermute | solution.py:27
  62.7 1.4 copy-start.6
  65.7 8.9 %copy-start.11 = (f32[96,96]{0,1:T(8,128)}, f32[96,96]{0,1:T(8,128)S(1)}, u32[]{:S(2)}) copy-start(f32[96,96]{0,1:T(8,128)S(1)} %fusion.65) | copy-start | bytes 110596
  66.4 9.8 %all-to-all-start.1 = ((f32[1,96,96]{2,0,1:T(1,128)}), f32[1,96,96]{2,0,1:T(1,128)S(1)}, u32[]{:S(2)}, u32[]{:S(2)}) async-start(f32[1,96,96]{2,0,1:T(1,128)} %copy.126), calls=%async_computation.1 | async-start | bytes 98304 | tf_op jit(solution)/shard_map/all_to_all | solution.py:133
  90.7 30.4 %all-to-all-start.2 = ((f32[12,32,192]{2,0,1:T(8,128)}), f32[12,32,192]{2,0,1:T(8,128)}, u32[]{:S(2)}, u32[]{:S(2)}) async-start(f32[12,32,192]{2,0,1:T(8,128)} %copy.131), calls=%async_computation.2 | async-start | bytes 1048576 | tf_op jit(solution)/shard_map/all_to_all | solution.py:137
  131.9 24.9 %all-to-all-start.3 = ((f32[32,12,192]{2,1,0:T(8,128)}), f32[32,12,192]{2,1,0:T(8,128)}, u32[]{:S(2)}, u32[]{:S(2)}) async-start(f32[32,12,192]{2,1,0:T(8,128)} %copy.136), calls=%async_computation.3 | async-start | bytes 1048576 | tf_op jit(solution)/shard_map/all_to_all | solution.py:143
  169.9 0.8 copy-start.3
  170.7 19.3 %copy-start.12 = (f32[96,96]{0,1:T(8,128)S(1)}, f32[96,96]{0,1:T(8,128)}, u32[]{:S(2)}) copy-start(f32[96,96]{0,1:T(8,128)} %copy-done.11) | copy-start | bytes 110596
  175.0 17.3 %copy-start.18 = (f32[96]{0:T(128)S(1)}, f32[96]{0:T(128)}, u32[]{:S(2)}) copy-start(f32[96]{0:T(128)} %param.18) | copy-start | bytes 1156
  175.0 17.3 %copy-start.20 = (f32[96]{0:T(128)S(1)}, f32[96]{0:T(128)}, u32[]{:S(2)}) copy-start(f32[96]{0:T(128)} %copy-done.19) | copy-start | bytes 1156
  176.9 9.7 %all-to-all-start.4 = ((f32[8,1,1152]{2,1,0:T(1,128)}), f32[8,1,1152]{2,1,0:T(1,128)S(1)}, u32[]{:S(2)}, u32[]{:S(2)}) async-start(f32[8,1,1152]{2,1,0:T(1,128)} %reshape.718), calls=%async_computation.4 | async-start | bytes 73728 | tf_op jit(solution)/shard_map/all_to_all | solution.py:124
  181.3 11.0 %collective-permute-start.6 = (f32[1,96,1]{2,1,0:T(8,128)S(1)}, f32[1,96,1]{2,1,0:T(8,128)}, u32[]{:S(2)}, u32[]{:S(2)}) collective-permute-start(f32[1,96,1]{2,1,0:T(8,128)S(1)} %get-tuple-element.42), channel_id=1, source_target_pairs={{1,0},{2,1},{3,2},{4,3},{5,4},{6,5},{7,6},{0,7},{9,8},{10,9},{11,1... | collective-permute-start | bytes 1160 | tf_op jit(solution)/shard_map/ppermute | solution.py:30
  185.4 6.9 %collective-permute-start.7 = (f32[1,96,1]{2,1,0:T(8,128)S(1)}, f32[1,96,1]{2,1,0:T(8,128)}, u32[]{:S(2)}, u32[]{:S(2)}) collective-permute-start(f32[1,96,1]{2,1,0:T(8,128)S(1)} %get-tuple-element.43), channel_id=1, source_target_pairs={{0,1},{1,2},{2,3},{3,4},{4,5},{5,6},{6,7},{7,0},{8,9},{9,10},{10,1... | collective-permute-start | bytes 1160 | tf_op jit(solution)/shard_map/ppermute | solution.py:27
  190.0 2.3 copy-start.7
  196.6 4.9 %collective-permute-start.8 = (f32[1,96,1]{2,1,0:T(8,128)S(1)}, f32[1,96,1]{2,1,0:T(8,128)S(1)}, u32[]{:S(2)}, u32[]{:S(2)}) collective-permute-start(f32[1,96,1]{2,1,0:T(8,128)S(1)} %get-tuple-element.40), channel_id=1, source_target_pairs={{1,0},{2,1},{3,2},{4,3},{5,4},{6,5},{7,6},{0,7},{9,8},{10,9},{11,1... | collective-permute-start | bytes 1160 | tf_op jit(solution)/shard_map/ppermute | solution.py:30
  199.7 6.2 %collective-permute-start.9 = (f32[1,96,1]{2,1,0:T(8,128)S(1)}, f32[1,96,1]{2,1,0:T(8,128)S(1)}, u32[]{:S(2)}, u32[]{:S(2)}) collective-permute-start(f32[1,96,1]{2,1,0:T(8,128)S(1)} %get-tuple-element.41), channel_id=1, source_target_pairs={{0,1},{1,2},{2,3},{3,4},{4,5},{5,6},{6,7},{7,0},{8,9},{9,10},{10,1... | collective-permute-start | bytes 1160 | tf_op jit(solution)/shard_map/ppermute | solution.py:27
  209.3 4.1 %collective-permute-start.10 = (f32[1,96,1]{2,1,0:T(8,128)S(1)}, f32[1,96,1]{2,1,0:T(8,128)S(1)}, u32[]{:S(2)}, u32[]{:S(2)}) collective-permute-start(f32[1,96,1]{2,1,0:T(8,128)S(1)} %get-tuple-element.38), channel_id=1, source_target_pairs={{1,0},{2,1},{3,2},{4,3},{5,4},{6,5},{7,6},{0,7},{9,8},{10,9},{11,1... | collective-permute-start | bytes 1160 | tf_op jit(solution)/shard_map/ppermute | solution.py:30
  209.4 6.5 %collective-permute-start.11 = (f32[1,96,1]{2,1,0:T(8,128)S(1)}, f32[1,96,1]{2,1,0:T(8,128)S(1)}, u32[]{:S(2)}, u32[]{:S(2)}) collective-permute-start(f32[1,96,1]{2,1,0:T(8,128)S(1)} %get-tuple-element.39), channel_id=1, source_target_pairs={{0,1},{1,2},{2,3},{3,4},{4,5},{5,6},{6,7},{7,0},{8,9},{9,10},{10,1... | collective-permute-start | bytes 1160 | tf_op jit(solution)/shard_map/ppermute | solution.py:27
  219.2 1.4 copy-start.8
  242.7 23.9 %copy-start.14 = (f32[256]{0:T(256)S(1)}, f32[256]{0:T(256)}, u32[]{:S(2)}) copy-start(f32[256]{0:T(256)} %get-tuple-element.62) | copy-start | bytes 3076
  266.3 2.8 copy-start.1
where the time goes:
time: 310 us; the launch traced here: 305 us
  matrix products  65.8 us (21%)
  local copies, waits for them, and re-layouts  59.4 us (19%)
  blocking collectives  55 us (18%)
  waiting for transfers between devices  52.8 us (17%)
  starting transfers between devices  49.8 us (16%)
  other arithmetic  20 us (6%)
    dot_general x6, matrix products, advance(): mixed_levels = jnp.einsum('kl,clx->ckx', mixing, center, precision=HIGHEST)  26.6 us
    all_to_all x1, blocking collectives, shards(): lax.all_to_all(coeff_flat, 'lat', split_axis=1, concat_axis=0, tiled=True)  23.3 us
    all_to_all x1, blocking collectives, shards(): lax.all_to_all(back_rows, 'lat', split_axis=0, concat_axis=1, tiled=True)  23 us
    all_to_all x1, waiting for transfers between devices, shards(): lax.all_to_all(coeff_flat, 'lat', split_axis=1, concat_axis=0, tiled=True)  17.3 us
    ppermute x6, starting transfers between devices, padded_2(): lax.ppermute(lax.slice_in_dim(block, 0, width, axis=dim), axis, backward)  16.1 us
    dot_general x2, matrix products, shards(): jnp.einsum('jnk,xn->jkx', restored.reshape(lat_dev, M * 2, pairs_here), i...  15.1 us
    all_to_all x1, waiting for transfers between devices, shards(): lax.all_to_all(back_rows, 'lat', split_axis=0, concat_axis=1, tiled=True)  14.7 us
    ppermute x6, waiting for transfers between devices, padded_2(): lax.ppermute(lax.slice_in_dim(block, block.shape[dim] - width, None, axis...  13.1 us
  transfers between devices with their start and end apart: 17, of which 11 were waited for; matrix products, arithmetic and copies ran while one was open for 11% of the time, Pallas kernels for 0%

commit v1 on v0

v1 whole, which is shorter than its diff:
```python
import numpy as np

import jax
import jax.numpy as jnp
from jax import lax
from jax.experimental import pallas as pl
from jax.experimental.pallas import tpu as pltpu
from jax.sharding import PartitionSpec as P

NLON = 768
M = 256
NT = 256
NLAT = 384
LAT_DEV = 12
K = 96
KD = 12
COLS = 96
CELLS = 6144
LATS = 32
SEGS = 8
TILE = 256
EXT = CELLS + 512
RELAXATION = 0.5
MIXING_RATE = 0.3
DAMPING = 0.2
COUPLING = 2.0
F32 = jnp.float32
BF16 = jnp.bfloat16
HIGHEST = lax.Precision.HIGHEST
HIGH = lax.Precision.HIGH

CHIP_GROUPS = [[16 * q + i for i in range(16)] for q in range(16)]
ROW_GROUPS = [[2 * q + b for q in range(16)] for b in range(2)]
CORE_SWAP = [(i, i ^ 1) for i in range(LATS)]


def tables():
    m = np.arange(M)
    x = np.arange(NLON)
    angles = 2.0 * np.pi * ((m[:, None] * x[None, :]) % NLON) / NLON
    waves = np.stack([np.cos(angles), np.sin(angles)])
    sigma = np.where(m == 0, 1.0, 2.0)
    inverse = (waves * sigma[None, :, None]).reshape(2 * M, NLON)
    forward = (waves / NLON).reshape(2 * M, NLON).T
    forward_seg = np.zeros((SEGS, 128, 2 * M))
    forward_seg[:, :COLS] = forward.reshape(SEGS, COLS, 2 * M)
    inverse_seg = np.zeros((2 * M, SEGS, 128))
    for s in range(SEGS):
        inverse_seg[:, s, : COLS + 1] = inverse[:, (COLS * s + np.arange(COLS + 1)) % NLON]
        inverse_seg[:, s, COLS + 1] = inverse[:, (COLS * s - 1) % NLON]
    n = np.arange(NT)
    j = np.arange(NLAT)
    basis = np.cos(np.pi * ((n[:, None] * (2 * j[None, :] + 1)) % (4 * NLAT)) / (2 * NLAT))
    weights = np.where(n == 0, 1.0, 2.0) / NLAT
    size = (m[None, :] ** 2 + n[:, None] ** 2) / (NT * NT)
    damping = 1.0 + size * size
    coupling = COUPLING * size
    det = damping**2 + coupling**2
    keep = (m[None, :] + n[:, None] < NT).astype(np.float64)
    update = np.stack([keep / damping, keep * damping / det, keep * coupling / det])
    row_weights = np.transpose(update * weights[None, :, None], (1, 0, 2)).reshape(NT, 3 * M)
    f = np.float32
    return dict(
        forward=forward.astype(f),
        inverse=inverse.astype(f),
        forward_seg=forward_seg.reshape(SEGS * 128, 2 * M).astype(f),
        inverse_seg=inverse_seg.reshape(2 * M, SEGS * 128).astype(f),
        to_spec=(basis * weights[:, None]).astype(f),
        from_spec=np.ascontiguousarray(basis.T).astype(f),
        update=update.astype(f),
        row_weights=row_weights.astype(f),
    )


def permutations():
    natural = np.zeros((K, SEGS * 24), np.float32)
    grouped = np.zeros((K, SEGS * 24), np.float32)
    for s in range(SEGS):
        for i in range(KD):
            natural[KD * s + i, 24 * s + i] = 1.0
            grouped[KD * s + i, 24 * s + (i % 3) * 4 + i // 3] = 1.0
    return natural, grouped


def lanes_of(shape):
    return lax.broadcasted_iota(jnp.int32, shape, len(shape) - 1)


def split(x):
    high = x.astype(BF16)
    low = (x - high.astype(F32)).astype(BF16)
    return high, low


def mixing_block(mixing):
    high, low = split(MIXING_RATE * mixing)
    return jnp.concatenate(
        [jnp.concatenate([high, high], axis=1), jnp.concatenate([low, low], axis=1)], axis=0
    )


def substep_tile(window, mix, diffusivity, wind):
    width = window.shape[1]
    center = window[:, 128 : width - 128]
    right = pltpu.roll(window, width - 1, 1)[:, 128 : width - 128]
    left = pltpu.roll(window, 1, 1)[:, 128 : width - 128]
    high, low = split(center)
    mixed = jnp.dot(mix, jnp.concatenate([high, low], axis=0), preferred_element_type=F32)
    return (
        center
        + diffusivity * (right - 2.0 * center + left)
        - 0.5 * wind * (right - left)
        + (mixed[:K] + mixed[K:])
        - DAMPING * jnp.tanh(center)
    )


def column_hits(col):
    ids = lax.broadcasted_iota(jnp.int32, (128, col.shape[1]), 0)
    return jnp.where(ids == col, 1.0, 0.0).astype(BF16)


def edge_rows(first, last, mean_first, mean_last):
    lane = lanes_of((K, 128))
    edge = jnp.where(
        lane < 3,
        first,
        jnp.where(
            lane < 6, pltpu.roll(last, 6, 1), jnp.where(lane == 6, mean_first, mean_last)
        ),
    )
    padded = jnp.concatenate([edge, jnp.zeros((32, 128), F32)], axis=0)
    return padded.T[:8]


def prepare_kernel(off_ref, row_ref, first_ref, last_ref, colf_ref, coll_ref, send_ref):
    del off_ref
    row = row_ref[0]
    lane = lanes_of((KD, 128))
    hit_first = jnp.where(colf_ref[...] == 0, 1.0, 0.0)
    hit_last = jnp.where(coll_ref[...] == COLS - 1, 1.0, 0.0)
    first, last = first_ref[...], last_ref[...]
    mean_first = jnp.sum(first * hit_first, axis=1, keepdims=True) / jnp.sum(
        hit_first, axis=1, keepdims=True
    )
    mean_last = jnp.sum(last * hit_last, axis=1, keepdims=True) / jnp.sum(
        hit_last, axis=1, keepdims=True
    )
    edge = edge_rows(first, last, mean_first, mean_last)
    for s in range(SEGS):
        own = pltpu.roll(row, (NLON - COLS * s) % NLON, 1)[:, :128]
        before = pltpu.roll(row, (COLS + 1 - (COLS * s - 1)) % NLON, 1)[:, :128]
        chunk = jnp.where(lane <= COLS, own, jnp.where(lane == COLS + 1, before, 0.0))
        send_ref[s, 0:KD, :] = chunk
        send_ref[s, KD:16, :] = jnp.zeros((16 - KD, 128), F32)
        send_ref[s, 16:24, :] = edge


def prepare(offset, atmosphere, clouds, col):
    last = CELLS // 128 - 1
    return pl.pallas_call(
        prepare_kernel,
        grid_spec=pltpu.PrefetchScalarGridSpec(
            num_scalar_prefetch=1,
            grid=(1,),
            in_specs=[
                pl.BlockSpec((1, KD, NLON), lambda i, off: (off[0], 0, 0)),
                pl.BlockSpec((K, 128), lambda i, off: (0, 0)),
                pl.BlockSpec((K, 128), lambda i, off: (0, last)),
                pl.BlockSpec((1, 128), lambda i, off: (0, 0)),
                pl.BlockSpec((1, 128), lambda i, off: (0, last)),
            ],
            out_specs=pl.BlockSpec((SEGS, 24, 128), lambda i, off: (0, 0, 0)),
        ),
        out_shape=jax.ShapeDtypeStruct((SEGS, 24, 128), F32),
        name="prepare",
    )(offset, atmosphere, clouds, clouds, col, col)


def inner_kernel(with_mean, *refs):
    if with_mean:
        c_ref, col_ref, diff_ref, wind_ref, mixing_ref, base_ref, mean_ref, inv_ref, ext, sem = refs
    else:
        c_ref, diff_ref, wind_ref, mixing_ref, base_ref, ext, sem = refs
    copy = pltpu.make_async_copy(c_ref, ext.at[:, 128 : 128 + CELLS], sem)
    copy.start()
    ext[:, 0:128] = jnp.zeros((K, 128), F32)
    ext[:, 128 + CELLS :] = jnp.zeros((K, 128), F32)
    mix = mixing_block(mixing_ref[...])
    diffusivity, wind = diff_ref[...], wind_ref[...]
    copy.wait()

    def step(t, total):
        start = pl.multiple_of(t * TILE, TILE)
        window = ext[:, pl.ds(start, TILE + 256)]
        base_ref[:, pl.ds(start, TILE)] = substep_tile(window, mix, diffusivity, wind)
        if not with_mean:
            return total
        hits = column_hits(col_ref[:, pl.ds(start, TILE)])
        high, low = split(window[:, 128 : 128 + TILE])
        rows = jnp.concatenate([high, low, jnp.ones((16, TILE), BF16)], axis=0)
        return total + lax.dot_general(
            rows, hits, (((1,), (1,)), ((), ())), preferred_element_type=F32
        )

    if with_mean:
        total = lax.fori_loop(0, CELLS // TILE, step, jnp.zeros((2 * K + 16, 128), F32))
        counts = total[2 * K : 2 * K + 8]
        inv = jnp.where(counts > 0.0, 1.0 / jnp.maximum(counts, 1.0), 0.0)
        inv_ref[...] = inv
        mean_ref[...] = (total[:K] + total[K : 2 * K]) * inv[0:1]
    else:
        lax.fori_loop(0, CELLS // TILE, step, 0)


VMEM_SPEC = pl.BlockSpec(memory_space=pltpu.VMEM)
ANY_SPEC = pl.BlockSpec(memory_space=pl.ANY)


def inner(clouds, col, diffusivity, wind, mixing, with_mean):
    args = [clouds] + ([col] if with_mean else []) + [diffusivity, wind, mixing]
    shapes = [jax.ShapeDtypeStruct((K, CELLS), F32)]
    if with_mean:
        shapes += [jax.ShapeDtypeStruct((K, 128), F32), jax.ShapeDtypeStruct((8, 128), F32)]
    out = pl.pallas_call(
        lambda *refs: inner_kernel(with_mean, *refs),
        in_specs=[ANY_SPEC] + [VMEM_SPEC] * (len(args) - 1),
        out_specs=[VMEM_SPEC] * len(shapes),
        out_shape=shapes,
        scratch_shapes=[pltpu.VMEM((K, CELLS + 256), F32), pltpu.SemaphoreType.DMA],
        compiler_params=pltpu.CompilerParams(vmem_limit_bytes=40 << 20),
        name="inner",
    )(*args)
    return out if with_mean else out[0]


def outer_kernel(
    seg_ref, base_ref, first_ref, last_ref, prof_ref, halo_ref, perm_ref, back_ref, mean_ref, inv_ref,
    col_ref, diff_ref, wind_ref, mixing_ref, out_ref, end_ref, send_ref, ext1, ext2, force, cols, sem,
):
    copy = pltpu.make_async_copy(base_ref, ext1.at[:, 256 : 256 + CELLS], sem)
    copy.start()
    seg = seg_ref[0]
    lane = lanes_of((K, 128))
    zeros = jnp.zeros((K, 128), F32)
    mix = mixing_block(mixing_ref[...])
    diffusivity, wind = diff_ref[...], wind_ref[...]

    from_left = halo_ref[lax.rem(seg + SEGS - 1, SEGS), 16:24, :]
    from_right = halo_ref[lax.rem(seg + 1, SEGS), 16:24, :]
    edges = jnp.concatenate([from_left, from_right, jnp.zeros((112, 128), F32)], axis=0).T[:K]
    left_tile = jnp.where(lane >= 125, pltpu.roll(edges, 122, 1), 0.0)
    right_tile = jnp.where(lane < 3, pltpu.roll(edges, 120, 1), 0.0)
    mean = mean_ref[...]
    mean_all = jnp.where(
        lane < COLS,
        mean,
        jnp.where(
            lane == COLS,
            pltpu.roll(edges, COLS - 14, 1),
            jnp.where(lane == COLS + 1, pltpu.roll(edges, COLS + 1 - 7, 1), 0.0),
        ),
    )
    profile = jnp.dot(
        perm_ref[...],
        prof_ref[...].reshape(SEGS * 24, 128),
        precision=HIGHEST,
        preferred_element_type=F32,
    )
    pulled = jnp.where(lane < COLS + 2, RELAXATION * (profile - mean_all), 0.0)
    pulled = jnp.concatenate(split(pulled), axis=1)

    cols[:, 0:256] = jnp.full((1, 256), COLS + 1, jnp.int32)
    cols[:, 256 + CELLS :] = jnp.full((1, 256), COLS, jnp.int32)
    cols[:, 256 : 256 + CELLS] = col_ref[...]
    ext1[:, 0:128] = zeros
    ext1[:, EXT - 128 :] = zeros
    copy.wait()
    left_window = jnp.concatenate([zeros, left_tile, first_ref[...]], axis=1)
    ext1[:, 128:384] = substep_tile(left_window, mix, diffusivity, wind)
    right_window = jnp.concatenate([last_ref[...], right_tile, zeros], axis=1)
    ext1[:, EXT - 384 : EXT - 128] = substep_tile(right_window, mix, diffusivity, wind)

    def force_step(t, _):
        start = pl.multiple_of(128 + t * TILE, 128)
        hits = column_hits(cols[:, pl.ds(start, TILE)])
        forced = jnp.dot(
            pulled, jnp.concatenate([hits, hits], axis=0), preferred_element_type=F32
        )
        force[:, pl.ds(start, TILE)] = forced
        ext1[:, pl.ds(start, TILE)] += forced
        return 0

    lax.fori_loop(0, CELLS // TILE + 1, force_step, 0)

    def second_step(t, _):
        start = pl.multiple_of(t * TILE, TILE)
        here = pl.multiple_of(start + 128, 128)
        window = ext1[:, pl.ds(start, TILE + 256)]
        ext2[:, pl.ds(here, TILE)] = (
            substep_tile(window, mix, diffusivity, wind) + force[:, pl.ds(here, TILE)]
        )
        return 0

    lax.fori_loop(0, CELLS // TILE + 1, second_step, 0)

    def third_step(t, total):
        start = pl.multiple_of(t * TILE, TILE)
        here = pl.multiple_of(start + 256, 128)
        window = ext2[:, pl.ds(pl.multiple_of(start + 128, 128), TILE + 256)]
        value = substep_tile(window, mix, diffusivity, wind) + force[:, pl.ds(here, TILE)]
        out_ref[:, pl.ds(start, TILE)] = value
        hits = column_hits(cols[:, pl.ds(here, TILE)])
        rows = jnp.concatenate(split(value), axis=0)
        return total + lax.dot_general(
            rows, hits, (((1,), (1,)), ((), ())), preferred_element_type=F32
        )

    total = lax.fori_loop(0, CELLS // TILE, third_step, jnp.zeros((2 * K, 128), F32))
    end = (total[:K] + total[K:]) * inv_ref[0:1]
    end_ref[...] = end
    tendency = jnp.where(lane < COLS, end - mean, 0.0)
    sent = jnp.dot(back_ref[...], tendency, precision=HIGHEST, preferred_element_type=F32)
    edge = edge_rows(
        out_ref[:, 0:128], out_ref[:, CELLS - 128 :], end[:, 0:1], end[:, COLS - 1 : COLS]
    )
    for s in range(SEGS):
        send_ref[s, 0:16, :] = sent[24 * s : 24 * s + 16]
        send_ref[s, 16:24, :] = edge


def outer(seg, base, clouds, profile, halo, perm, back, mean, inv, col, diffusivity, wind, mixing):
    ends = CELLS // 256 - 1
    full = lambda shape: pl.BlockSpec(shape, lambda i, seg: (0,) * len(shape))
    return pl.pallas_call(
        outer_kernel,
        grid_spec=pltpu.PrefetchScalarGridSpec(
            num_scalar_prefetch=1,
            grid=(1,),
            in_specs=[
                ANY_SPEC,
                pl.BlockSpec((K, 256), lambda i, seg: (0, 0)),
                pl.BlockSpec((K, 256), lambda i, seg: (0, ends)),
                full((SEGS, 24, 128)),
                full((SEGS, 24, 128)),
                full((K, SEGS * 24)),
                full((SEGS * 24, K)),
                full((K, 128)),
                full((8, 128)),
                full((1, CELLS)),
                full((K, 1)),
                full((K, 1)),
                full((K, K)),
            ],
            out_specs=[full((K, CELLS)), full((K, 128)), full((SEGS, 24, 128))],
            scratch_shapes=[
                pltpu.VMEM((K, EXT), F32),
                pltpu.VMEM((K, EXT), F32),
                pltpu.VMEM((K, EXT), F32),
                pltpu.VMEM((1, EXT), jnp.int32),
                pltpu.SemaphoreType.DMA,
            ],
        ),
        out_shape=[
            jax.ShapeDtypeStruct((K, CELLS), F32),
            jax.ShapeDtypeStruct((K, 128), F32),
            jax.ShapeDtypeStruct((SEGS, 24, 128), F32),
        ],
        compiler_params=pltpu.CompilerParams(vmem_limit_bytes=48 << 20),
        name="outer",
    )(seg, base, clouds, clouds, profile, halo, perm, back, mean, inv, col, diffusivity, wind, mixing)


def dft_rows(received, table):
    lead = received.shape[:-3]
    rows = jnp.moveaxis(received[..., :KD, :], -3, -2).reshape(lead + (KD, SEGS * 128))
    coeffs = jnp.dot(rows, table, precision=HIGH).reshape(lead + (3, 4, 2, M))
    return jnp.moveaxis(coeffs, -2, -3).reshape(lead + (3, 8, M))


def weigh(factors, rows, axis):
    vort, div, geo = rows[:, :, 0], rows[:, :, 1], rows[:, :, 2]
    f = factors[:, :, :, None, :]
    return jnp.stack(
        (
            jnp.sum(f[0] * vort, axis=axis),
            jnp.sum(f[1] * div + f[2] * geo, axis=axis),
            jnp.sum(f[1] * geo - f[2] * div, axis=axis),
        ),
        axis=1,
    )


def spectral_twice(rows, tab, lat):
    sent = rows.reshape(LAT_DEV, 3, 8, LATS, 8).transpose(3, 0, 1, 2, 4)
    sent = sent.reshape(LATS, LAT_DEV * 3 * 64)
    got = lax.all_to_all(sent, "lat", 0, 0, tiled=True).reshape(NLAT, 3 * 64)
    spec = jnp.dot(tab["to_spec"], got, precision=HIGH).reshape(NT, 3, 8, 8)
    factors = lax.dynamic_slice_in_dim(tab["update"], lat * 8, 8, axis=2)[:, :, None, :]
    vort, div, geo = spec[:, 0], spec[:, 1], spec[:, 2]
    for _ in range(2):
        vort = factors[0] * vort
        div, geo = factors[1] * div + factors[2] * geo, factors[1] * geo - factors[2] * div
    spec = jnp.stack((vort, div, geo), axis=1).reshape(NT, 3 * 64)
    back = jnp.dot(tab["from_spec"], spec, precision=HIGH).reshape(LATS, LAT_DEV * 3 * 64)
    got = lax.all_to_all(back, "lat", 0, 0, tiled=True)
    return got.reshape(LATS, LAT_DEV, 3, 8, 8).transpose(1, 2, 3, 0, 4).reshape(LAT_DEV, 3, 8, M)


def shards(atmosphere, cloud_state, channel_lat, cell_column, channel_wind, diffusivity, mixing):
    tab = {name: jnp.asarray(value) for name, value in tables().items()}
    natural, grouped = permutations()
    lat = lax.axis_index("lat")
    seg = lax.axis_index("seg").astype(jnp.int32).reshape(1)
    core = lat % 2
    chip = lat // 2
    offset = channel_lat - (lat * LAT_DEV).astype(jnp.int32)
    clouds = cloud_state[0]
    col = cell_column
    wind = channel_wind.reshape(K, 1)
    diff = diffusivity.reshape(K, 1)

    position = lax.all_to_all(
        jnp.broadcast_to(channel_lat[None, :], (LATS, 128)), "lat", 0, 0, tiled=True
    )[:, 0]

    first_send = prepare(offset, atmosphere, clouds, col)
    first_got = lax.all_to_all(first_send, "seg", 0, 0, tiled=True)
    base, mean, inv = inner(clouds, col, diff, wind, mixing, True)

    basis = tab["from_spec"]
    picks = (position[:, None] == jnp.arange(NLAT, dtype=jnp.int32)[None, :]).astype(F32)
    channel_basis = jnp.dot(picks, basis, precision=HIGHEST).reshape(16, 2, NT)
    mine = lax.dynamic_index_in_dim(channel_basis, core, 1, keepdims=False)
    others = lax.dynamic_index_in_dim(channel_basis, 1 - core, 1, keepdims=False)
    here = lax.dynamic_slice_in_dim(basis, lat * LAT_DEV, LAT_DEV, axis=0)
    pair = lax.dynamic_index_in_dim(channel_basis, chip, 0, keepdims=False)
    products = jnp.concatenate(
        (
            (mine[:, None] * here[None]).reshape(-1, NT),
            (others[:, None] * here[None]).reshape(-1, NT),
            (mine[:, None] * pair[None]).reshape(-1, NT),
        ),
        axis=0,
    )
    weights = jnp.dot(products, tab["row_weights"], precision=HIGH).reshape(-1, 3, M)
    weights = weights.transpose(1, 0, 2)
    to_mine = weights[:, :192].reshape(3, 16, LAT_DEV, M)
    to_others = weights[:, 192:384].reshape(3, 16, LAT_DEV, M)
    to_pair = weights[:, 384:].reshape(3, 16, 2, M)

    ordered = atmosphere.reshape(LAT_DEV, 4, 3, NLON).transpose(0, 2, 1, 3).reshape(-1, NLON)
    rows = jnp.dot(ordered, tab["forward"], precision=HIGH).reshape(LAT_DEV, 3, 4, 2, M)
    rows = rows.transpose(0, 1, 3, 2, 4).reshape(LAT_DEV, 3, 8, M)
    base_mine = weigh(to_mine, rows[None], 1)
    base_others = weigh(to_others, rows[None], 1)
    base_sum = base_mine + lax.ppermute(base_others, "lat", CORE_SWAP)

    clouds, mean_1, send = outer(
        seg, base, clouds, first_got, first_got, jnp.asarray(natural), jnp.asarray(grouped.T.copy()),
        mean, inv, col, diff, wind, mixing,
    )
    got = lax.all_to_all(
        jnp.concatenate((send, send), axis=0), ("lat", "seg"), 0, 0,
        axis_index_groups=CHIP_GROUPS, tiled=True,
    ).reshape(2, SEGS, 24, 128)
    base = inner(clouds, col, diff, wind, mixing, False)
    pair_rows = dft_rows(got, tab["forward_seg"])
    parts = base_sum + weigh(to_pair, pair_rows[None], 1)
    parts = lax.all_to_all(parts, "lat", 0, 0, axis_index_groups=ROW_GROUPS, tiled=True)
    profile_rows = jnp.sum(parts, axis=0).reshape(3, 2, 4, M).transpose(0, 2, 1, 3).reshape(KD, 2 * M)
    profile = jnp.dot(profile_rows, tab["inverse_seg"], precision=HIGH).reshape(KD, SEGS, 128)
    profile = jnp.pad(profile.transpose(1, 0, 2), ((0, 0), (0, 24 - KD), (0, 0)))
    profile = lax.all_to_all(profile, "seg", 0, 0, tiled=True)

    own_row = lax.dynamic_index_in_dim(pair_rows, core, 0)
    at_channel = jnp.arange(LAT_DEV, dtype=jnp.int32) == offset[0]
    forced_rows = rows + jnp.where(at_channel[:, None, None, None], own_row, 0.0)
    settled = spectral_twice(forced_rows, tab, lat)

    halo = lax.dynamic_index_in_dim(got, core, 0, keepdims=False)
    clouds, _, send = outer(
        seg, base, clouds, profile, halo, jnp.asarray(grouped), jnp.asarray(grouped.T.copy()),
        mean_1, inv, col, diff, wind, mixing,
    )
    got = lax.all_to_all(send, "seg", 0, 0, tiled=True)
    last_rows = dft_rows(got, tab["forward_seg"])
    from_mine = lax.all_to_all(
        jnp.broadcast_to(last_rows[None], (16, 3, 8, M)), "lat", 0, 0,
        axis_index_groups=ROW_GROUPS, tiled=True,
    )
    from_others = lax.ppermute(from_mine, "lat", CORE_SWAP)
    final = settled + weigh(to_mine, from_mine[:, None], 0) + weigh(to_others, from_others[:, None], 0)
    final = final.reshape(LAT_DEV, 3, 2, 4, M).transpose(0, 3, 1, 2, 4).reshape(LAT_DEV * KD, 2 * M)
    grid = jnp.dot(final, tab["inverse"], precision=HIGH).reshape(LAT_DEV, KD, NLON)
    return grid, clouds[None]


def solution(mesh):
    placed = (
        P("lat", "seg", None),
        P("lat", None, "seg"),
        P("lat"),
        P("lat", "seg"),
        P("lat", None),
        P(),
        P(),
    )
    return jax.shard_map(
        shards,
        mesh=mesh,
        in_specs=placed,
        out_specs=(P("lat", "seg", None), P("lat", None, "seg")),
        check_vma=False,
    )
```

time: 310 us -> 237 us (0.76)
  blocking collectives: 55 us -> 0 us
  matrix products: 65.8 us -> 14.1 us
  Pallas kernels: 0 us -> 50.9 us
  waiting for transfers between devices: 52.8 us -> 39.7 us
  local copies, waits for them, and re-layouts: 59.4 us -> 46.7 us
  starting transfers between devices: 49.8 us -> 60.4 us
    all_to_all x3 -> x0, blocking collectives: 55 us -> none  [the longest x1 23.3 us: shards(): lax.all_to_all(coeff_flat, 'lat', split_axis=1, concat_axis=0, tiled=True)]
    dot_general x19 -> x9, matrix products: 65.8 us -> 14.1 us  [the longest x2 3.56 us: dft_rows(): coeffs = jnp.dot(rows, table, precision=HIGH).reshape(lead + (3, 4, 2, M))]
    pallas_call x0 -> x5, Pallas kernels: none -> 50.9 us  [the longest x2 38.3 us: outer(): pl.pallas_call(outer_kernel, grid_spec=pltpu.PrefetchScalarGridSpec(num_s...]
    all_to_all x5 -> x9, starting transfers between devices: 29.1 us -> 60.4 us  [the longest x1 11.4 us: shards(): lax.all_to_all(jnp.broadcast_to(channel_lat[None, :], (LATS, 128)), 'lat'...]
    ppermute x12 -> x2, starting transfers between devices: 20.7 us -> 0.01 us  [the longest x1 0.01 us: shards(): base_sum = base_mine + lax.ppermute(base_others, 'lat', CORE_SWAP)]
    ppermute x12 -> x2, waiting for transfers between devices: 18.1 us -> 0.95 us  [the longest x1 0.95 us: shards(): from_others = lax.ppermute(from_mine, 'lat', CORE_SWAP)]
    all_to_all x17 -> x3, local copies, waits for them, and re-layouts: 15.6 us -> 3.77 us  [the longest x1 2.15 us: spectral_twice(): got = lax.all_to_all(sent, 'lat', 0, 0, tiled=True).reshape(NLAT, 3 * 64)]
    unnamed x3 -> x0, other arithmetic: 6.9 us -> none
  transfers between devices with their start and end apart: 17 -> 11, of which waited for: 11 -> 7; matrix products, arithmetic and copies ran while one was open for 11% -> 27% of each run, Pallas kernels for 0% -> 14%
where the time goes in v1:
time: 237 us; the launch traced here: 233 us
  starting transfers between devices  60.4 us (25%)
  Pallas kernels  50.9 us (21%)
  local copies, waits for them, and re-layouts  46.7 us (20%)
  waiting for transfers between devices  39.7 us (17%)
  other arithmetic  19.5 us (8%)
  matrix products  14.1 us (6%)
    pallas_call x2, Pallas kernels, outer(): pl.pallas_call(outer_kernel, grid_spec=pltpu.PrefetchScalarGridSpec(num_s...  38.3 us
    all_to_all x1, waiting for transfers between devices, spectral_twice(): got = lax.all_to_all(back, 'lat', 0, 0, tiled=True)  13.3 us
    all_to_all x1, starting transfers between devices, shards(): lax.all_to_all(jnp.broadcast_to(channel_lat[None, :], (LATS, 128)), 'lat'...  11.4 us
    pallas_call x2, Pallas kernels, inner(): pl.pallas_call(lambda *refs: inner_kernel(with_mean, *refs), in_specs=[AN...  10.7 us
    all_to_all x1, waiting for transfers between devices, spectral_twice(): got = lax.all_to_all(sent, 'lat', 0, 0, tiled=True).reshape(NLAT, 3 * 64)  10.7 us
    all_to_all x1, starting transfers between devices, spectral_twice(): got = lax.all_to_all(back, 'lat', 0, 0, tiled=True)  10.5 us
    all_to_all x1, starting transfers between devices, spectral_twice(): got = lax.all_to_all(sent, 'lat', 0, 0, tiled=True).reshape(NLAT, 3 * 64)  10.4 us
    unnamed x63, local copies, waits for them, and re-layouts  8.92 us
  transfers between devices with their start and end apart: 11, of which 7 were waited for; matrix products, arithmetic and copies ran while one was open for 27% of the time, Pallas kernels for 14%

profile of v1, /device:TPU:32, one launch (start us, length us, event | category | flops | bytes accessed | tf_op | source)
XLA Modules:
  0.0 233.3 jit_solution(16566626409292575170)
XLA Ops:
  1.9 11.4 %all-to-all-start.4 = ((s32[32,1,128]{2,1,0:T(1,128)}), s32[32,1,128]{2,1,0:T(1,128)S(1)}, u32[]{:S(2)}, u32[]{:S(2)}) async-start(s32[32,1,128]{2,1,0:T(1,128)} %broadcast_in_dim.60), calls=%async_computation.4 | async-start | bytes 32768 | tf_op jit(solution)/shard_map/all_to_all | solution.py:423
  13.3 1.3 copy.179
  14.6 2.3 %convolution_bitcast_fusion = f32[12,3,2,4,256]{4,0,3,1,2:T(8,128)S(1)} fusion(f32[2,256,768,1,1]{2,1,4,3,0:T(8,128)} %constant.113, f32[12,3,4,768]{3,0,1,2:T(8,128)S(1)} %bitcast.142), kind=kOutput, calls=%fused_computation.13 | convolution fusion | flops 339738624 | bytes 2310144 | tf_op jit(solution)/shard_map/dot_general | solution.py:453
  18.1 4.1 %reshape.171 = f32[12,3,8,32,8]{4,3,2,1,0:T(8,128)} reshape(f32[12,3,2,4,256]{4,3,2,1,0:T(4,128)S(1)} %copy.181) | data formatting | bytes 589824 | tf_op jit(solution)/shard_map/reshape | solution.py:454
  22.4 1.9 prepare.1
  24.3 5.7 %inner.2 = (f32[96,6144]{1,0:T(8,128)S(1)}, f32[96,128]{1,0:T(8,128)S(1)}, f32[8,128]{1,0:T(8,128)S(1)}) custom-call(f32[96,6144]{1,0:T(8,128)S(1)} %bitcast.137, s32[1,6144]{1,0:T(1,128)S(1)} %copy-done.6, f32[96,1]{1,0:T(8,128)S(1)} %copy.182.refs_2_.diff_ref.refs_1_, f32[96,1]{1,0:T(8,128)S(1)} %copy.183.refs_3_.wind_ref.refs_2_, f32[96,96]{1,0:T(8,128)S(1)} %copy-done.5), custom_call_target="tpu_custom_call" | custom-call | tf_op jit(solution)/shard_map/inner/pallas_call | solution.py:225
  30.0 1.4 copy-done.3
  31.4 4.5 %all-to-all-start = ((f32[8,24,128]{2,1,0:T(8,128)}), f32[8,24,128]{2,1,0:T(8,128)S(1)}, u32[]{:S(2)}, u32[]{:S(2)}) async-start(f32[8,24,128]{2,1,0:T(8,128)} %prepare.1), calls=%async_computation | async-start | bytes 196608 | tf_op jit(solution)/shard_map/all_to_all | solution.py:428
  37.4 1.2 fusion.19
  38.7 1.1 copy.194
  41.2 2.4 %add_reduce_fusion.3 = (f32[16,8,256]{2,1,0:T(8,128)}, f32[16,8,256]{2,1,0:T(8,128)}, f32[16,8,256]{2,1,0:T(8,128)S(1)}, f32[16,8,256]{2,1,0:T(8,128)S(1)}, f32[16,8,256]{2,1,0:T(8,128)S(1)}, /*index=5*/f32[16,8,256]{2,1,0:T(8,128)}) fusion(f32[12,8,256]{2,1,0:T(8,128)S(1)} %copy-done.26, f32[16,12,256]{2,1,0:T(8,128)S(1)} %mul.499, ...), kind=kLoop, calls=%fused_computation.11 | loop fusion | flops 7667712 | bytes 2260992 | tf_op jit(solution)/shard_map/reduce_sum | solution.py:387
  44.4 1.7 copy-done.4
  46.1 19.1 %outer.2 = (f32[96,6144]{1,0:T(8,128)S(1)}, f32[96,128]{1,0:T(8,128)S(1)}, f32[8,24,128]{2,1,0:T(8,128)S(1)}) custom-call(s32[1]{0:T(128)} %bitcast.9.seg_ref, f32[96,6144]{1,0:T(8,128)S(1)} %copy-done.4, f32[96,6144]{1,0:T(8,128)} %bitcast.135, f32[96,6144]{1,0:T(8,128)} %bitcast.136, f32[8,24,128]{2,1,0:T(8,128)S(1)} %all-to-all-done.prof_ref.halo_ref, ...), custom_call_target="tpu_custom_call" | custom-call | tf_op jit(solution)/shard_map/outer/pallas_call | solution.py:335
  65.9 5.9 %all-to-all-start.1 = ((f32[16,24,128]{2,1,0:T(8,128)}), f32[16,24,128]{2,1,0:T(8,128)S(1)}, u32[]{:S(2)}, u32[]{:S(2)}) async-start(f32[16,24,128]{2,1,0:T(8,128)} %pad_maximum_fusion.1), calls=%async_computation.1 | async-start | bytes 393216 | tf_op jit(solution)/shard_map/all_to_all | solution.py:463
  71.8 1.8 fusion.18
  73.6 1.0 copy.204
  79.7 2.6 %convolution_bitcast_fusion.2 = f32[2,3,2,4,256]{4,3,2,1,0:T(4,128)S(1)} fusion(f32[2,256,1024,1,1]{2,1,0,4,3:T(8,128)} %constant.114, f32[2,3,4,1024,1]{3,2,1,0,4:T(4,128)} %reshape.188), kind=kOutput, calls=%fused_computation.15 | convolution fusion | flops 75497472 | bytes 2244608 | tf_op jit(solution)/shard_map/dot_general | solution.py:377
  82.4 1.0 broadcast_in_dim.56
  83.4 5.6 %add_bitcast_fusion = f32[32,12,3,8,8]{4,0,3,2,1:T(8,128)} fusion(f32[12,3,8,32,8]{4,3,2,1,0:T(8,128)} %reshape.171, f32[3,8,32,8]{3,2,1,0:T(8,128)} %broadcast_in_dim.56, pred[12]{0:T(512)(128)(4,1)S(1)} %iota_compare_fusion.2), kind=kLoop, calls=%fused_computation | loop fusion | flops 147456 | bytes 614412 | tf_op jit(solution)/shard_map/transpose | solution.py:395
  89.0 3.9 %copy.187 = f32[32,12,3,8,8]{0,4,3,2,1:T(8,128)} copy(f32[32,12,3,8,8]{4,0,3,2,1:T(8,128)} %add_bitcast_fusion) | data formatting | bytes 589824 | tf_op jit(solution)/shard_map/transpose | solution.py:395
  92.8 2.1 copy.188
  95.0 10.4 %all-to-all-start.2 = ((f32[32,1,2304]{2,1,0:T(1,128)}), f32[32,1,2304]{2,1,0:T(1,128)S(1)}, u32[]{:S(2)}, u32[]{:S(2)}) async-start(f32[32,1,2304]{2,1,0:T(1,128)} %copy.188), calls=%async_computation.2 | async-start | bytes 589824 | tf_op jit(solution)/shard_map/all_to_all | solution.py:397
  107.1 1.2 fusion.8
  109.1 10.7 %all-to-all-done.2 = f32[32,1,2304]{2,1,0:T(1,128)S(1)} async-done(((f32[32,1,2304]{2,1,0:T(1,128)}), f32[32,1,2304]{2,1,0:T(1,128)S(1)}, u32[]{:S(2)}, u32[]{:S(2)}) %all-to-all-start.2) | async-done | bytes 294944 | tf_op jit(solution)/shard_map/all_to_all | solution.py:397
  119.7 5.2 %all-to-all-start.5 = ((f32[16,3,8,256]{3,2,1,0:T(8,128)}), f32[16,3,8,256]{3,2,1,0:T(8,128)}, u32[]{:S(2)}, u32[]{:S(2)}) async-start(f32[16,3,8,256]{3,2,1,0:T(8,128)} %copy.206), calls=%async_computation.5 | async-start | bytes 786432 | tf_op jit(solution)/shard_map/all_to_all | solution.py:470
  125.7 5.0 %inner.3.base_ref = f32[96,6144]{1,0:T(8,128)S(1)} custom-call(f32[96,6144]{1,0:T(8,128)S(1)} %get-tuple-element.14.refs_0_.first_ref.last_ref, f32[96,1]{1,0:T(8,128)S(1)} %copy.182.refs_2_.diff_ref.refs_1_, f32[96,1]{1,0:T(8,128)S(1)} %copy.183.refs_3_.wind_ref.refs_2_, f32[96,96]{1,0:T(8,128)S(1)} %copy-done.5), custom_call_target="tpu_custom_call" | custom-call | tf_op jit(solution)/shard_map/inner/pallas_call | solution.py:225
  130.7 1.4 copy-done.1
  132.1 2.4 %reduce = f32[32,2304]{1,0:T(8,128)} reduce(f32[32,1,2304]{2,1,0:T(1,128)} %copy-done.22, f32[]{:T(128)} %constant.117), dimensions={1}, to_apply=%all_to_all.39.reduce_sub_computation | reduce | bytes 589828 | tf_op jit(solution)/shard_map/all_to_all | solution.py:397
  134.5 1.9 reshape.177
  136.4 1.6 fusion.20
  138.7 1.0 reduce_sum.153
  139.8 2.5 %convolution_bitcast_fusion.1 = f32[8,12,128]{2,1,0:T(8,128)S(1)} fusion(f32[12,512,1]{1,0,2:T(8,128)S(1)} %reshape.190, f32[8,128,512]{2,1,0:T(8,128)} %constant.112), kind=kOutput, calls=%fused_computation.14 | convolution fusion | flops 37748736 | bytes 2170880 | tf_op jit(solution)/shard_map/dot_general | solution.py:472
  143.0 4.4 %all-to-all-start.6 = ((f32[8,24,128]{2,1,0:T(8,128)}), f32[8,24,128]{2,1,0:T(8,128)S(1)}, u32[]{:S(2)}, u32[]{:S(2)}) async-start(f32[8,24,128]{2,1,0:T(8,128)} %pad.4), calls=%async_computation.6 | async-start | bytes 196608 | tf_op jit(solution)/shard_map/all_to_all | solution.py:474
  147.4 1.6 pad_maximum_fusion.2
  149.0 4.8 %all-to-all-done.6.prof_ref = f32[8,24,128]{2,1,0:T(8,128)S(1)} async-done(((f32[8,24,128]{2,1,0:T(8,128)}), f32[8,24,128]{2,1,0:T(8,128)S(1)}, u32[]{:S(2)}, u32[]{:S(2)}) %all-to-all-start.6) | async-done | bytes 98336 | tf_op jit(solution)/shard_map/all_to_all | solution.py:474
  153.8 1.7 copy-done.2
  155.5 19.2 %outer.3 = (f32[96,6144]{1,0:T(8,128)}, f32[96,128]{1,0:T(8,128)}, f32[8,24,128]{2,1,0:T(8,128)}) custom-call(s32[1]{0:T(128)} %bitcast.9.seg_ref, f32[96,6144]{1,0:T(8,128)S(1)} %copy-done.2, f32[96,6144]{1,0:T(8,128)S(1)} %get-tuple-element.14.refs_0_.first_ref.last_ref, f32[96,6144]{1,0:T(8,128)S(1)} %get-tuple-element.14.refs_0_.first_ref.last_ref, ...), custom_call_target="tpu_custom_call" | custom-call | tf_op jit(solution)/shard_map/outer/pallas_call | solution.py:335
  174.8 3.5 %all-to-all-start.7 = ((f32[8,24,128]{2,1,0:T(8,128)}), f32[8,24,128]{2,1,0:T(8,128)S(1)}, u32[]{:S(2)}, u32[]{:S(2)}) async-start(f32[8,24,128]{2,1,0:T(8,128)} %get-tuple-element.16), calls=%async_computation.7 | async-start | bytes 196608 | tf_op jit(solution)/shard_map/all_to_all | solution.py:486
  178.3 1.4 fusion.21
  179.7 1.1 all_to_all.48
  180.7 3.9 %all-to-all-done.7 = f32[8,24,128]{2,1,0:T(8,128)S(1)} async-done(((f32[8,24,128]{2,1,0:T(8,128)}), f32[8,24,128]{2,1,0:T(8,128)S(1)}, u32[]{:S(2)}, u32[]{:S(2)}) %all-to-all-start.7) | async-done | bytes 98336 | tf_op jit(solution)/shard_map/all_to_all | solution.py:486
  184.6 10.5 %all-to-all-start.3 = ((f32[32,1,2304]{2,1,0:T(1,128)}), f32[32,1,2304]{2,1,0:T(1,128)S(1)}, u32[]{:S(2)}, u32[]{:S(2)}) async-start(f32[32,1,2304]{2,1,0:T(1,128)} %all_to_all.48), calls=%async_computation.3 | async-start | bytes 589824 | tf_op jit(solution)/shard_map/all_to_all | solution.py:406
  196.1 13.3 %all-to-all-done.3 = f32[32,1,2304]{2,1,0:T(1,128)S(1)} async-done(((f32[32,1,2304]{2,1,0:T(1,128)}), f32[32,1,2304]{2,1,0:T(1,128)S(1)}, u32[]{:S(2)}, u32[]{:S(2)}) %all-to-all-start.3) | async-done | bytes 294944 | tf_op jit(solution)/shard_map/all_to_all | solution.py:406
  210.2 4.6 %all-to-all-start.8 = ((f32[16,3,8,256]{3,2,1,0:T(8,128)}), f32[16,3,8,256]{3,2,1,0:T(8,128)S(1)}, u32[]{:S(2)}, u32[]{:S(2)}) async-start(f32[16,3,8,256]{3,2,1,0:T(8,128)} %broadcast_in_dim.62), calls=%async_computation.8 | async-start | bytes 786432 | tf_op jit(solution)/shard_map/all_to_all | solution.py:488
  215.3 2.9 %copy.192 = f32[12,3,8,32,8]{4,3,2,1,0:T(8,128)} copy(f32[12,3,8,32,8]{3,4,2,1,0:T(8,128)S(1)} %bitcast.141) | data formatting | bytes 589824 | tf_op jit(solution)/shard_map/transpose | solution.py:407
  218.3 4.2 %reshape.181 = f32[12,3,2,4,256]{4,3,2,1,0:T(4,128)S(1)} reshape(f32[12,3,8,32,8]{4,3,2,1,0:T(8,128)} %copy.192) | data formatting | bytes 589824 | tf_op jit(solution)/shard_map/reshape | solution.py:407
  222.5 5.5 %all-to-all-done.8 = f32[16,3,8,256]{3,2,1,0:T(8,128)S(1)} async-done(((f32[16,3,8,256]{3,2,1,0:T(8,128)}), f32[16,3,8,256]{3,2,1,0:T(8,128)S(1)}, u32[]{:S(2)}, u32[]{:S(2)}) %all-to-all-start.8) | async-done | bytes 393248 | tf_op jit(solution)/shard_map/all_to_all | solution.py:488
  231.8 1.5 fusion.22
  (142 shorter events, 21.9 us)
Async XLA Ops:
  1.9 29.5 %all-to-all-start.4 = ((s32[32,1,128]{2,1,0:T(1,128)}), s32[32,1,128]{2,1,0:T(1,128)S(1)}, u32[]{:S(2)}, u32[]{:S(2)}) async-start(s32[32,1,128]{2,1,0:T(1,128)} %broadcast_in_dim.60), calls=%async_computation.4 | async-start | bytes 32768 | tf_op jit(solution)/shard_map/all_to_all | solution.py:423
  16.9 1.0 copy-start.20
  18.0 4.1 %copy-start.28 = (f32[96]{0:T(128)S(1)}, f32[96]{0:T(128)}, u32[]{:S(2)}) copy-start(f32[96]{0:T(128)} %param.24) | copy-start | bytes 1156
  18.0 4.2 %copy-start.29 = (f32[1,96]{1,0:T(1,128)S(1)}, f32[1,96]{1,0:T(1,128)}, u32[]{:S(2)}) copy-start(f32[1,96]{1,0:T(1,128)} %param.23) | copy-start | bytes 1156
  22.3 1.9 copy-start
  22.3 1.9 copy-start.5
  22.4 1.9 copy-start.6
  30.0 1.4 copy-start.3
  31.4 5.2 %copy-start.25 = (f32[256,768]{1,0:T(8,128)S(1)}, f32[256,768]{1,0:T(8,128)}, u32[]{:S(2)}) copy-start(f32[256,768]{1,0:T(8,128)} %constant.96.clone) | copy-start | bytes 2359300
  31.4 13.0 %all-to-all-start = ((f32[8,24,128]{2,1,0:T(8,128)}), f32[8,24,128]{2,1,0:T(8,128)S(1)}, u32[]{:S(2)}, u32[]{:S(2)}) async-start(f32[8,24,128]{2,1,0:T(8,128)} %prepare.1), calls=%async_computation | async-start | bytes 196608 | tf_op jit(solution)/shard_map/all_to_all | solution.py:428
  37.4 1.3 copy-start.10
  39.8 0.8 copy-start.17
  40.0 0.7 copy-start.13
  40.1 0.9 copy-start.26
  40.1 1.0 copy-start.27
  40.2 3.4 %copy-start.15 = (f32[16,12,256]{2,1,0:T(8,128)}, f32[16,12,256]{2,1,0:T(8,128)S(1)}, u32[]{:S(2)}) copy-start(f32[16,12,256]{2,1,0:T(8,128)S(1)} %mul.499) | copy-start | bytes 589828
  40.6 3.7 %copy-start.11 = (f32[16,12,256]{2,1,0:T(8,128)}, f32[16,12,256]{2,1,0:T(8,128)S(1)}, u32[]{:S(2)}) copy-start(f32[16,12,256]{2,1,0:T(8,128)S(1)} %mul.512) | copy-start | bytes 589828
  41.2 3.2 %copy-start.7 = (f32[192,96]{1,0:T(8,128)S(1)}, f32[192,96]{1,0:T(8,128)}, u32[]{:S(2)}) copy-start(f32[192,96]{1,0:T(8,128)} %constant.98.clone.back_ref) | copy-start | bytes 221188
  41.2 3.2 %copy-start.9 = (f32[96,192]{1,0:T(8,128)S(1)}, f32[96,192]{1,0:T(8,128)}, u32[]{:S(2)}) copy-start(f32[96,192]{1,0:T(8,128)} %constant.97.clone.perm_ref) | copy-start | bytes 221188
  44.4 62.7 %collective-permute-start = (f32[16,3,8,256]{3,2,0,1:T(8,128)}, f32[16,3,8,256]{3,2,0,1:T(8,128)}, u32[]{:S(2)}, u32[]{:S(2)}) collective-permute-start(f32[16,3,8,256]{3,2,0,1:T(8,128)} %pad_maximum_fusion), channel_id=1, source_target_pairs={{0,8},{8,0},{16,24},{24,16},{32,40},{40,32},{48,56},{56,48},{64,72... | collective-permute-start | bytes 1179656 | tf_op jit(solution)/shard_map/ppermute | solution.py:457
  44.4 1.7 copy-start.4
  65.9 13.1 %all-to-all-start.1 = ((f32[16,24,128]{2,1,0:T(8,128)}), f32[16,24,128]{2,1,0:T(8,128)S(1)}, u32[]{:S(2)}, u32[]{:S(2)}) async-start(f32[16,24,128]{2,1,0:T(8,128)} %pad_maximum_fusion.1), calls=%async_computation.1 | async-start | bytes 393216 | tf_op jit(solution)/shard_map/all_to_all | solution.py:463
  78.9 3.4 %copy-start.23 = (f32[16,24,128]{2,1,0:T(8,128)}, f32[16,24,128]{2,1,0:T(8,128)S(1)}, u32[]{:S(2)}) copy-start(f32[16,24,128]{2,1,0:T(8,128)S(1)} %all-to-all-done.1) | copy-start | bytes 589828
  95.0 24.8 %all-to-all-start.2 = ((f32[32,1,2304]{2,1,0:T(1,128)}), f32[32,1,2304]{2,1,0:T(1,128)S(1)}, u32[]{:S(2)}, u32[]{:S(2)}) async-start(f32[32,1,2304]{2,1,0:T(1,128)} %copy.188), calls=%async_computation.2 | async-start | bytes 589824 | tf_op jit(solution)/shard_map/all_to_all | solution.py:397
  119.7 5.9 %copy-start.22 = (f32[32,1,2304]{2,1,0:T(1,128)}, f32[32,1,2304]{2,1,0:T(1,128)S(1)}, u32[]{:S(2)}) copy-start(f32[32,1,2304]{2,1,0:T(1,128)S(1)} %all-to-all-done.2) | copy-start | bytes 884740
  119.7 19.0 %all-to-all-start.5 = ((f32[16,3,8,256]{3,2,1,0:T(8,128)}), f32[16,3,8,256]{3,2,1,0:T(8,128)}, u32[]{:S(2)}, u32[]{:S(2)}) async-start(f32[16,3,8,256]{3,2,1,0:T(8,128)} %copy.206), calls=%async_computation.5 | async-start | bytes 786432 | tf_op jit(solution)/shard_map/all_to_all | solution.py:470
  125.7 6.4 %copy-start.24 = (f32[16,24,128]{2,1,0:T(8,128)S(1)}, f32[16,24,128]{2,1,0:T(8,128)}, u32[]{:S(2)}) copy-start(f32[16,24,128]{2,1,0:T(8,128)} %copy-done.23) | copy-start | bytes 589828
  130.7 1.4 copy-start.1
  139.7 14.1 %copy-start.8 = (f32[96,192]{1,0:T(8,128)S(1)}, f32[96,192]{1,0:T(8,128)}, u32[]{:S(2)}) copy-start(f32[96,192]{1,0:T(8,128)} %constant.99.clone.perm_ref) | copy-start | bytes 221188
  143.0 10.9 %all-to-all-start.6 = ((f32[8,24,128]{2,1,0:T(8,128)}), f32[8,24,128]{2,1,0:T(8,128)S(1)}, u32[]{:S(2)}, u32[]{:S(2)}) async-start(f32[8,24,128]{2,1,0:T(8,128)} %pad.4), calls=%async_computation.6 | async-start | bytes 196608 | tf_op jit(solution)/shard_map/all_to_all | solution.py:474
  153.8 1.7 copy-start.2
  174.7 20.4 %copy-start.19 = (f32[2,256,1024,1]{2,1,0,3:T(8,128)S(1)}, f32[2,256,1024,1]{2,1,0,3:T(8,128)}, u32[]{:S(2)}) copy-start(f32[2,256,1024,1]{2,1,0,3:T(8,128)} %constant.115) | copy-start | bytes 6291460
  174.8 9.9 %all-to-all-start.7 = ((f32[8,24,128]{2,1,0:T(8,128)}), f32[8,24,128]{2,1,0:T(8,128)S(1)}, u32[]{:S(2)}, u32[]{:S(2)}) async-start(f32[8,24,128]{2,1,0:T(8,128)} %get-tuple-element.16), calls=%async_computation.7 | async-start | bytes 196608 | tf_op jit(solution)/shard_map/all_to_all | solution.py:486
  184.6 24.8 %all-to-all-start.3 = ((f32[32,1,2304]{2,1,0:T(1,128)}), f32[32,1,2304]{2,1,0:T(1,128)S(1)}, u32[]{:S(2)}, u32[]{:S(2)}) async-start(f32[32,1,2304]{2,1,0:T(1,128)} %all_to_all.48), calls=%async_computation.3 | async-start | bytes 589824 | tf_op jit(solution)/shard_map/all_to_all | solution.py:406
  210.2 17.8 %all-to-all-start.8 = ((f32[16,3,8,256]{3,2,1,0:T(8,128)}), f32[16,3,8,256]{3,2,1,0:T(8,128)S(1)}, u32[]{:S(2)}, u32[]{:S(2)}) async-start(f32[16,3,8,256]{3,2,1,0:T(8,128)} %broadcast_in_dim.62), calls=%async_computation.8 | async-start | bytes 786432 | tf_op jit(solution)/shard_map/all_to_all | solution.py:488
  218.3 9.8 %copy-start.18 = (f32[16,12,256]{2,1,0:T(8,128)S(1)}, f32[16,12,256]{2,1,0:T(8,128)}, u32[]{:S(2)}) copy-start(f32[16,12,256]{2,1,0:T(8,128)} %copy-done.17) | copy-start | bytes 589828
  222.5 5.8 %copy-start.14 = (f32[16,12,256]{2,1,0:T(8,128)S(1)}, f32[16,12,256]{2,1,0:T(8,128)}, u32[]{:S(2)}) copy-start(f32[16,12,256]{2,1,0:T(8,128)} %copy-done.13) | copy-start | bytes 589828
  222.5 5.8 %copy-start.16 = (f32[16,12,256]{2,1,0:T(8,128)S(1)}, f32[16,12,256]{2,1,0:T(8,128)}, u32[]{:S(2)}) copy-start(f32[16,12,256]{2,1,0:T(8,128)} %copy-done.15) | copy-start | bytes 589828
  228.0 1.7 collective-permute-start.1
  228.2 1.7 copy-start.12
  230.4 1.4 copy-start.21

commit v2 on v1

--- a/solution.py
+++ b/solution.py
@@ -1,3 +1,4 @@
+import ml_dtypes
 import numpy as np
 
 import jax
@@ -58,27 +59,46 @@
     det = damping**2 + coupling**2
     keep = (m[None, :] + n[:, None] < NT).astype(np.float64)
     update = np.stack([keep / damping, keep * damping / det, keep * coupling / det])
+    twice = np.stack(
+        [
+            keep / damping**2,
+            keep * (damping**2 - coupling**2) / det**2,
+            keep * 2.0 * damping * coupling / det**2,
+        ]
+    )
     row_weights = np.transpose(update * weights[None, :, None], (1, 0, 2)).reshape(NT, 3 * M)
+    parity = basis.reshape(NT, 16, 2, LAT_DEV)
+    spread = np.zeros((2, NT, 16, 16))
+    spread[:, :, :, :LAT_DEV] = np.transpose(parity, (2, 0, 1, 3))
+    spread = spread.reshape(2, NT, 256)
     f = np.float32
     return dict(
-        forward=forward.astype(f),
-        inverse=inverse.astype(f),
-        forward_seg=forward_seg.reshape(SEGS * 128, 2 * M).astype(f),
-        inverse_seg=inverse_seg.reshape(2 * M, SEGS * 128).astype(f),
-        to_spec=(basis * weights[:, None]).astype(f),
-        from_spec=np.ascontiguousarray(basis.T).astype(f),
-        update=update.astype(f),
+        forward=pair_of(forward),
+        inverse=pair_of(inverse),
+        forward_seg=pair_of(forward_seg.reshape(SEGS * 128, 2 * M)),
+        inverse_seg=pair_of(inverse_seg.reshape(2 * M, SEGS * 128)),
+        to_spec=pair_of(spread * weights[None, :, None]),
+        from_spec=pair_of(np.transpose(spread, (0, 2, 1))),
+        basis=np.ascontiguousarray(basis.T).astype(f),
+        twice=np.ascontiguousarray(np.transpose(twice.reshape(3, NT, 2, 128), (2, 0, 1, 3))).astype(f),
         row_weights=row_weights.astype(f),
     )
 
 
+def pair_of(x):
+    x = x.astype(np.float32)
+    high = x.astype(ml_dtypes.bfloat16)
+    low = (x - high.astype(np.float32)).astype(ml_dtypes.bfloat16)
+    return np.stack((high, low))
+
+
 def permutations():
-    natural = np.zeros((K, SEGS * 24), np.float32)
-    grouped = np.zeros((K, SEGS * 24), np.float32)
+    natural = np.zeros((K, SEGS * 16), np.float32)
+    grouped = np.zeros((K, SEGS * 16), np.float32)
     for s in range(SEGS):
         for i in range(KD):
-            natural[KD * s + i, 24 * s + i] = 1.0
-            grouped[KD * s + i, 24 * s + (i % 3) * 4 + i // 3] = 1.0
+            natural[KD * s + i, 16 * s + i] = 1.0
+            grouped[KD * s + i, 16 * s + (i % 3) * 4 + i // 3] = 1.0
     return natural, grouped
 
 
@@ -204,13 +224,13 @@
         )
 
     if with_mean:
-        total = lax.fori_loop(0, CELLS // TILE, step, jnp.zeros((2 * K + 16, 128), F32))
+        total = lax.fori_loop(0, CELLS // TILE, step, jnp.zeros((2 * K + 16, 128), F32), unroll=CELLS // TILE)
         counts = total[2 * K : 2 * K + 8]
         inv = jnp.where(counts > 0.0, 1.0 / jnp.maximum(counts, 1.0), 0.0)
         inv_ref[...] = inv
         mean_ref[...] = (total[:K] + total[K : 2 * K]) * inv[0:1]
     else:
-        lax.fori_loop(0, CELLS // TILE, step, 0)
+        lax.fori_loop(0, CELLS // TILE, step, 0, unroll=CELLS // TILE)
 
 
 VMEM_SPEC = pl.BlockSpec(memory_space=pltpu.VMEM)
@@ -228,7 +248,8 @@
         out_specs=[VMEM_SPEC] * len(shapes),
         out_shape=shapes,
         scratch_shapes=[pltpu.VMEM((K, CELLS + 256), F32), pltpu.SemaphoreType.DMA],
-        compiler_params=pltpu.CompilerParams(vmem_limit_bytes=40 << 20),
+        cost_estimate=pl.CostEstimate(flops=1 << 30, bytes_accessed=12 << 20, transcendentals=0),
+        compiler_params=pltpu.CompilerParams(vmem_limit_bytes=16 << 20),
         name="inner",
     )(*args)
     return out if with_mean else out[0]
@@ -263,7 +284,7 @@
     )
     profile = jnp.dot(
         perm_ref[...],
-        prof_ref[...].reshape(SEGS * 24, 128),
+        prof_ref[...].reshape(SEGS * 16, 128),
         precision=HIGHEST,
         preferred_element_type=F32,
     )
@@ -291,7 +312,7 @@
         ext1[:, pl.ds(start, TILE)] += forced
         return 0
 
-    lax.fori_loop(0, CELLS // TILE + 1, force_step, 0)
+    lax.fori_loop(0, CELLS // TILE + 1, force_step, 0, unroll=CELLS // TILE + 1)
 
     def second_step(t, _):
         start = pl.multiple_of(t * TILE, TILE)
@@ -302,7 +323,7 @@
         )
         return 0
 
-    lax.fori_loop(0, CELLS // TILE + 1, second_step, 0)
+    lax.fori_loop(0, CELLS // TILE + 1, second_step, 0, unroll=CELLS // TILE + 1)
 
     def third_step(t, total):
         start = pl.multiple_of(t * TILE, TILE)
@@ -316,7 +337,7 @@
             rows, hits, (((1,), (1,)), ((), ())), preferred_element_type=F32
         )
 
-    total = lax.fori_loop(0, CELLS // TILE, third_step, jnp.zeros((2 * K, 128), F32))
+    total = lax.fori_loop(0, CELLS // TILE, third_step, jnp.zeros((2 * K, 128), F32), unroll=CELLS // TILE)
     end = (total[:K] + total[K:]) * inv_ref[0:1]
     end_ref[...] = end
     tendency = jnp.where(lane < COLS, end - mean, 0.0)
@@ -325,11 +346,11 @@
         out_ref[:, 0:128], out_ref[:, CELLS - 128 :], end[:, 0:1], end[:, COLS - 1 : COLS]
     )
     for s in range(SEGS):
-        send_ref[s, 0:16, :] = sent[24 * s : 24 * s + 16]
+        send_ref[s, 0:16, :] = sent[16 * s : 16 * s + 16]
         send_ref[s, 16:24, :] = edge
 
 
-def outer(seg, base, clouds, profile, halo, perm, back, mean, inv, col, diffusivity, wind, mixing):
+def outer(seg, halo_block, base, clouds, profile, halo, perm, back, mean, inv, col, diffusivity, wind, mixing):
     ends = CELLS // 256 - 1
     full = lambda shape: pl.BlockSpec(shape, lambda i, seg: (0,) * len(shape))
     return pl.pallas_call(
@@ -341,10 +362,10 @@
                 ANY_SPEC,
                 pl.BlockSpec((K, 256), lambda i, seg: (0, 0)),
                 pl.BlockSpec((K, 256), lambda i, seg: (0, ends)),
-                full((SEGS, 24, 128)),
-                full((SEGS, 24, 128)),
-                full((K, SEGS * 24)),
-                full((SEGS * 24, K)),
+                full((SEGS, 16, 128)),
+                pl.BlockSpec((SEGS, 24, 128), lambda i, seg: (seg[1] * halo_block, 0, 0)),
+                full((K, SEGS * 16)),
+                full((SEGS * 16, K)),
                 full((K, 128)),
                 full((8, 128)),
                 full((1, CELLS)),
@@ -366,133 +387,346 @@
             jax.ShapeDtypeStruct((K, 128), F32),
             jax.ShapeDtypeStruct((SEGS, 24, 128), F32),
         ],
-        compiler_params=pltpu.CompilerParams(vmem_limit_bytes=48 << 20),
+        cost_estimate=pl.CostEstimate(flops=1 << 31, bytes_accessed=24 << 20, transcendentals=0),
+        compiler_params=pltpu.CompilerParams(vmem_limit_bytes=26 << 20),
         name="outer",
     )(seg, base, clouds, clouds, profile, halo, perm, back, mean, inv, col, diffusivity, wind, mixing)
 
 
-def dft_rows(received, table):
-    lead = received.shape[:-3]
-    rows = jnp.moveaxis(received[..., :KD, :], -3, -2).reshape(lead + (KD, SEGS * 128))
-    coeffs = jnp.dot(rows, table, precision=HIGH).reshape(lead + (3, 4, 2, M))
-    return jnp.moveaxis(coeffs, -2, -3).reshape(lead + (3, 8, M))
-
-
-def weigh(factors, rows, axis):
-    vort, div, geo = rows[:, :, 0], rows[:, :, 1], rows[:, :, 2]
-    f = factors[:, :, :, None, :]
-    return jnp.stack(
-        (
-            jnp.sum(f[0] * vort, axis=axis),
-            jnp.sum(f[1] * div + f[2] * geo, axis=axis),
-            jnp.sum(f[1] * geo - f[2] * div, axis=axis),
+def upper(shape):
+    return lax.broadcasted_iota(jnp.int32, shape, len(shape) - 2) % 8 < 4
+
+
+def swap4(x):
+    tiles = x.reshape(-1, 8, x.shape[-1])
+    return pltpu.roll(tiles, 4, 1).reshape(x.shape)
+
+
+def dot3(x, table):
+    high, low = split(x)
+    rows = x.shape[0]
+    both = jnp.dot(jnp.concatenate([high, low], axis=0), table[0], preferred_element_type=F32)
+    return both[:rows] + both[rows:] + jnp.dot(high, table[1], preferred_element_type=F32)
+
+
+def dot3_left(table, x):
+    high, low = split(x)
+    cols = x.shape[1]
+    both = jnp.dot(table[0], jnp.concatenate([high, low], axis=1), preferred_element_type=F32)
+    return both[:, :cols] + both[:, cols:] + jnp.dot(table[1], high, preferred_element_type=F32)
+
+
+def received_rows(chunks, table):
+    rows = jnp.concatenate(
+        [jnp.concatenate([c[s] for s in range(SEGS)], axis=1) for c in chunks], axis=0
+    )
+    coeffs = dot3(rows, table)
+    out = []
+    first = upper((8, M))
+    for a in range(len(chunks)):
+        c = [coeffs[16 * a + 8 * i : 16 * a + 8 * i + 8, :M] for i in range(2)]
+        s = [coeffs[16 * a + 8 * i : 16 * a + 8 * i + 8, M:] for i in range(2)]
+        out.append(
+            [
+                jnp.where(first, c[0], swap4(s[0])),
+                jnp.where(first, swap4(c[0]), s[0]),
+                jnp.where(first, c[1], swap4(s[1])),
+            ]
+        )
+    return out
+
+
+def weigh(total, factors, rows):
+    vort, mix, turn = factors[:, :M], factors[:, M : 2 * M], factors[:, 2 * M :]
+    return [
+        total[0] + vort * rows[0],
+        total[1] + (mix * rows[1] + turn * rows[2]),
+        total[2] + (mix * rows[2] - turn * rows[1]),
+    ]
+
+
+def call(kernel, name, args, shapes, scratch=(), prefetch=None, limit=12, specs=None, flops=1 << 28):
+    specs = specs or [VMEM_SPEC] * len(args)
+    common = dict(
+        out_shape=shapes,
+        name=name,
+        cost_estimate=pl.CostEstimate(flops=flops, bytes_accessed=6 << 20, transcendentals=0),
+        compiler_params=pltpu.CompilerParams(vmem_limit_bytes=limit << 20),
+    )
+    outs = [VMEM_SPEC] * len(shapes)
+    if prefetch is None:
+        return pl.pallas_call(
+            kernel, in_specs=specs, out_specs=outs, scratch_shapes=list(scratch), **common
+        )(*args)
+    return pl.pallas_call(
+        kernel,
+        grid_spec=pltpu.PrefetchScalarGridSpec(
+            num_scalar_prefetch=1, grid=(), in_specs=specs, out_specs=outs,
+            scratch_shapes=list(scratch),
         ),
-        axis=1,
-    )
-
-
-def spectral_twice(rows, tab, lat):
-    sent = rows.reshape(LAT_DEV, 3, 8, LATS, 8).transpose(3, 0, 1, 2, 4)
-    sent = sent.reshape(LATS, LAT_DEV * 3 * 64)
-    got = lax.all_to_all(sent, "lat", 0, 0, tiled=True).reshape(NLAT, 3 * 64)
-    spec = jnp.dot(tab["to_spec"], got, precision=HIGH).reshape(NT, 3, 8, 8)
-    factors = lax.dynamic_slice_in_dim(tab["update"], lat * 8, 8, axis=2)[:, :, None, :]
-    vort, div, geo = spec[:, 0], spec[:, 1], spec[:, 2]
-    for _ in range(2):
-        vort = factors[0] * vort
-        div, geo = factors[1] * div + factors[2] * geo, factors[1] * geo - factors[2] * div
-    spec = jnp.stack((vort, div, geo), axis=1).reshape(NT, 3 * 64)
-    back = jnp.dot(tab["from_spec"], spec, precision=HIGH).reshape(LATS, LAT_DEV * 3 * 64)
-    got = lax.all_to_all(back, "lat", 0, 0, tiled=True)
-    return got.reshape(LATS, LAT_DEV, 3, 8, 8).transpose(1, 2, 3, 0, 4).reshape(LAT_DEV, 3, 8, M)
+        **common,
+    )(prefetch, *args)
+
+
+def rows_kernel(grid_ref, table, rows_ref, lines):
+    for v in range(3):
+        for j in range(LAT_DEV):
+            for l in range(4):
+                at = v * 48 + 4 * j + l
+                lines[at : at + 1, :] = grid_ref[j, 3 * l + v : 3 * l + v + 1, :]
+    coeffs = dot3(lines[...], table)
+    cos, sin = coeffs[:, :M], coeffs[:, M:]
+    first = upper((144, M))
+    even = jnp.where(first, cos, swap4(sin))
+    odd = jnp.where(first, swap4(cos), sin)
+    for v in range(3):
+        for i in range(6):
+            at = v * 48 + 8 * i
+            rows_ref[v, 2 * i] = even[at : at + 8]
+            rows_ref[v, 2 * i + 1] = odd[at : at + 8]
+        for j in range(LAT_DEV, 16):
+            rows_ref[v, j] = jnp.zeros((8, M), F32)
+
+
+def base_kernel(factors, rows_ref, mine_ref, others_ref):
+    def channel(c, _):
+        for half, out in ((0, mine_ref), (16, others_ref)):
+            total = [jnp.zeros((8, M), F32)] * 3
+            for j in range(LAT_DEV):
+                total = weigh(
+                    total, factors[c + half, j : j + 1, :], [rows_ref[v, j] for v in range(3)]
+                )
+            for v in range(3):
+                out[c, 8 * v : 8 * v + 8, :] = total[v]
+        return 0
+
+    lax.fori_loop(0, 16, channel, 0)
+
+
+def parts_kernel(got_ref, table, base_ref, more_ref, factors, parts_ref, pair_ref):
+    pair = received_rows([got_ref[b, :, 0:16, :] for b in range(2)], table)
+    for b in range(2):
+        for v in range(3):
+            pair_ref[b, v] = pair[b][v]
+    for c in range(16):
+        total = [
+            base_ref[c, 8 * v : 8 * v + 8, :] + more_ref[c, 8 * v : 8 * v + 8, :] for v in range(3)
+        ]
+        for b in range(2):
+            total = weigh(total, factors[c, b : b + 1, :], pair[b])
+        for v in range(3):
+            parts_ref[c, 8 * v : 8 * v + 8, :] = total[v]
+
+
+def profile_kernel(parts_ref, table, out_ref):
+    total = parts_ref[0]
+    for c in range(1, 16):
+        total = total + parts_ref[c]
+    a, b, c = total[0:8], total[8:16], total[16:24]
+    first = upper((8, M))
+    cos = jnp.concatenate([jnp.where(first, a, swap4(b)), c], axis=0)
+    sin = jnp.concatenate([jnp.where(first, swap4(a), b), swap4(c)], axis=0)
+    lines = dot3(jnp.concatenate([cos, sin], axis=1), table)
+    for s in range(SEGS):
+        out_ref[s] = lines[:, 128 * s : 128 * s + 128]
+
+
+def spread_kernel(info, rows_ref, pair_ref, send_ref, held):
+    for h in range(2):
+        held[h] = rows_ref[:, :, :, 128 * h : 128 * h + 128].reshape(384, 128)
+        for v in range(3):
+            at = pl.ds(pl.multiple_of((v * 16 + info[2]) * 8, 8), 8)
+            held[h, at, :] += pair_ref[info[1], v, :, 128 * h : 128 * h + 128]
+    for u in range(8):
+        for h in range(2):
+            send_ref[2 * u + h] = held[h, pl.ds(u, 48, stride=8), :]
+
+
+def settle_kernel(info, mine_ref, others_ref, to_spec, from_spec, twice, out_ref):
+    core, half = info[1], info[3]
+
+    def columns(ref):
+        return jnp.concatenate(
+            [ref[:, 16 * v : 16 * v + 16, :].reshape(256, 128) for v in range(3)], axis=1
+        )
+
+    spec = dot3_left([to_spec[0, core], to_spec[1, core]], columns(mine_ref)) + dot3_left(
+        [to_spec[0, 1 - core], to_spec[1, 1 - core]], columns(others_ref)
+    )
+    vort, div, geo = spec[:, :128], spec[:, 128:256], spec[:, 256:]
+    f0, f1, f2 = twice[half, 0], twice[half, 1], twice[half, 2]
+    spec = jnp.concatenate([f0 * vort, f1 * div + f2 * geo, f1 * geo - f2 * div], axis=1)
+    back = dot3_left([from_spec[0, core], from_spec[1, core]], spec)
+    for v in range(3):
+        out_ref[:, 16 * v : 16 * v + 16, :] = back[:, 128 * v : 128 * v + 128].reshape(16, 16, 128)
+
+
+def last_kernel(got_ref, table, out_ref):
+    rows = received_rows([got_ref[:, 0:16, :]], table)[0]
+    line = jnp.concatenate(rows, axis=0)
+    for c in range(16):
+        out_ref[c] = line
+
+
+def add_channels(factors, half, from_ref, held):
+    def row_pair(i, _):
+        for h in range(2):
+            j = 2 * i + h
+            total = [held[v, j] for v in range(3)]
+            for c in range(16):
+                total = weigh(
+                    total,
+                    factors[c + half, pl.ds(j, 1), :],
+                    [from_ref[c, 8 * v : 8 * v + 8, :] for v in range(3)],
+                )
+            for v in range(3):
+                held[v, j] = total[v]
+        return 0
+
+    lax.fori_loop(0, LAT_DEV // 2, row_pair, 0)
+
+
+def gather_kernel(got_ref, factors, from_ref, held, flat):
+    for u in range(8):
+        for h in range(2):
+            flat[h, pl.ds(u, 48, stride=8), :] = got_ref[2 * u + h]
+    for h in range(2):
+        held[:, :, :, 128 * h : 128 * h + 128] = flat[h].reshape(3, 16, 8, 128)
+    add_channels(factors, 0, from_ref, held)
+
+
+def finish_kernel(part_ref, factors, from_ref, table, out_ref, held):
+    held[...] = part_ref[...]
+    add_channels(factors, 16, from_ref, held)
+    first = upper((8, M))
+    cos, sin = [], []
+    for v in range(3):
+        for i in range(6):
+            even, odd = held[v, 2 * i], held[v, 2 * i + 1]
+            cos.append(jnp.where(first, even, swap4(odd)))
+            sin.append(jnp.where(first, swap4(even), odd))
+    rows = jnp.concatenate(
+        [jnp.concatenate(cos, axis=0), jnp.concatenate(sin, axis=0)], axis=1
+    )
+    lines = dot3(rows, table)
+    for v in range(3):
+        for j in range(LAT_DEV):
+            for l in range(4):
+                at = v * 48 + 4 * j + l
+                out_ref[j, 3 * l + v : 3 * l + v + 1, :] = lines[at : at + 1]
+
+
+def shape(*dims):
+    return jax.ShapeDtypeStruct(dims, F32)
+
+
+def rows_exchange(x):
+    return lax.all_to_all(x, "lat", 0, 0, axis_index_groups=ROW_GROUPS, tiled=True)
+
+
+def core_swap(x):
+    return lax.ppermute(x, "lat", CORE_SWAP)
 
 
 def shards(atmosphere, cloud_state, channel_lat, cell_column, channel_wind, diffusivity, mixing):
     tab = {name: jnp.asarray(value) for name, value in tables().items()}
     natural, grouped = permutations()
-    lat = lax.axis_index("lat")
-    seg = lax.axis_index("seg").astype(jnp.int32).reshape(1)
+    lat = lax.axis_index("lat").astype(jnp.int32)
+    seg = lax.axis_index("seg").astype(jnp.int32)
     core = lat % 2
     chip = lat // 2
-    offset = channel_lat - (lat * LAT_DEV).astype(jnp.int32)
+    offset = channel_lat - lat * LAT_DEV
+    info = jnp.stack((seg, core, offset[0], chip % 2))
     clouds = cloud_state[0]
     col = cell_column
     wind = channel_wind.reshape(K, 1)
     diff = diffusivity.reshape(K, 1)
 
-    position = lax.all_to_all(
-        jnp.broadcast_to(channel_lat[None, :], (LATS, 128)), "lat", 0, 0, tiled=True
-    )[:, 0]
-
     first_send = prepare(offset, atmosphere, clouds, col)
     first_got = lax.all_to_all(first_send, "seg", 0, 0, tiled=True)
+    channel_lat, grid, first_send = lax.optimization_barrier((channel_lat, atmosphere, first_send))
+
+    own_position = jnp.broadcast_to(channel_lat.astype(F32)[None, :], (1, 128))
+    partner_position = core_swap(own_position)
+    positions = rows_exchange(
+        jnp.broadcast_to(
+            jnp.concatenate((own_position, partner_position), axis=0)[None], (16, 2, 128)
+        )
+    )[:, :, 0]
+    pair_positions = jnp.stack((own_position[0, 0], partner_position[0, 0]))
+    pair_positions = jnp.where(core == 0, pair_positions, pair_positions[::-1])
+    wanted = jnp.concatenate((positions[:, 0], positions[:, 1], pair_positions))
+    picks = (wanted.astype(jnp.int32)[:, None] == jnp.arange(NLAT, dtype=jnp.int32)[None, :])
+    basis = jnp.dot(picks.astype(F32), tab["basis"], precision=HIGHEST)
+    here = lax.dynamic_slice_in_dim(tab["basis"], lat * LAT_DEV, LAT_DEV, axis=0)
+    here = jnp.pad(here, ((0, 4), (0, 0)))
+    pair = jnp.pad(basis[32:], ((0, 6), (0, 0)))
+    products = (basis[:32, None] * here[None]).reshape(32 * 16, NT)
+    factors = jnp.dot(products, tab["row_weights"], precision=HIGH).reshape(32, 16, 3 * M)
+    products = (basis[:16, None] * pair[None]).reshape(16 * 8, NT)
+    pair_factors = jnp.dot(products, tab["row_weights"], precision=HIGH).reshape(16, 8, 3 * M)
+
     base, mean, inv = inner(clouds, col, diff, wind, mixing, True)
 
-    basis = tab["from_spec"]
-    picks = (position[:, None] == jnp.arange(NLAT, dtype=jnp.int32)[None, :]).astype(F32)
-    channel_basis = jnp.dot(picks, basis, precision=HIGHEST).reshape(16, 2, NT)
-    mine = lax.dynamic_index_in_dim(channel_basis, core, 1, keepdims=False)
-    others = lax.dynamic_index_in_dim(channel_basis, 1 - core, 1, keepdims=False)
-    here = lax.dynamic_slice_in_dim(basis, lat * LAT_DEV, LAT_DEV, axis=0)
-    pair = lax.dynamic_index_in_dim(channel_basis, chip, 0, keepdims=False)
-    products = jnp.concatenate(
-        (
-            (mine[:, None] * here[None]).reshape(-1, NT),
-            (others[:, None] * here[None]).reshape(-1, NT),
-            (mine[:, None] * pair[None]).reshape(-1, NT),
-        ),
-        axis=0,
-    )
-    weights = jnp.dot(products, tab["row_weights"], precision=HIGH).reshape(-1, 3, M)
-    weights = weights.transpose(1, 0, 2)
-    to_mine = weights[:, :192].reshape(3, 16, LAT_DEV, M)
-    to_others = weights[:, 192:384].reshape(3, 16, LAT_DEV, M)
-    to_pair = weights[:, 384:].reshape(3, 16, 2, M)
-
-    ordered = atmosphere.reshape(LAT_DEV, 4, 3, NLON).transpose(0, 2, 1, 3).reshape(-1, NLON)
-    rows = jnp.dot(ordered, tab["forward"], precision=HIGH).reshape(LAT_DEV, 3, 4, 2, M)
-    rows = rows.transpose(0, 1, 3, 2, 4).reshape(LAT_DEV, 3, 8, M)
-    base_mine = weigh(to_mine, rows[None], 1)
-    base_others = weigh(to_others, rows[None], 1)
-    base_sum = base_mine + lax.ppermute(base_others, "lat", CORE_SWAP)
+    rows = call(
+        rows_kernel, "rows", (grid, tab["forward"]), [shape(3, 16, 8, M)],
+        scratch=[pltpu.VMEM((144, NLON), F32)],
+    )[0]
+    base_mine, base_others = call(
+        base_kernel, "base", (factors, rows), [shape(16, 24, M), shape(16, 24, M)]
+    )
+    base_more = core_swap(base_others)
 
     clouds, mean_1, send = outer(
-        seg, base, clouds, first_got, first_got, jnp.asarray(natural), jnp.asarray(grouped.T.copy()),
+        info, 0, base, clouds, first_got, first_got, jnp.asarray(natural), jnp.asarray(grouped.T.copy()),
         mean, inv, col, diff, wind, mixing,
     )
     got = lax.all_to_all(
         jnp.concatenate((send, send), axis=0), ("lat", "seg"), 0, 0,
         axis_index_groups=CHIP_GROUPS, tiled=True,
-    ).reshape(2, SEGS, 24, 128)
+    )
     base = inner(clouds, col, diff, wind, mixing, False)
-    pair_rows = dft_rows(got, tab["forward_seg"])
-    parts = base_sum + weigh(to_pair, pair_rows[None], 1)
-    parts = lax.all_to_all(parts, "lat", 0, 0, axis_index_groups=ROW_GROUPS, tiled=True)
-    profile_rows = jnp.sum(parts, axis=0).reshape(3, 2, 4, M).transpose(0, 2, 1, 3).reshape(KD, 2 * M)
-    profile = jnp.dot(profile_rows, tab["inverse_seg"], precision=HIGH).reshape(KD, SEGS, 128)
-    profile = jnp.pad(profile.transpose(1, 0, 2), ((0, 0), (0, 24 - KD), (0, 0)))
+    parts, pair_rows = call(
+        parts_kernel, "parts",
+        (got.reshape(2, SEGS, 24, 128), tab["forward_seg"], base_mine, base_more, pair_factors),
+        [shape(16, 24, M), shape(2, 3, 8, M)],
+    )
+    parts = rows_exchange(parts)
+    profile = call(
+        profile_kernel, "profile", (parts, tab["inverse_seg"]), [shape(SEGS, 16, 128)]
+    )[0]
     profile = lax.all_to_all(profile, "seg", 0, 0, tiled=True)
 
-    own_row = lax.dynamic_index_in_dim(pair_rows, core, 0)
-    at_channel = jnp.arange(LAT_DEV, dtype=jnp.int32) == offset[0]
-    forced_rows = rows + jnp.where(at_channel[:, None, None, None], own_row, 0.0)
-    settled = spectral_twice(forced_rows, tab, lat)
-
-    halo = lax.dynamic_index_in_dim(got, core, 0, keepdims=False)
+    spread = call(
+        spread_kernel, "spread", (rows, pair_rows), [shape(16, 48, 128)],
+        scratch=[pltpu.VMEM((2, 384, 128), F32)], prefetch=info,
+    )[0]
+    spec_mine = rows_exchange(spread)
+    spec_others = core_swap(spec_mine)
+    settled = call(
+        settle_kernel, "settle",
+        (spec_mine, spec_others, tab["to_spec"], tab["from_spec"], tab["twice"]),
+        [shape(16, 48, 128)], prefetch=info,
+    )[0]
+    settled = rows_exchange(settled)
+
     clouds, _, send = outer(
-        seg, base, clouds, profile, halo, jnp.asarray(grouped), jnp.asarray(grouped.T.copy()),
+        info, 1, base, clouds, profile, got, jnp.asarray(grouped), jnp.asarray(grouped.T.copy()),
         mean_1, inv, col, diff, wind, mixing,
     )
     got = lax.all_to_all(send, "seg", 0, 0, tiled=True)
-    last_rows = dft_rows(got, tab["forward_seg"])
-    from_mine = lax.all_to_all(
-        jnp.broadcast_to(last_rows[None], (16, 3, 8, M)), "lat", 0, 0,
-        axis_index_groups=ROW_GROUPS, tiled=True,
-    )
-    from_others = lax.ppermute(from_mine, "lat", CORE_SWAP)
-    final = settled + weigh(to_mine, from_mine[:, None], 0) + weigh(to_others, from_others[:, None], 0)
-    final = final.reshape(LAT_DEV, 3, 2, 4, M).transpose(0, 3, 1, 2, 4).reshape(LAT_DEV * KD, 2 * M)
-    grid = jnp.dot(final, tab["inverse"], precision=HIGH).reshape(LAT_DEV, KD, NLON)
+    from_mine = rows_exchange(
+        call(last_kernel, "last", (got, tab["forward_seg"]), [shape(16, 24, M)])[0]
+    )
+    from_others = core_swap(from_mine)
+    part = call(
+        gather_kernel, "gather", (settled, factors, from_mine), [shape(3, 16, 8, M)],
+        scratch=[pltpu.VMEM((2, 384, 128), F32)],
+    )[0]
+    grid = call(
+        finish_kernel, "finish", (part, factors, from_others, tab["inverse"]),
+        [shape(LAT_DEV, KD, NLON)], scratch=[pltpu.VMEM((3, 16, 8, M), F32)],
+    )[0]
     return grid, clouds[None]
 
 

time: 237 us -> 183 us (0.77)
  local copies, waits for them, and re-layouts: 46.7 us -> 23.1 us
  other arithmetic: 19.5 us -> 1.06 us
  blocking collectives: 0 us -> 17.9 us
  starting transfers between devices: 60.4 us -> 43.8 us
  Pallas kernels: 50.9 us -> 37 us
  waiting for transfers between devices: 39.7 us -> 53 us
  matrix products: 14.1 us -> 3.73 us
    pallas_call x2, Pallas kernels: 38.3 us -> 15 us  [outer(): pl.pallas_call(outer_kernel, grid_spec=pltpu.PrefetchScalarGridSpec(num_s...]
    all_to_all x0 -> x1, blocking collectives: none -> 17.9 us  [rows_exchange(): lax.all_to_all(x, 'lat', 0, 0, axis_index_groups=ROW_GROUPS, tiled=True)]
    all_to_all x5 -> x4, starting transfers between devices: 42 us -> 26.2 us  [rows_exchange(): lax.all_to_all(x, 'lat', 0, 0, axis_index_groups=ROW_GROUPS, tiled=True)]
    pallas_call x0 -> x9, Pallas kernels: none -> 15 us  [the longest x7 11.4 us: call(): pl.pallas_call(kernel, in_specs=specs, out_specs=outs, scratch_shapes=lis...]
    unnamed x63 -> x64, local copies, waits for them, and re-layouts: 8.92 us -> 19.8 us
    dot_general x9 -> x3, matrix products: 14.1 us -> 3.73 us  [the longest x1 1.97 us: shards(): jnp.dot(products, tab['row_weights'], precision=HIGH).reshape(32, 16, 3 * M)]
    reshape x7 -> x0, local copies, waits for them, and re-layouts: 10.2 us -> none  [the longest x1 4.17 us: spectral_twice(): got.reshape(LATS, LAT_DEV, 3, 8, 8).transpose(1, 2, 3, 0, 4)]
    all_to_all x5 -> x4, waiting for transfers between devices: 29.5 us -> 38.7 us  [rows_exchange(): lax.all_to_all(x, 'lat', 0, 0, axis_index_groups=ROW_GROUPS, tiled=True)]
  transfers between devices with their start and end apart: 11 -> 12, of which waited for: 7 -> 9; matrix products, arithmetic and copies ran while one was open for 27% -> 4% of each run, Pallas kernels for 14% -> 13%
where the time goes in v2:
time: 183 us; the launch traced here: 181 us
  waiting for transfers between devices  53 us (29%)
  starting transfers between devices  43.8 us (24%)
  Pallas kernels  37 us (20%)
  local copies, waits for them, and re-layouts  23.1 us (13%)
  blocking collectives  17.9 us (10%)
  matrix products  3.73 us (2%)
    all_to_all x4, waiting for transfers between devices, rows_exchange(): lax.all_to_all(x, 'lat', 0, 0, axis_index_groups=ROW_GROUPS, tiled=True)  38.7 us
    all_to_all x4, starting transfers between devices, rows_exchange(): lax.all_to_all(x, 'lat', 0, 0, axis_index_groups=ROW_GROUPS, tiled=True)  26.2 us
    unnamed x64, local copies, waits for them, and re-layouts  19.8 us
    all_to_all x1, blocking collectives, rows_exchange(): lax.all_to_all(x, 'lat', 0, 0, axis_index_groups=ROW_GROUPS, tiled=True)  17.9 us
    pallas_call x2, Pallas kernels, outer(): pl.pallas_call(outer_kernel, grid_spec=pltpu.PrefetchScalarGridSpec(num_s...  15 us
    pallas_call x7, Pallas kernels, call(): pl.pallas_call(kernel, in_specs=specs, out_specs=outs, scratch_shapes=lis...  11.4 us
    all_to_all x1, waiting for transfers between devices, shards(): lax.all_to_all(jnp.concatenate((send, send), axis=0), ('lat', 'seg'), 0,...  5.67 us
    pallas_call x2, Pallas kernels, inner(): pl.pallas_call(lambda *refs: inner_kernel(with_mean, *refs), in_specs=[AN...  5.12 us
  transfers between devices with their start and end apart: 12, of which 9 were waited for; matrix products, arithmetic and copies ran while one was open for 4% of the time, Pallas kernels for 13%

profile of v2, /device:TPU:32, one launch (start us, length us, event | category | flops | bytes accessed | tf_op | source)
XLA Modules:
  0.0 181.2 jit_solution(2994801399146671344)
XLA Ops:
  1.4 0.8 copy.31.refs_3_.wind_ref.refs_2_
  2.2 0.8 copy.30.refs_2_.diff_ref.refs_1_
  3.0 1.9 %prepare.1 = f32[8,24,128]{2,1,0:T(8,128)} custom-call(s32[1]{0:T(128)S(6)} %sub.11.off_ref, f32[12,12,768]{2,1,0:T(8,128)} %grid_ref, f32[96,6144]{1,0:T(8,128)} %bitcast.22, f32[96,6144]{1,0:T(8,128)} %bitcast.23, s32[1,6144]{1,0:T(1,128)} %col_ref.3, s32[1,6144]{1,0:T(1,128)} %col_ref.3), custom_call_target="tpu_custom_call" | custom-call | tf_op jit(solution)/shard_map/prepare/pallas_call | solution.py:181
  4.9 0.9 constant_dynamic-slice_fusion
  5.9 2.6 %inner.2 = (f32[96,6144]{1,0:T(8,128)S(1)}, f32[96,128]{1,0:T(8,128)S(1)}, f32[8,128]{1,0:T(8,128)S(1)}) custom-call(f32[96,6144]{1,0:T(8,128)S(1)} %bitcast.24, s32[1,6144]{1,0:T(1,128)S(1)} %copy-done.16, f32[96,1]{1,0:T(8,128)S(1)} %copy.30.refs_2_.diff_ref.refs_1_, f32[96,1]{1,0:T(8,128)S(1)} %copy.31.refs_3_.wind_ref.refs_2_, f32[96,96]{1,0:T(8,128)S(1)} %copy-done.17), custom_call_target="tpu_custom_call" | custom-call | flops 1073741824 | bytes 12582912 | tf_op jit(solution)/shard_map/inner/pallas_call | solution.py:245
  8.5 1.4 copy-done.24
  11.4 11.2 %all-to-all-start.2 = ((f32[16,2,128]{2,1,0:T(2,128)}), f32[16,2,128]{2,1,0:T(2,128)S(1)}, u32[]{:S(2)}, u32[]{:S(2)}) async-start(f32[16,2,128]{2,1,0:T(2,128)} %broadcast_in_dim.10), calls=%async_computation.2 | async-start | bytes 32768 | tf_op jit(solution)/shard_map/all_to_all | solution.py:624
  22.7 8.6 %all-to-all-done.2 = f32[16,2,128]{2,1,0:T(2,128)S(1)} async-done(((f32[16,2,128]{2,1,0:T(2,128)}), f32[16,2,128]{2,1,0:T(2,128)S(1)}, u32[]{:S(2)}, u32[]{:S(2)}) %all-to-all-start.2) | async-done | bytes 16416 | tf_op jit(solution)/shard_map/all_to_all | solution.py:624
  31.3 4.4 %all-to-all-start = ((f32[8,24,128]{2,1,0:T(8,128)}), f32[8,24,128]{2,1,0:T(8,128)S(1)}, u32[]{:S(2)}, u32[]{:S(2)}) async-start(f32[8,24,128]{2,1,0:T(8,128)} %prepare.1), calls=%async_computation | async-start | bytes 196608 | tf_op jit(solution)/shard_map/all_to_all | solution.py:646
  36.2 2.0 %fusion.factors = f32[32,16,768]{2,1,0:T(8,128)S(1)} fusion(f32[256,768,1]{1,0,2:T(8,128)} %constant.91, f32[16,256]{1,0:T(8,128)S(1)} %pad.9, f32[32,256]{1,0:T(8,128)S(1)} %slice.30), kind=kOutput, calls=%fused_computation | convolution fusion | flops 604110848 | bytes 2408448 | tf_op jit(solution)/shard_map/dot_general | solution.py:665
  38.3 2.5 %base.1 = (f32[16,24,256]{2,1,0:T(8,128)S(1)}, f32[16,24,256]{2,1,0:T(8,128)}) custom-call(f32[32,16,768]{2,1,0:T(8,128)S(1)} %fusion.factors, f32[3,16,8,256]{3,2,1,0:T(8,128)S(1)} %rows.1.rows_ref), custom_call_target="tpu_custom_call" | custom-call | flops 268435456 | bytes 6291456 | tf_op jit(solution)/shard_map/base/pallas_call | solution.py:458
  40.8 1.4 all-to-all-done.prof_ref.halo_ref
  42.2 1.7 copy-done.1
  43.8 1.7 copy-done.25
  45.5 0.8 copy-done.29
  46.3 6.9 %outer.2 = (f32[96,6144]{1,0:T(8,128)S(1)}, f32[96,128]{1,0:T(8,128)S(1)}, f32[8,24,128]{2,1,0:T(8,128)S(1)}) custom-call(s32[4]{0:T(128)S(1)} %pad_add_fusion.seg_ref.info, f32[96,6144]{1,0:T(8,128)S(1)} %copy-done.25, f32[96,6144]{1,0:T(8,128)S(1)} %bitcast.25, f32[96,6144]{1,0:T(8,128)S(1)} %bitcast.26, f32[8,24,128]{2,1,0:T(8,128)S(1)} %all-to-all-done.prof_ref.halo_ref, ...), custom_call_target="tpu_custom_call" | custom-call | flops 2147483648 | bytes 25165824 | tf_op jit(solution)/shard_map/outer/pallas_call | solution.py:356
  53.3 1.4 copy-done.4
  55.3 0.7 pad_maximum_fusion
  56.0 4.5 %all-to-all-start.1 = ((f32[16,24,128]{2,1,0:T(8,128)}), f32[16,24,128]{2,1,0:T(8,128)S(1)}, u32[]{:S(2)}, u32[]{:S(2)}) async-start(f32[16,24,128]{2,1,0:T(8,128)} %pad_maximum_fusion), calls=%async_computation.1 | async-start | bytes 393216 | tf_op jit(solution)/shard_map/all_to_all | solution.py:684
  60.5 1.5 fusion.4.factors
  62.0 5.7 %all-to-all-done.1.halo_ref = f32[16,24,128]{2,1,0:T(8,128)S(1)} async-done(((f32[16,24,128]{2,1,0:T(8,128)}), f32[16,24,128]{2,1,0:T(8,128)S(1)}, u32[]{:S(2)}, u32[]{:S(2)}) %all-to-all-start.1) | async-done | bytes 196640 | tf_op jit(solution)/shard_map/all_to_all | solution.py:684
  67.7 1.6 copy-done.2
  70.5 17.9 %all_to_all.45.parts_ref = f32[16,24,256]{2,1,0:T(8,128)S(1)} all-to-all(f32[16,24,256]{2,1,0:T(8,128)S(1)} %get-tuple-element.26), channel_id=1, replica_groups={{0,16,32,48,64,80,96,112,128,144,160,176,192,208,224,240},{8,24,40,56,7..., dimensions={0} | all-to-all | bytes 786432 | tf_op jit(solution)/shard_map/all_to_all | solution.py:624
  88.4 1.1 profile.1
  89.5 3.6 %all-to-all-start.6 = ((f32[8,16,128]{2,1,0:T(8,128)}), f32[8,16,128]{2,1,0:T(8,128)S(1)}, u32[]{:S(2)}, u32[]{:S(2)}) async-start(f32[8,16,128]{2,1,0:T(8,128)} %profile.1), calls=%async_computation.6 | async-start | bytes 131072 | tf_op jit(solution)/shard_map/all_to_all | solution.py:698
  93.1 1.7 copy-done.5
  94.7 2.5 %inner.3.base_ref = f32[96,6144]{1,0:T(8,128)S(1)} custom-call(f32[96,6144]{1,0:T(8,128)S(1)} %copy-done.5, f32[96,1]{1,0:T(8,128)S(1)} %copy.30.refs_2_.diff_ref.refs_1_, f32[96,1]{1,0:T(8,128)S(1)} %copy.31.refs_3_.wind_ref.refs_2_, f32[96,96]{1,0:T(8,128)S(1)} %copy-done.17), custom_call_target="tpu_custom_call" | custom-call | flops 1073741824 | bytes 12582912 | tf_op jit(solution)/shard_map/inner/pallas_call | solution.py:245
  97.2 1.4 copy-done.7
  99.1 1.7 copy-done.6
  100.8 1.7 copy-done.8
  102.5 8.0 %outer.3 = (f32[96,6144]{1,0:T(8,128)}, f32[96,128]{1,0:T(8,128)}, f32[8,24,128]{2,1,0:T(8,128)}) custom-call(s32[4]{0:T(128)S(1)} %pad_add_fusion.seg_ref.info, f32[96,6144]{1,0:T(8,128)S(1)} %copy-done.8, f32[96,6144]{1,0:T(8,128)S(1)} %copy-done.6, f32[96,6144]{1,0:T(8,128)S(1)} %copy-done.6, f32[8,16,128]{2,1,0:T(8,128)S(1)} %all-to-all-done.6.prof_ref, ...), custom_call_target="tpu_custom_call" | custom-call | flops 2147483648 | bytes 25165824 | tf_op jit(solution)/shard_map/outer/pallas_call | solution.py:356
  110.5 5.0 %all-to-all-start.7 = ((f32[8,24,128]{2,1,0:T(8,128)}), f32[8,24,128]{2,1,0:T(8,128)S(1)}, u32[]{:S(2)}, u32[]{:S(2)}) async-start(f32[8,24,128]{2,1,0:T(8,128)} %get-tuple-element.28), calls=%async_computation.7 | async-start | bytes 196608 | tf_op jit(solution)/shard_map/all_to_all | solution.py:717
  115.4 1.4 spread.1
  116.8 5.0 %all-to-all-done.7.got_ref = f32[8,24,128]{2,1,0:T(8,128)S(1)} async-done(((f32[8,24,128]{2,1,0:T(8,128)}), f32[8,24,128]{2,1,0:T(8,128)S(1)}, u32[]{:S(2)}, u32[]{:S(2)}) %all-to-all-start.7) | async-done | bytes 98336 | tf_op jit(solution)/shard_map/all_to_all | solution.py:717
  121.9 5.6 %all-to-all-start.3 = ((f32[16,48,128]{2,1,0:T(8,128)}), f32[16,48,128]{2,1,0:T(8,128)S(1)}, u32[]{:S(2)}, u32[]{:S(2)}) async-start(f32[16,48,128]{2,1,0:T(8,128)} %spread.1), calls=%async_computation.3 | async-start | bytes 786432 | tf_op jit(solution)/shard_map/all_to_all | solution.py:624
  127.5 1.6 copy-done.3
  129.1 1.2 last.1
  130.3 10.0 %all-to-all-done.3.mine_ref = f32[16,48,128]{2,1,0:T(8,128)S(1)} async-done(((f32[16,48,128]{2,1,0:T(8,128)}), f32[16,48,128]{2,1,0:T(8,128)S(1)}, u32[]{:S(2)}, u32[]{:S(2)}) %all-to-all-start.3) | async-done | bytes 393248 | tf_op jit(solution)/shard_map/all_to_all | solution.py:624
  140.3 4.7 %all-to-all-start.8 = ((f32[16,24,256]{2,1,0:T(8,128)}), f32[16,24,256]{2,1,0:T(8,128)S(1)}, u32[]{:S(2)}, u32[]{:S(2)}) async-start(f32[16,24,256]{2,1,0:T(8,128)} %last.1), calls=%async_computation.8 | async-start | bytes 786432 | tf_op jit(solution)/shard_map/all_to_all | solution.py:624
  145.0 1.7 collective-permute-done.2.others_ref
  146.7 1.0 copy-done.14
  147.8 1.0 copy-done.15
  148.8 2.2 %settle.1 = f32[16,48,128]{2,1,0:T(8,128)} custom-call(s32[4]{0:T(128)S(1)} %pad_add_fusion.seg_ref.info, f32[16,48,128]{2,1,0:T(8,128)S(1)} %all-to-all-done.3.mine_ref, f32[16,48,128]{2,1,0:T(8,128)S(1)} %collective-permute-done.2.others_ref, bf16[2,2,256,256]{3,2,1,0:T(8,128)(2,1)S(1)} %copy-done.15, bf16[2,2,256,256]{3,2,1,0:T(8,128)(2,1)S(1)} %copy-done.14, ...), custom_call_target="tpu_custom_call" | custom-call | flops 268435456 | bytes 6291456 | tf_op jit(solution)/shard_map/settle/pallas_call | solution.py:461
  151.0 7.0 %all-to-all-done.8.from_ref = f32[16,24,256]{2,1,0:T(8,128)S(1)} async-done(((f32[16,24,256]{2,1,0:T(8,128)}), f32[16,24,256]{2,1,0:T(8,128)S(1)}, u32[]{:S(2)}, u32[]{:S(2)}) %all-to-all-start.8) | async-done | bytes 393248 | tf_op jit(solution)/shard_map/all_to_all | solution.py:624
  158.0 4.7 %all-to-all-start.4 = ((f32[16,48,128]{2,1,0:T(8,128)}), f32[16,48,128]{2,1,0:T(8,128)}, u32[]{:S(2)}, u32[]{:S(2)}) async-start(f32[16,48,128]{2,1,0:T(8,128)} %settle.1), calls=%async_computation.4 | async-start | bytes 786432 | tf_op jit(solution)/shard_map/all_to_all | solution.py:624
  162.7 13.1 %all-to-all-done.4.got_ref = f32[16,48,128]{2,1,0:T(8,128)} async-done(((f32[16,48,128]{2,1,0:T(8,128)}), f32[16,48,128]{2,1,0:T(8,128)}, u32[]{:S(2)}, u32[]{:S(2)}) %all-to-all-start.4) | async-done | bytes 393248 | tf_op jit(solution)/shard_map/all_to_all | solution.py:624
  175.8 2.1 %gather.1.part_ref = f32[3,16,8,256]{3,2,1,0:T(8,128)S(1)} custom-call(f32[16,48,128]{2,1,0:T(8,128)} %all-to-all-done.4.got_ref, f32[32,16,768]{2,1,0:T(8,128)S(1)} %fusion.factors, f32[16,24,256]{2,1,0:T(8,128)S(1)} %all-to-all-done.8.from_ref), custom_call_target="tpu_custom_call" | custom-call | flops 268435456 | bytes 6291456 | tf_op jit(solution)/shard_map/gather/pallas_call | solution.py:458
  177.9 3.4 %finish.1 = f32[12,12,768]{2,1,0:T(8,128)} custom-call(f32[3,16,8,256]{3,2,1,0:T(8,128)S(1)} %gather.1.part_ref, f32[32,16,768]{2,1,0:T(8,128)S(1)} %fusion.factors, f32[16,24,256]{2,1,0:T(8,128)} %collective-permute-done.3.from_ref, bf16[2,512,768]{2,1,0:T(8,128)(2,1)S(1)} %copy-done.11), custom_call_target="tpu_custom_call" | custom-call | flops 268435456 | bytes 6291456 | tf_op jit(solution)/shard_map/finish/pallas_call | solution.py:458
  (78 shorter events, 4.6 us)
Async XLA Ops:
  1.3 9.2 %collective-permute-start = (f32[1,128]{1,0:T(1,128)S(1)}, f32[1,128]{1,0:T(1,128)S(1)}, u32[]{:S(2)}, u32[]{:S(2)}) collective-permute-start(f32[1,128]{1,0:T(1,128)S(1)} %broadcast_in_dim.9), channel_id=1, source_target_pairs={{0,8},{8,0},{16,24},{24,16},{32,40},{40,32},{48,56},{56,48},{64,72... | collective-permute-start | bytes 1544 | tf_op jit(solution)/shard_map/ppermute | solution.py:628
  2.9 2.9 %copy-start = (f32[1,96,6144]{2,1,0:T(8,128)S(1)}, f32[1,96,6144]{2,1,0:T(8,128)}, u32[]{:S(2)}) copy-start(f32[1,96,6144]{2,1,0:T(8,128)} %param.21) | copy-start | bytes 7077892
  2.9 2.9 %copy-start.16 = (s32[1,6144]{1,0:T(1,128)S(1)}, s32[1,6144]{1,0:T(1,128)}, u32[]{:S(2)}) copy-start(s32[1,6144]{1,0:T(1,128)} %col_ref.3) | copy-start | bytes 73732
  3.0 2.9 %copy-start.17 = (f32[96,96]{1,0:T(8,128)S(1)}, f32[96,96]{1,0:T(8,128)}, u32[]{:S(2)}) copy-start(f32[96,96]{1,0:T(8,128)} %mixing_ref.3) | copy-start | bytes 110596
  4.9 5.0 %copy-start.9 = (f32[12,12,768]{2,1,0:T(8,128)S(1)}, f32[12,12,768]{2,1,0:T(8,128)}, u32[]{:S(2)}) copy-start(f32[12,12,768]{2,1,0:T(8,128)} %grid_ref) | copy-start | bytes 1327108
  4.9 5.0 %copy-start.12 = (bf16[2,768,512]{2,1,0:T(8,128)(2,1)S(1)}, bf16[2,768,512]{2,1,0:T(8,128)(2,1)}, u32[]{:S(2)}) copy-start(bf16[2,768,512]{2,1,0:T(8,128)(2,1)} %constant.68.clone.table) | copy-start | bytes 4718596
  8.5 1.4 copy-start.24
  9.9 28.3 %copy-start.28 = (f32[96,128]{1,0:T(8,128)}, f32[96,128]{1,0:T(8,128)S(1)}, u32[]{:S(2)}) copy-start(f32[96,128]{1,0:T(8,128)S(1)} %get-tuple-element.18.mean_ref) | copy-start | bytes 147460
  9.9 26.0 %copy-start.30 = (f32[384,256]{1,0:T(8,128)S(1)}, f32[384,256]{1,0:T(8,128)}, u32[]{:S(2)}) copy-start(f32[384,256]{1,0:T(8,128)} %constant.74.clone) | copy-start | bytes 1179652
  11.4 19.9 %all-to-all-start.2 = ((f32[16,2,128]{2,1,0:T(2,128)}), f32[16,2,128]{2,1,0:T(2,128)S(1)}, u32[]{:S(2)}, u32[]{:S(2)}) async-start(f32[16,2,128]{2,1,0:T(2,128)} %broadcast_in_dim.10), calls=%async_computation.2 | async-start | bytes 32768 | tf_op jit(solution)/shard_map/all_to_all | solution.py:624
  31.3 10.9 %all-to-all-start = ((f32[8,24,128]{2,1,0:T(8,128)}), f32[8,24,128]{2,1,0:T(8,128)S(1)}, u32[]{:S(2)}, u32[]{:S(2)}) async-start(f32[8,24,128]{2,1,0:T(8,128)} %prepare.1), calls=%async_computation | async-start | bytes 196608 | tf_op jit(solution)/shard_map/all_to_all | solution.py:646
  36.2 4.6 %copy-start.31 = (f32[34,256]{1,0:T(8,128)}, f32[34,256]{1,0:T(8,128)S(1)}, u32[]{:S(2)}) copy-start(f32[34,256]{1,0:T(8,128)S(1)} %fusion.8) | copy-start | bytes 104452
  36.2 5.9 %copy-start.20 = (f32[128,96]{1,0:T(8,128)S(1)}, f32[128,96]{1,0:T(8,128)}, u32[]{:S(2)}) copy-start(f32[128,96]{1,0:T(8,128)} %constant.78.clone.back_ref) | copy-start | bytes 147460
  36.2 5.9 %copy-start.23 = (f32[96,128]{1,0:T(8,128)S(1)}, f32[96,128]{1,0:T(8,128)}, u32[]{:S(2)}) copy-start(f32[96,128]{1,0:T(8,128)} %constant.77.clone.perm_ref) | copy-start | bytes 147460
  40.8 26.9 %collective-permute-start.1 = (f32[16,24,256]{2,1,0:T(8,128)}, f32[16,24,256]{2,1,0:T(8,128)S(1)}, u32[]{:S(2)}, u32[]{:S(2)}) collective-permute-start(f32[16,24,256]{2,1,0:T(8,128)} %get-tuple-element.23), channel_id=1, source_target_pairs={{0,8},{8,0},{16,24},{24,16},{32,40},{40,32},{48,56},{56,48},{64,72... | collective-permute-start | bytes 1179656 | tf_op jit(solution)/shard_map/ppermute | solution.py:628
  42.2 1.7 copy-start.1
  43.8 1.7 copy-start.25
  45.5 0.8 copy-start.29
  46.3 14.2 %slice-start = ((f32[34,256]{1,0:T(8,128)}), f32[16,256]{1,0:T(8,128)S(1)}, s32[]{:S(2)}) async-start(f32[34,256]{1,0:T(8,128)} %copy-done.31), calls=%async_computation.9 | async-start | bytes 32768 | tf_op jit(solution)/shard_map/slice | solution.py:666
  53.3 1.4 copy-start.4
  54.7 0.6 copy-start.26
  56.0 11.7 %all-to-all-start.1 = ((f32[16,24,128]{2,1,0:T(8,128)}), f32[16,24,128]{2,1,0:T(8,128)S(1)}, u32[]{:S(2)}, u32[]{:S(2)}) async-start(f32[16,24,128]{2,1,0:T(8,128)} %pad_maximum_fusion), calls=%async_computation.1 | async-start | bytes 393216 | tf_op jit(solution)/shard_map/all_to_all | solution.py:684
  67.7 1.6 copy-start.2
  69.3 19.2 %copy-start.10 = (bf16[2,512,1024]{2,1,0:T(8,128)(2,1)S(1)}, bf16[2,512,1024]{2,1,0:T(8,128)(2,1)}, u32[]{:S(2)}) copy-start(bf16[2,512,1024]{2,1,0:T(8,128)(2,1)} %constant.71.clone.table) | copy-start | bytes 6291460
  69.9 0.6 copy-start.18
  89.5 9.6 %all-to-all-start.6 = ((f32[8,16,128]{2,1,0:T(8,128)}), f32[8,16,128]{2,1,0:T(8,128)S(1)}, u32[]{:S(2)}, u32[]{:S(2)}) async-start(f32[8,16,128]{2,1,0:T(8,128)} %profile.1), calls=%async_computation.6 | async-start | bytes 131072 | tf_op jit(solution)/shard_map/all_to_all | solution.py:698
  93.0 1.7 copy-start.5
  94.7 4.4 %copy-start.21 = (f32[128,96]{1,0:T(8,128)S(1)}, f32[128,96]{1,0:T(8,128)}, u32[]{:S(2)}) copy-start(f32[128,96]{1,0:T(8,128)} %constant.78.clone.back_ref) | copy-start | bytes 147460
  94.7 4.4 %copy-start.22 = (f32[96,128]{1,0:T(8,128)S(1)}, f32[96,128]{1,0:T(8,128)}, u32[]{:S(2)}) copy-start(f32[96,128]{1,0:T(8,128)} %constant.79.clone.perm_ref) | copy-start | bytes 147460
  94.7 4.4 %copy-start.27 = (f32[96,128]{1,0:T(8,128)S(1)}, f32[96,128]{1,0:T(8,128)}, u32[]{:S(2)}) copy-start(f32[96,128]{1,0:T(8,128)} %copy-done.26) | copy-start | bytes 147460
  97.2 1.4 copy-start.7
  99.1 1.7 copy-start.6
  100.8 1.7 copy-start.8
  102.5 13.0 %copy-start.19 = (f32[2,3,8,256]{3,2,1,0:T(8,128)S(1)}, f32[2,3,8,256]{3,2,1,0:T(8,128)}, u32[]{:S(2)}) copy-start(f32[2,3,8,256]{3,2,1,0:T(8,128)} %copy-done.18) | copy-start | bytes 147460
  110.5 11.4 %all-to-all-start.7 = ((f32[8,24,128]{2,1,0:T(8,128)}), f32[8,24,128]{2,1,0:T(8,128)S(1)}, u32[]{:S(2)}, u32[]{:S(2)}) async-start(f32[8,24,128]{2,1,0:T(8,128)} %get-tuple-element.28), calls=%async_computation.7 | async-start | bytes 196608 | tf_op jit(solution)/shard_map/all_to_all | solution.py:717
  116.8 29.9 %copy-start.13 = (f32[2,3,256,128]{3,2,1,0:T(8,128)S(1)}, f32[2,3,256,128]{3,2,1,0:T(8,128)}, u32[]{:S(2)}) copy-start(f32[2,3,256,128]{3,2,1,0:T(8,128)} %constant.75.clone.twice) | copy-start | bytes 2359300
  121.9 18.4 %all-to-all-start.3 = ((f32[16,48,128]{2,1,0:T(8,128)}), f32[16,48,128]{2,1,0:T(8,128)S(1)}, u32[]{:S(2)}, u32[]{:S(2)}) async-start(f32[16,48,128]{2,1,0:T(8,128)} %spread.1), calls=%async_computation.3 | async-start | bytes 786432 | tf_op jit(solution)/shard_map/all_to_all | solution.py:624
  127.5 1.6 copy-start.3
  140.3 17.7 %all-to-all-start.8 = ((f32[16,24,256]{2,1,0:T(8,128)}), f32[16,24,256]{2,1,0:T(8,128)S(1)}, u32[]{:S(2)}, u32[]{:S(2)}) async-start(f32[16,24,256]{2,1,0:T(8,128)} %last.1), calls=%async_computation.8 | async-start | bytes 786432 | tf_op jit(solution)/shard_map/all_to_all | solution.py:624
  145.0 1.7 collective-permute-start.2
  146.7 1.0 copy-start.14
  147.8 1.0 copy-start.15
  151.0 26.9 %copy-start.11 = (bf16[2,512,768]{2,1,0:T(8,128)(2,1)S(1)}, bf16[2,512,768]{2,1,0:T(8,128)(2,1)}, u32[]{:S(2)}) copy-start(bf16[2,512,768]{2,1,0:T(8,128)(2,1)} %constant.69.clone.table) | copy-start | bytes 4718596
  158.0 17.8 %all-to-all-start.4 = ((f32[16,48,128]{2,1,0:T(8,128)}), f32[16,48,128]{2,1,0:T(8,128)}, u32[]{:S(2)}, u32[]{:S(2)}) async-start(f32[16,48,128]{2,1,0:T(8,128)} %settle.1), calls=%async_computation.4 | async-start | bytes 786432 | tf_op jit(solution)/shard_map/all_to_all | solution.py:624
  162.7 15.2 %collective-permute-start.3 = (f32[16,24,256]{2,1,0:T(8,128)S(1)}, f32[16,24,256]{2,1,0:T(8,128)}, u32[]{:S(2)}, u32[]{:S(2)}) collective-permute-start(f32[16,24,256]{2,1,0:T(8,128)S(1)} %all-to-all-done.8.from_ref), channel_id=1, source_target_pairs={{0,8},{8,0},{16,24},{24,16},{32,40},{40,32},{48,56},{56,48},{64,72... | collective-permute-start | bytes 1179656 | tf_op jit(solution)/shard_map/ppermute | solution.py:628

commit v3 on v2

--- a/solution.py
+++ b/solution.py
@@ -30,7 +30,6 @@
 HIGHEST = lax.Precision.HIGHEST
 HIGH = lax.Precision.HIGH
 
-CHIP_GROUPS = [[16 * q + i for i in range(16)] for q in range(16)]
 ROW_GROUPS = [[2 * q + b for q in range(16)] for b in range(2)]
 CORE_SWAP = [(i, i ^ 1) for i in range(LATS)]
 
@@ -80,6 +79,7 @@
         to_spec=pair_of(spread * weights[None, :, None]),
         from_spec=pair_of(np.transpose(spread, (0, 2, 1))),
         basis=np.ascontiguousarray(basis.T).astype(f),
+        once=np.ascontiguousarray(np.transpose(update.reshape(3, NT, 2, 128), (2, 0, 1, 3))).astype(f),
         twice=np.ascontiguousarray(np.transpose(twice.reshape(3, NT, 2, 128), (2, 0, 1, 3))).astype(f),
         row_weights=row_weights.astype(f),
     )
@@ -197,75 +197,72 @@
     )(offset, atmosphere, clouds, clouds, col, col)
 
 
+def column_of(row):
+    size = row.shape[1]
+    diagonal = lax.broadcasted_iota(jnp.int32, (size, size), 0) == lanes_of((size, size))
+    return jnp.sum(jnp.where(diagonal, row, 0.0), axis=1, keepdims=True)
+
+
 def inner_kernel(with_mean, *refs):
     if with_mean:
-        c_ref, col_ref, diff_ref, wind_ref, mixing_ref, base_ref, mean_ref, inv_ref, ext, sem = refs
+        c_ref, col_ref, diff_ref, wind_ref, mixing_ref, base_ref, ends_ref, mean_ref, inv_ref = refs
     else:
-        c_ref, diff_ref, wind_ref, mixing_ref, base_ref, ext, sem = refs
-    copy = pltpu.make_async_copy(c_ref, ext.at[:, 128 : 128 + CELLS], sem)
-    copy.start()
-    ext[:, 0:128] = jnp.zeros((K, 128), F32)
-    ext[:, 128 + CELLS :] = jnp.zeros((K, 128), F32)
+        c_ref, diff_ref, wind_ref, mixing_ref, base_ref, ends_ref = refs
+    zeros = jnp.zeros((K, 128), F32)
     mix = mixing_block(mixing_ref[...])
-    diffusivity, wind = diff_ref[...], wind_ref[...]
-    copy.wait()
-
-    def step(t, total):
-        start = pl.multiple_of(t * TILE, TILE)
-        window = ext[:, pl.ds(start, TILE + 256)]
-        base_ref[:, pl.ds(start, TILE)] = substep_tile(window, mix, diffusivity, wind)
-        if not with_mean:
-            return total
-        hits = column_hits(col_ref[:, pl.ds(start, TILE)])
-        high, low = split(window[:, 128 : 128 + TILE])
-        rows = jnp.concatenate([high, low, jnp.ones((16, TILE), BF16)], axis=0)
-        return total + lax.dot_general(
-            rows, hits, (((1,), (1,)), ((), ())), preferred_element_type=F32
-        )
-
+    diffusivity, wind = column_of(diff_ref[...]), column_of(wind_ref[...])
+    ends_ref[:, 0:256] = c_ref[:, 0:256]
+    ends_ref[:, 256:512] = c_ref[:, CELLS - 256 :]
+    total = jnp.zeros((2 * K + 16, 128), F32)
+    for start in range(0, CELLS, TILE):
+        window = c_ref[:, max(start - 128, 0) : min(start + TILE + 128, CELLS)]
+        if start == 0:
+            window = jnp.concatenate([zeros, window], axis=1)
+        if start + TILE == CELLS:
+            window = jnp.concatenate([window, zeros], axis=1)
+        base_ref[:, start : start + TILE] = substep_tile(window, mix, diffusivity, wind)
+        if with_mean:
+            hits = column_hits(col_ref[:, start : start + TILE])
+            high, low = split(window[:, 128 : 128 + TILE])
+            rows = jnp.concatenate([high, low, jnp.ones((16, TILE), BF16)], axis=0)
+            total = total + lax.dot_general(
+                rows, hits, (((1,), (1,)), ((), ())), preferred_element_type=F32
+            )
     if with_mean:
-        total = lax.fori_loop(0, CELLS // TILE, step, jnp.zeros((2 * K + 16, 128), F32), unroll=CELLS // TILE)
         counts = total[2 * K : 2 * K + 8]
         inv = jnp.where(counts > 0.0, 1.0 / jnp.maximum(counts, 1.0), 0.0)
         inv_ref[...] = inv
         mean_ref[...] = (total[:K] + total[K : 2 * K]) * inv[0:1]
-    else:
-        lax.fori_loop(0, CELLS // TILE, step, 0, unroll=CELLS // TILE)
 
 
 VMEM_SPEC = pl.BlockSpec(memory_space=pltpu.VMEM)
-ANY_SPEC = pl.BlockSpec(memory_space=pl.ANY)
 
 
 def inner(clouds, col, diffusivity, wind, mixing, with_mean):
     args = [clouds] + ([col] if with_mean else []) + [diffusivity, wind, mixing]
-    shapes = [jax.ShapeDtypeStruct((K, CELLS), F32)]
+    shapes = [jax.ShapeDtypeStruct((K, CELLS), F32), jax.ShapeDtypeStruct((K, 512), F32)]
     if with_mean:
         shapes += [jax.ShapeDtypeStruct((K, 128), F32), jax.ShapeDtypeStruct((8, 128), F32)]
-    out = pl.pallas_call(
+    return pl.pallas_call(
         lambda *refs: inner_kernel(with_mean, *refs),
-        in_specs=[ANY_SPEC] + [VMEM_SPEC] * (len(args) - 1),
+        in_specs=[VMEM_SPEC] * len(args),
         out_specs=[VMEM_SPEC] * len(shapes),
         out_shape=shapes,
-        scratch_shapes=[pltpu.VMEM((K, CELLS + 256), F32), pltpu.SemaphoreType.DMA],
-        cost_estimate=pl.CostEstimate(flops=1 << 30, bytes_accessed=12 << 20, transcendentals=0),
-        compiler_params=pltpu.CompilerParams(vmem_limit_bytes=16 << 20),
+        cost_estimate=pl.CostEstimate(flops=1 << 10, bytes_accessed=1 << 10, transcendentals=0),
+        compiler_params=pltpu.CompilerParams(vmem_limit_bytes=6 << 20),
         name="inner",
     )(*args)
-    return out if with_mean else out[0]
 
 
 def outer_kernel(
-    seg_ref, base_ref, first_ref, last_ref, prof_ref, halo_ref, perm_ref, back_ref, mean_ref, inv_ref,
-    col_ref, diff_ref, wind_ref, mixing_ref, out_ref, end_ref, send_ref, ext1, ext2, force, cols, sem,
+    info, base_ref, ends_ref, prof_ref, halo_ref, perm_ref, back_ref, mean_ref, inv_ref,
+    col_ref, diff_ref, wind_ref, mixing_ref, out_ref, end_ref, send_ref, ext1, ext2, force,
 ):
-    copy = pltpu.make_async_copy(base_ref, ext1.at[:, 256 : 256 + CELLS], sem)
-    copy.start()
-    seg = seg_ref[0]
+    seg = info[0]
     lane = lanes_of((K, 128))
     zeros = jnp.zeros((K, 128), F32)
     mix = mixing_block(mixing_ref[...])
-    diffusivity, wind = diff_ref[...], wind_ref[...]
+    diffusivity, wind = column_of(diff_ref[...]), column_of(wind_ref[...])
 
     from_left = halo_ref[lax.rem(seg + SEGS - 1, SEGS), 16:24, :]
     from_right = halo_ref[lax.rem(seg + 1, SEGS), 16:24, :]
@@ -284,60 +281,54 @@
     )
     profile = jnp.dot(
         perm_ref[...],
-        prof_ref[...].reshape(SEGS * 16, 128),
+        prof_ref[:, 0:16, :].reshape(SEGS * 16, 128),
         precision=HIGHEST,
         preferred_element_type=F32,
     )
     pulled = jnp.where(lane < COLS + 2, RELAXATION * (profile - mean_all), 0.0)
     pulled = jnp.concatenate(split(pulled), axis=1)
 
-    cols[:, 0:256] = jnp.full((1, 256), COLS + 1, jnp.int32)
-    cols[:, 256 + CELLS :] = jnp.full((1, 256), COLS, jnp.int32)
-    cols[:, 256 : 256 + CELLS] = col_ref[...]
     ext1[:, 0:128] = zeros
     ext1[:, EXT - 128 :] = zeros
-    copy.wait()
-    left_window = jnp.concatenate([zeros, left_tile, first_ref[...]], axis=1)
-    ext1[:, 128:384] = substep_tile(left_window, mix, diffusivity, wind)
-    right_window = jnp.concatenate([last_ref[...], right_tile, zeros], axis=1)
-    ext1[:, EXT - 384 : EXT - 128] = substep_tile(right_window, mix, diffusivity, wind)
-
-    def force_step(t, _):
-        start = pl.multiple_of(128 + t * TILE, 128)
-        hits = column_hits(cols[:, pl.ds(start, TILE)])
+    left_col = jnp.full((1, 128), COLS + 1, jnp.int32)
+    right_col = jnp.full((1, 128), COLS, jnp.int32)
+    for at in range(128, EXT - 128, TILE):
+        cell = at - 256
+        if cell < 0:
+            window = jnp.concatenate([zeros, left_tile, ends_ref[:, 0:256]], axis=1)
+            value = substep_tile(window, mix, diffusivity, wind)
+            col = jnp.concatenate([left_col, col_ref[:, 0:128]], axis=1)
+        elif cell + TILE > CELLS:
+            window = jnp.concatenate([ends_ref[:, 256:512], right_tile, zeros], axis=1)
+            value = substep_tile(window, mix, diffusivity, wind)
+            col = jnp.concatenate([col_ref[:, CELLS - 128 :], right_col], axis=1)
+        else:
+            value = base_ref[:, cell : cell + TILE]
+            col = col_ref[:, cell : cell + TILE]
+        hits = column_hits(col)
         forced = jnp.dot(
             pulled, jnp.concatenate([hits, hits], axis=0), preferred_element_type=F32
         )
-        force[:, pl.ds(start, TILE)] = forced
-        ext1[:, pl.ds(start, TILE)] += forced
-        return 0
-
-    lax.fori_loop(0, CELLS // TILE + 1, force_step, 0, unroll=CELLS // TILE + 1)
-
-    def second_step(t, _):
-        start = pl.multiple_of(t * TILE, TILE)
-        here = pl.multiple_of(start + 128, 128)
-        window = ext1[:, pl.ds(start, TILE + 256)]
-        ext2[:, pl.ds(here, TILE)] = (
-            substep_tile(window, mix, diffusivity, wind) + force[:, pl.ds(here, TILE)]
+        force[:, at : at + TILE] = forced
+        ext1[:, at : at + TILE] = value + forced
+
+    for at in range(128, EXT - 128, TILE):
+        window = ext1[:, at - 128 : at + TILE + 128]
+        ext2[:, at : at + TILE] = (
+            substep_tile(window, mix, diffusivity, wind) + force[:, at : at + TILE]
         )
-        return 0
-
-    lax.fori_loop(0, CELLS // TILE + 1, second_step, 0, unroll=CELLS // TILE + 1)
-
-    def third_step(t, total):
-        start = pl.multiple_of(t * TILE, TILE)
-        here = pl.multiple_of(start + 256, 128)
-        window = ext2[:, pl.ds(pl.multiple_of(start + 128, 128), TILE + 256)]
-        value = substep_tile(window, mix, diffusivity, wind) + force[:, pl.ds(here, TILE)]
-        out_ref[:, pl.ds(start, TILE)] = value
-        hits = column_hits(cols[:, pl.ds(here, TILE)])
+
+    total = jnp.zeros((2 * K, 128), F32)
+    for cell in range(0, CELLS, TILE):
+        at = cell + 256
+        window = ext2[:, at - 128 : at + TILE + 128]
+        value = substep_tile(window, mix, diffusivity, wind) + force[:, at : at + TILE]
+        out_ref[:, cell : cell + TILE] = value
+        hits = column_hits(col_ref[:, cell : cell + TILE])
         rows = jnp.concatenate(split(value), axis=0)
-        return total + lax.dot_general(
+        total = total + lax.dot_general(
             rows, hits, (((1,), (1,)), ((), ())), preferred_element_type=F32
         )
-
-    total = lax.fori_loop(0, CELLS // TILE, third_step, jnp.zeros((2 * K, 128), F32), unroll=CELLS // TILE)
     end = (total[:K] + total[K:]) * inv_ref[0:1]
     end_ref[...] = end
     tendency = jnp.where(lane < COLS, end - mean, 0.0)
@@ -345,52 +336,16 @@
     edge = edge_rows(
         out_ref[:, 0:128], out_ref[:, CELLS - 128 :], end[:, 0:1], end[:, COLS - 1 : COLS]
     )
-    for s in range(SEGS):
-        send_ref[s, 0:16, :] = sent[16 * s : 16 * s + 16]
+    for s in range(send_ref.shape[0]):
+        send_ref[s, 0:16, :] = sent[16 * (s % SEGS) : 16 * (s % SEGS) + 16]
         send_ref[s, 16:24, :] = edge
 
 
-def outer(seg, halo_block, base, clouds, profile, halo, perm, back, mean, inv, col, diffusivity, wind, mixing):
-    ends = CELLS // 256 - 1
-    full = lambda shape: pl.BlockSpec(shape, lambda i, seg: (0,) * len(shape))
-    return pl.pallas_call(
-        outer_kernel,
-        grid_spec=pltpu.PrefetchScalarGridSpec(
-            num_scalar_prefetch=1,
-            grid=(1,),
-            in_specs=[
-                ANY_SPEC,
-                pl.BlockSpec((K, 256), lambda i, seg: (0, 0)),
-                pl.BlockSpec((K, 256), lambda i, seg: (0, ends)),
-                full((SEGS, 16, 128)),
-                pl.BlockSpec((SEGS, 24, 128), lambda i, seg: (seg[1] * halo_block, 0, 0)),
-                full((K, SEGS * 16)),
-                full((SEGS * 16, K)),
-                full((K, 128)),
-                full((8, 128)),
-                full((1, CELLS)),
-                full((K, 1)),
-                full((K, 1)),
-                full((K, K)),
-            ],
-            out_specs=[full((K, CELLS)), full((K, 128)), full((SEGS, 24, 128))],
-            scratch_shapes=[
-                pltpu.VMEM((K, EXT), F32),
-                pltpu.VMEM((K, EXT), F32),
-                pltpu.VMEM((K, EXT), F32),
-                pltpu.VMEM((1, EXT), jnp.int32),
-                pltpu.SemaphoreType.DMA,
-            ],
-        ),
-        out_shape=[
-            jax.ShapeDtypeStruct((K, CELLS), F32),
-            jax.ShapeDtypeStruct((K, 128), F32),
-            jax.ShapeDtypeStruct((SEGS, 24, 128), F32),
-        ],
-        cost_estimate=pl.CostEstimate(flops=1 << 31, bytes_accessed=24 << 20, transcendentals=0),
-        compiler_params=pltpu.CompilerParams(vmem_limit_bytes=26 << 20),
-        name="outer",
-    )(seg, base, clouds, clouds, profile, halo, perm, back, mean, inv, col, diffusivity, wind, mixing)
+def outer(info, *args):
+    return call(
+        outer_kernel, "outer", args, [shape(K, CELLS), shape(K, 128), shape(SEGS, 24, 128)],
+        scratch=[pltpu.VMEM((K, EXT), F32)] * 3, prefetch=info, limit=14,
+    )
 
 
 def upper(shape):
@@ -445,12 +400,12 @@
     ]
 
 
-def call(kernel, name, args, shapes, scratch=(), prefetch=None, limit=12, specs=None, flops=1 << 28):
+def call(kernel, name, args, shapes, scratch=(), prefetch=None, limit=8, specs=None):
     specs = specs or [VMEM_SPEC] * len(args)
     common = dict(
         out_shape=shapes,
         name=name,
-        cost_estimate=pl.CostEstimate(flops=flops, bytes_accessed=6 << 20, transcendentals=0),
+        cost_estimate=pl.CostEstimate(flops=1 << 10, bytes_accessed=1 << 10, transcendentals=0),
         compiler_params=pltpu.CompilerParams(vmem_limit_bytes=limit << 20),
     )
     outs = [VMEM_SPEC] * len(shapes)
@@ -488,40 +443,58 @@
             rows_ref[v, j] = jnp.zeros((8, M), F32)
 
 
-def base_kernel(factors, rows_ref, mine_ref, others_ref):
-    def channel(c, _):
-        for half, out in ((0, mine_ref), (16, others_ref)):
-            total = [jnp.zeros((8, M), F32)] * 3
-            for j in range(LAT_DEV):
-                total = weigh(
-                    total, factors[c + half, j : j + 1, :], [rows_ref[v, j] for v in range(3)]
-                )
-            for v in range(3):
-                out[c, 8 * v : 8 * v + 8, :] = total[v]
-        return 0
-
-    lax.fori_loop(0, 16, channel, 0)
-
-
-def parts_kernel(got_ref, table, base_ref, more_ref, factors, parts_ref, pair_ref):
-    pair = received_rows([got_ref[b, :, 0:16, :] for b in range(2)], table)
-    for b in range(2):
+def spread_kernel(info, got_ref, table, rows_ref, send_ref, held):
+    forced = received_rows([got_ref[:, 0:16, :]], table)[0]
+    for h in range(2):
+        held[h] = rows_ref[:, :, :, 128 * h : 128 * h + 128].reshape(384, 128)
         for v in range(3):
-            pair_ref[b, v] = pair[b][v]
-    for c in range(16):
-        total = [
-            base_ref[c, 8 * v : 8 * v + 8, :] + more_ref[c, 8 * v : 8 * v + 8, :] for v in range(3)
-        ]
-        for b in range(2):
-            total = weigh(total, factors[c, b : b + 1, :], pair[b])
-        for v in range(3):
-            parts_ref[c, 8 * v : 8 * v + 8, :] = total[v]
-
-
-def profile_kernel(parts_ref, table, out_ref):
-    total = parts_ref[0]
-    for c in range(1, 16):
-        total = total + parts_ref[c]
+            at = pl.ds(pl.multiple_of((v * 16 + info[2]) * 8, 8), 8)
+            held[h, at, :] += forced[v][:, 128 * h : 128 * h + 128]
+        held[h, LAT_DEV * 8 : LAT_DEV * 8 + 8, :] = jnp.full((8, 128), info[2], jnp.int32).astype(F32)
+    for u in range(8):
+        for h in range(2):
+            send_ref[2 * u + h] = held[h, pl.ds(u, 48, stride=8), :]
+
+
+def settle_kernel(info, mine_ref, others_ref, to_spec, from_spec, once, twice, out_ref):
+    core, half = info[1], info[3]
+
+    def columns(ref):
+        return jnp.concatenate(
+            [ref[:, 16 * v : 16 * v + 16, :].reshape(256, 128) for v in range(3)], axis=1
+        )
+
+    def update(factors, spec):
+        vort, div, geo = spec[:, :128], spec[:, 128:256], spec[:, 256:]
+        f0, f1, f2 = factors[half, 0], factors[half, 1], factors[half, 2]
+        return jnp.concatenate([f0 * vort, f1 * div + f2 * geo, f1 * geo - f2 * div], axis=1)
+
+    spec = dot3_left([to_spec[0, core], to_spec[1, core]], columns(mine_ref)) + dot3_left(
+        [to_spec[0, 1 - core], to_spec[1, 1 - core]], columns(others_ref)
+    )
+    table = [from_spec[0, core], from_spec[1, core]]
+    back = dot3_left(table, update(twice, spec))
+    offsets = mine_ref[:, LAT_DEV, :][:, 0:1].astype(jnp.int32)
+    wanted = 16 * lax.broadcasted_iota(jnp.int32, (16, 256), 0) + offsets
+    picks = jnp.where(lanes_of((16, 256)) == wanted, 1.0, 0.0).astype(BF16)
+    picked = [jnp.dot(picks, t, preferred_element_type=F32).astype(BF16) for t in table]
+    channels = dot3_left(picked, update(once, spec))
+    for v in range(3):
+        out_ref[:, 16 * v : 16 * v + 16, :] = back[:, 128 * v : 128 * v + 128].reshape(16, 16, 128)
+        for q in range(16):
+            out_ref[q, 16 * v + LAT_DEV : 16 * v + LAT_DEV + 1, :] = channels[
+                q : q + 1, 128 * v : 128 * v + 128
+            ]
+
+
+def profile_kernel(got_ref, table, out_ref, total):
+    for v in range(3):
+        for u in range(8):
+            for h in range(2):
+                at = 16 * v + LAT_DEV
+                total[8 * v + u : 8 * v + u + 1, 128 * h : 128 * h + 128] = got_ref[
+                    2 * u + h, at : at + 1, :
+                ]
     a, b, c = total[0:8], total[8:16], total[16:24]
     first = upper((8, M))
     cos = jnp.concatenate([jnp.where(first, a, swap4(b)), c], axis=0)
@@ -529,36 +502,6 @@
     lines = dot3(jnp.concatenate([cos, sin], axis=1), table)
     for s in range(SEGS):
         out_ref[s] = lines[:, 128 * s : 128 * s + 128]
-
-
-def spread_kernel(info, rows_ref, pair_ref, send_ref, held):
-    for h in range(2):
-        held[h] = rows_ref[:, :, :, 128 * h : 128 * h + 128].reshape(384, 128)
-        for v in range(3):
-            at = pl.ds(pl.multiple_of((v * 16 + info[2]) * 8, 8), 8)
-            held[h, at, :] += pair_ref[info[1], v, :, 128 * h : 128 * h + 128]
-    for u in range(8):
-        for h in range(2):
-            send_ref[2 * u + h] = held[h, pl.ds(u, 48, stride=8), :]
-
-
-def settle_kernel(info, mine_ref, others_ref, to_spec, from_spec, twice, out_ref):
-    core, half = info[1], info[3]
-
-    def columns(ref):
-        return jnp.concatenate(
-            [ref[:, 16 * v : 16 * v + 16, :].reshape(256, 128) for v in range(3)], axis=1
-        )
-
-    spec = dot3_left([to_spec[0, core], to_spec[1, core]], columns(mine_ref)) + dot3_left(
-        [to_spec[0, 1 - core], to_spec[1, 1 - core]], columns(others_ref)
-    )
-    vort, div, geo = spec[:, :128], spec[:, 128:256], spec[:, 256:]
-    f0, f1, f2 = twice[half, 0], twice[half, 1], twice[half, 2]
-    spec = jnp.concatenate([f0 * vort, f1 * div + f2 * geo, f1 * geo - f2 * div], axis=1)
-    back = dot3_left([from_spec[0, core], from_spec[1, core]], spec)
-    for v in range(3):
-        out_ref[:, 16 * v : 16 * v + 16, :] = back[:, 128 * v : 128 * v + 128].reshape(16, 16, 128)
 
 
 def last_kernel(got_ref, table, out_ref):
@@ -639,84 +582,66 @@
     info = jnp.stack((seg, core, offset[0], chip % 2))
     clouds = cloud_state[0]
     col = cell_column
-    wind = channel_wind.reshape(K, 1)
-    diff = diffusivity.reshape(K, 1)
-
-    first_send = prepare(offset, atmosphere, clouds, col)
-    first_got = lax.all_to_all(first_send, "seg", 0, 0, tiled=True)
-    channel_lat, grid, first_send = lax.optimization_barrier((channel_lat, atmosphere, first_send))
-
-    own_position = jnp.broadcast_to(channel_lat.astype(F32)[None, :], (1, 128))
-    partner_position = core_swap(own_position)
-    positions = rows_exchange(
-        jnp.broadcast_to(
-            jnp.concatenate((own_position, partner_position), axis=0)[None], (16, 2, 128)
-        )
-    )[:, :, 0]
-    pair_positions = jnp.stack((own_position[0, 0], partner_position[0, 0]))
-    pair_positions = jnp.where(core == 0, pair_positions, pair_positions[::-1])
-    wanted = jnp.concatenate((positions[:, 0], positions[:, 1], pair_positions))
-    picks = (wanted.astype(jnp.int32)[:, None] == jnp.arange(NLAT, dtype=jnp.int32)[None, :])
-    basis = jnp.dot(picks.astype(F32), tab["basis"], precision=HIGHEST)
-    here = lax.dynamic_slice_in_dim(tab["basis"], lat * LAT_DEV, LAT_DEV, axis=0)
-    here = jnp.pad(here, ((0, 4), (0, 0)))
-    pair = jnp.pad(basis[32:], ((0, 6), (0, 0)))
-    products = (basis[:32, None] * here[None]).reshape(32 * 16, NT)
-    factors = jnp.dot(products, tab["row_weights"], precision=HIGH).reshape(32, 16, 3 * M)
-    products = (basis[:16, None] * pair[None]).reshape(16 * 8, NT)
-    pair_factors = jnp.dot(products, tab["row_weights"], precision=HIGH).reshape(16, 8, 3 * M)
-
-    base, mean, inv = inner(clouds, col, diff, wind, mixing, True)
-
+    wind = channel_wind
+    diff = diffusivity.reshape(1, K)
+    spread_table = tab["forward_seg"]
+    gather_rows = jnp.asarray(grouped)
+    scatter_rows = jnp.asarray(grouped.T.copy())
+
+    send = prepare(offset, atmosphere, clouds, col)
+    got = lax.all_to_all(send, "seg", 0, 0, tiled=True)
+    grid, state, send = lax.optimization_barrier((atmosphere, clouds, send))
+    base, ends, mean, inv = inner(state, col, diff, wind, mixing, True)
     rows = call(
         rows_kernel, "rows", (grid, tab["forward"]), [shape(3, 16, 8, M)],
         scratch=[pltpu.VMEM((144, NLON), F32)],
     )[0]
-    base_mine, base_others = call(
-        base_kernel, "base", (factors, rows), [shape(16, 24, M), shape(16, 24, M)]
-    )
-    base_more = core_swap(base_others)
-
     clouds, mean_1, send = outer(
-        info, 0, base, clouds, first_got, first_got, jnp.asarray(natural), jnp.asarray(grouped.T.copy()),
+        info, base, ends, got, got, jnp.asarray(natural), scatter_rows,
         mean, inv, col, diff, wind, mixing,
     )
-    got = lax.all_to_all(
-        jnp.concatenate((send, send), axis=0), ("lat", "seg"), 0, 0,
-        axis_index_groups=CHIP_GROUPS, tiled=True,
-    )
-    base = inner(clouds, col, diff, wind, mixing, False)
-    parts, pair_rows = call(
-        parts_kernel, "parts",
-        (got.reshape(2, SEGS, 24, 128), tab["forward_seg"], base_mine, base_more, pair_factors),
-        [shape(16, 24, M), shape(2, 3, 8, M)],
-    )
-    parts = rows_exchange(parts)
-    profile = call(
-        profile_kernel, "profile", (parts, tab["inverse_seg"]), [shape(SEGS, 16, 128)]
-    )[0]
-    profile = lax.all_to_all(profile, "seg", 0, 0, tiled=True)
+    halo = lax.all_to_all(send, "seg", 0, 0, tiled=True)
+    base, ends = inner(clouds, col, diff, wind, mixing, False)
+    base, ends, halo = lax.optimization_barrier((base, ends, halo))
 
     spread = call(
-        spread_kernel, "spread", (rows, pair_rows), [shape(16, 48, 128)],
+        spread_kernel, "spread", (halo, spread_table, rows), [shape(16, 48, 128)],
         scratch=[pltpu.VMEM((2, 384, 128), F32)], prefetch=info,
     )[0]
     spec_mine = rows_exchange(spread)
     spec_others = core_swap(spec_mine)
     settled = call(
         settle_kernel, "settle",
-        (spec_mine, spec_others, tab["to_spec"], tab["from_spec"], tab["twice"]),
+        (spec_mine, spec_others, tab["to_spec"], tab["from_spec"], tab["once"], tab["twice"]),
         [shape(16, 48, 128)], prefetch=info,
     )[0]
     settled = rows_exchange(settled)
+    profile = call(
+        profile_kernel, "profile", (settled, tab["inverse_seg"]), [shape(SEGS, 16, 128)],
+        scratch=[pltpu.VMEM((24, M), F32)],
+    )[0]
+    profile = lax.all_to_all(profile, "seg", 0, 0, tiled=True)
+
+    numbers = jnp.arange(16, dtype=jnp.int32)
+    near = (2 * numbers + core) * LAT_DEV + spec_mine[:, LAT_DEV, 0].astype(jnp.int32)
+    far = (2 * numbers + 1 - core) * LAT_DEV + spec_others[:, LAT_DEV, 0].astype(jnp.int32)
+    wanted = jnp.concatenate((near, far))
+    picks = (wanted[:, None] == jnp.arange(NLAT, dtype=jnp.int32)[None, :]).astype(F32)
+    basis = jnp.dot(picks, tab["basis"], precision=HIGHEST)
+    here = lax.dynamic_slice_in_dim(tab["basis"], lat * LAT_DEV, LAT_DEV, axis=0)
+    here = jnp.pad(here, ((0, 4), (0, 0)))
+    products = (basis[:, None] * here[None]).reshape(32 * 16, NT)
+    factors = jnp.dot(products, tab["row_weights"], precision=HIGH).reshape(32, 16, 3 * M)
+
+    factors, profile = lax.optimization_barrier((factors, profile))
 
     clouds, _, send = outer(
-        info, 1, base, clouds, profile, got, jnp.asarray(grouped), jnp.asarray(grouped.T.copy()),
+        info, base, ends, profile, halo, gather_rows, scatter_rows,
         mean_1, inv, col, diff, wind, mixing,
     )
     got = lax.all_to_all(send, "seg", 0, 0, tiled=True)
     from_mine = rows_exchange(
-        call(last_kernel, "last", (got, tab["forward_seg"]), [shape(16, 24, M)])[0]
+        call(last_kernel, "last", (got, spread_table), [shape(16, 24, M)])[0]
     )
     from_others = core_swap(from_mine)
     part = call(

time: 183 us -> 146 us (0.80)
  blocking collectives: 17.9 us -> 49.6 us
  waiting for transfers between devices: 53 us -> 22.6 us
  starting transfers between devices: 43.8 us -> 18.9 us
  local copies, waits for them, and re-layouts: 23.1 us -> 17.1 us
  Pallas kernels: 37 us -> 31.5 us
  matrix products: 3.73 us -> 1.09 us
    all_to_all x4 -> x1, waiting for transfers between devices: 38.7 us -> 13.4 us  [rows_exchange(): lax.all_to_all(x, 'lat', 0, 0, axis_index_groups=ROW_GROUPS, tiled=True)]
    all_to_all x1 -> x2, blocking collectives: 17.9 us -> 40.8 us  [rows_exchange(): lax.all_to_all(x, 'lat', 0, 0, axis_index_groups=ROW_GROUPS, tiled=True)]
    all_to_all x4 -> x1, starting transfers between devices: 26.2 us -> 5.05 us  [rows_exchange(): lax.all_to_all(x, 'lat', 0, 0, axis_index_groups=ROW_GROUPS, tiled=True)]
    pallas_call x2 -> x4, Pallas kernels: 3.59 us -> 18.9 us  [call(): pl.pallas_call(kernel, grid_spec=pltpu.PrefetchScalarGridSpec(num_scalar_...]
    pallas_call x4 -> x2, Pallas kernels: 20.1 us -> 5.1 us  [inner(): pl.pallas_call(lambda *refs: inner_kernel(with_mean, *refs), in_specs=[VM...]
    all_to_all x0 -> x1, blocking collectives: none -> 8.85 us  [shards(): got = lax.all_to_all(send, 'seg', 0, 0, tiled=True)]
    all_to_all x2 -> x1, waiting for transfers between devices: 7.07 us -> 0.01 us  [shards(): halo = lax.all_to_all(send, 'seg', 0, 0, tiled=True)]
    pallas_call x7 -> x5, Pallas kernels: 11.4 us -> 5.57 us  [call(): pl.pallas_call(kernel, in_specs=specs, out_specs=outs, scratch_shapes=lis...]
  transfers between devices with their start and end apart: 12 -> 6, of which waited for: 9 -> 5; matrix products, arithmetic and copies ran while one was open for 4% -> 2% of each run, Pallas kernels for 13% -> 5%
where the time goes in v3:
time: 146 us; the launch traced here: 143 us
  blocking collectives  49.6 us (34%)
  Pallas kernels  31.5 us (22%)
  waiting for transfers between devices  22.6 us (15%)
  starting transfers between devices  18.9 us (13%)
  local copies, waits for them, and re-layouts  17.1 us (12%)
  between operations  1.52 us (1%)
    all_to_all x2, blocking collectives, rows_exchange(): lax.all_to_all(x, 'lat', 0, 0, axis_index_groups=ROW_GROUPS, tiled=True)  40.8 us
    pallas_call x4, Pallas kernels, call(): pl.pallas_call(kernel, grid_spec=pltpu.PrefetchScalarGridSpec(num_scalar_...  18.9 us
    unnamed x56, local copies, waits for them, and re-layouts  16.4 us
    all_to_all x1, waiting for transfers between devices, rows_exchange(): lax.all_to_all(x, 'lat', 0, 0, axis_index_groups=ROW_GROUPS, tiled=True)  13.4 us
    all_to_all x1, blocking collectives, shards(): got = lax.all_to_all(send, 'seg', 0, 0, tiled=True)  8.85 us
    pallas_call x5, Pallas kernels, call(): pl.pallas_call(kernel, in_specs=specs, out_specs=outs, scratch_shapes=lis...  5.57 us
    all_to_all x1, waiting for transfers between devices, shards(): profile = lax.all_to_all(profile, 'seg', 0, 0, tiled=True)  5.53 us
    all_to_all x1, starting transfers between devices, shards(): got = lax.all_to_all(send, 'seg', 0, 0, tiled=True)  5.44 us
  transfers between devices with their start and end apart: 6, of which 5 were waited for; matrix products, arithmetic and copies ran while one was open for 2% of the time, Pallas kernels for 5%

profile of v3, /device:TPU:32, one launch (start us, length us, event | category | flops | bytes accessed | tf_op | source)
XLA Modules:
  0.0 143.2 jit_solution(9274795380822147304)
XLA Ops:
  1.3 1.9 %prepare.1 = f32[8,24,128]{2,1,0:T(8,128)} custom-call(s32[1]{0:T(128)S(6)} %sub.15.off_ref, f32[12,12,768]{2,1,0:T(8,128)} %grid_ref, f32[96,6144]{1,0:T(8,128)} %bitcast.10, f32[96,6144]{1,0:T(8,128)} %bitcast.11, s32[1,6144]{1,0:T(1,128)} %col_ref.3, s32[1,6144]{1,0:T(1,128)} %col_ref.3), custom_call_target="tpu_custom_call" | custom-call | tf_op jit(solution)/shard_map/prepare/pallas_call | solution.py:181
  3.2 5.4 %all-to-all-start = ((f32[8,24,128]{2,1,0:T(8,128)}), f32[8,24,128]{2,1,0:T(8,128)S(1)}, u32[]{:S(2)}, u32[]{:S(2)}) async-start(f32[8,24,128]{2,1,0:T(8,128)} %prepare.1), calls=%async_computation | async-start | bytes 196608 | tf_op jit(solution)/shard_map/all_to_all | solution.py:592
  8.7 0.0 copy-start.9
  8.7 2.5 %inner.2 = (f32[96,6144]{1,0:T(8,128)S(1)}, f32[96,512]{1,0:T(8,128)S(1)}, f32[96,128]{1,0:T(8,128)S(1)}, f32[8,128]{1,0:T(8,128)S(1)}) custom-call(f32[96,6144]{1,0:T(8,128)S(1)} %bitcast.12, s32[1,6144]{1,0:T(1,128)S(1)} %copy-done.16, f32[1,96]{1,0:T(1,128)S(1)} %bitcast.13, f32[1,96]{1,0:T(1,128)S(1)} %copy-done.25, f32[96,96]{1,0:T(8,128)S(1)} %copy-done.15), custom_call_target="tpu_custom_call" | custom-call | flops 1024 | bytes 1024 | tf_op jit(solution)/shard_map/inner/pallas_call | solution.py:246
  11.2 0.0 copy-start.5
  11.3 1.4 copy-done.5
  12.6 0.1 pad_add_fusion.info
  12.7 2.4 %all-to-all-done.prof_ref.halo_ref = f32[8,24,128]{2,1,0:T(8,128)S(1)} async-done(((f32[8,24,128]{2,1,0:T(8,128)}), f32[8,24,128]{2,1,0:T(8,128)S(1)}, u32[]{:S(2)}, u32[]{:S(2)}) %all-to-all-start) | async-done | bytes 98336 | tf_op jit(solution)/shard_map/all_to_all | solution.py:592
  15.1 1.7 %copy-done.6 = f32[96,6144]{1,0:T(8,128)S(1)} copy-done((f32[96,6144]{1,0:T(8,128)S(1)}, f32[96,6144]{1,0:T(8,128)}, u32[]{:S(2)}) %copy-start.6) | copy-done | bytes 2359320
  16.8 7.5 %outer.2 = (f32[96,6144]{1,0:T(8,128)S(1)}, f32[96,128]{1,0:T(8,128)S(1)}, f32[8,24,128]{2,1,0:T(8,128)}) custom-call(s32[4]{0:T(128)S(1)} %pad_add_fusion.info, f32[96,6144]{1,0:T(8,128)S(1)} %copy-done.6, f32[96,512]{1,0:T(8,128)S(1)} %get-tuple-element.22.ends_ref, f32[8,24,128]{2,1,0:T(8,128)S(1)} %all-to-all-done.prof_ref.halo_ref, ...), custom_call_target="tpu_custom_call" | custom-call | flops 1024 | bytes 1024 | tf_op jit(solution)/shard_map/outer/pallas_call | solution.py:416
  24.3 1.4 copy-done.7
  25.7 3.5 %all-to-all-start.1 = ((f32[8,24,128]{2,1,0:T(8,128)}), f32[8,24,128]{2,1,0:T(8,128)S(1)}, u32[]{:S(2)}, u32[]{:S(2)}) async-start(f32[8,24,128]{2,1,0:T(8,128)} %get-tuple-element.28), calls=%async_computation.1 | async-start | bytes 196608 | tf_op jit(solution)/shard_map/all_to_all | solution.py:603
  29.2 0.0 copy-start.12
  29.3 1.4 copy-done.12
  30.7 0.6 rows.1.rows_ref
  31.3 1.7 %copy-done.8 = f32[96,6144]{1,0:T(8,128)S(1)} copy-done((f32[96,6144]{1,0:T(8,128)S(1)}, f32[96,6144]{1,0:T(8,128)}, u32[]{:S(2)}) %copy-start.8) | copy-done | bytes 2359320
  33.0 2.6 %inner.3 = (f32[96,6144]{1,0:T(8,128)S(1)}, f32[96,512]{1,0:T(8,128)S(1)}) custom-call(f32[96,6144]{1,0:T(8,128)S(1)} %copy-done.8, f32[1,96]{1,0:T(1,128)S(1)} %bitcast.15, f32[1,96]{1,0:T(1,128)S(1)} %copy-done.25, f32[96,96]{1,0:T(8,128)S(1)} %copy-done.15), custom_call_target="tpu_custom_call" | custom-call | flops 1024 | bytes 1024 | tf_op jit(solution)/shard_map/inner/pallas_call | solution.py:246
  35.6 0.0 copy-start.3
  35.6 1.4 copy-done.3
  37.0 0.7 copy-done.20
  37.7 1.0 spread.1
  38.7 23.7 %all_to_all.35.mine_ref = f32[16,48,128]{2,1,0:T(8,128)S(1)} all-to-all(f32[16,48,128]{2,1,0:T(8,128)S(1)} %spread.1), channel_id=1, replica_groups={{0,16,32,48,64,80,96,112,128,144,160,176,192,208,224,240},{8,24,40,56,7..., dimensions={0} | all-to-all | bytes 786432 | tf_op jit(solution)/shard_map/all_to_all | solution.py:567
  62.4 0.7 constant_dynamic-slice_fusion
  63.1 0.4 fusion.7
  63.5 0.6 collective-permute-done.others_ref
  64.1 1.1 copy-done.13
  65.3 1.1 copy-done.14
  66.4 1.0 copy-done.18
  67.4 2.3 %settle.1 = f32[16,48,128]{2,1,0:T(8,128)} custom-call(s32[4]{0:T(128)S(1)} %pad_add_fusion.info, f32[16,48,128]{2,1,0:T(8,128)S(1)} %all_to_all.35.mine_ref, f32[16,48,128]{2,1,0:T(8,128)S(1)} %collective-permute-done.others_ref, bf16[2,2,256,256]{3,2,1,0:T(8,128)(2,1)S(1)} %copy-done.18, bf16[2,2,256,256]{3,2,1,0:T(8,128)(2,1)S(1)} %copy-done.17, ...), custom_call_target="tpu_custom_call" | custom-call | flops 1024 | bytes 1024 | tf_op jit(solution)/shard_map/settle/pallas_call | solution.py:416
  69.7 5.0 %all-to-all-start.3 = ((f32[16,48,128]{2,1,0:T(8,128)}), f32[16,48,128]{2,1,0:T(8,128)S(1)}, u32[]{:S(2)}, u32[]{:S(2)}) async-start(f32[16,48,128]{2,1,0:T(8,128)} %settle.1), calls=%async_computation.3 | async-start | bytes 786432 | tf_op jit(solution)/shard_map/all_to_all | solution.py:567
  74.8 0.4 fusion.6
  75.2 0.1 pad_add_fusion.1
  75.3 0.3 fusion.4
  75.6 13.4 %all-to-all-done.3.got_ref = f32[16,48,128]{2,1,0:T(8,128)S(1)} async-done(((f32[16,48,128]{2,1,0:T(8,128)}), f32[16,48,128]{2,1,0:T(8,128)S(1)}, u32[]{:S(2)}, u32[]{:S(2)}) %all-to-all-start.3) | async-done | bytes 393248 | tf_op jit(solution)/shard_map/all_to_all | solution.py:567
  89.0 1.6 %copy-done.10 = bf16[2,512,1024]{2,1,0:T(8,128)(2,1)S(1)} copy-done((bf16[2,512,1024]{2,1,0:T(8,128)(2,1)S(1)}, bf16[2,512,1024]{2,1,0:T(8,128)(2,1)}, u32[]{:S(2)}) %copy-start.10) | copy-done | bytes 2097176
  90.6 1.1 profile.1
  91.6 4.8 %all-to-all-start.4 = ((f32[8,16,128]{2,1,0:T(8,128)}), f32[8,16,128]{2,1,0:T(8,128)S(1)}, u32[]{:S(2)}, u32[]{:S(2)}) async-start(f32[8,16,128]{2,1,0:T(8,128)} %profile.1), calls=%async_computation.4 | async-start | bytes 131072 | tf_op jit(solution)/shard_map/all_to_all | solution.py:623
  96.5 0.8 fusion.factors
  97.3 5.5 %all-to-all-done.4.prof_ref = f32[8,16,128]{2,1,0:T(8,128)S(1)} async-done(((f32[8,16,128]{2,1,0:T(8,128)}), f32[8,16,128]{2,1,0:T(8,128)S(1)}, u32[]{:S(2)}, u32[]{:S(2)}) %all-to-all-start.4) | async-done | bytes 65568 | tf_op jit(solution)/shard_map/all_to_all | solution.py:623
  102.8 1.8 %copy-done.4 = f32[96,6144]{1,0:T(8,128)S(1)} copy-done((f32[96,6144]{1,0:T(8,128)S(1)}, f32[96,6144]{1,0:T(8,128)}, u32[]{:S(2)}) %copy-start.4) | copy-done | bytes 2359320
  104.6 8.1 %outer.3 = (f32[96,6144]{1,0:T(8,128)}, f32[96,128]{1,0:T(8,128)}, f32[8,24,128]{2,1,0:T(8,128)S(1)}) custom-call(s32[4]{0:T(128)S(1)} %pad_add_fusion.info, f32[96,6144]{1,0:T(8,128)S(1)} %copy-done.4, f32[96,512]{1,0:T(8,128)S(1)} %copy-done.21, f32[8,16,128]{2,1,0:T(8,128)S(1)} %all-to-all-done.4.prof_ref, ...), custom_call_target="tpu_custom_call" | custom-call | flops 1024 | bytes 1024 | tf_op jit(solution)/shard_map/outer/pallas_call | solution.py:416
  112.7 8.8 %all_to_all.36.got_ref = f32[8,24,128]{2,1,0:T(8,128)S(1)} all-to-all(f32[8,24,128]{2,1,0:T(8,128)S(1)} %get-tuple-element.36), channel_id=1, replica_groups=mesh['lat'=32,'seg'=8] {'seg'}, dimensions={0} | all-to-all | bytes 196608 | tf_op jit(solution)/shard_map/all_to_all | solution.py:642
  121.6 0.4 last.1
  122.0 0.0 copy-start.11
  122.0 17.1 %all_to_all.37.from_ref = f32[16,24,256]{2,1,0:T(8,128)S(1)} all-to-all(f32[16,24,256]{2,1,0:T(8,128)S(1)} %last.1), channel_id=1, replica_groups={{0,16,32,48,64,80,96,112,128,144,160,176,192,208,224,240},{8,24,40,56,7..., dimensions={0} | all-to-all | bytes 786432 | tf_op jit(solution)/shard_map/all_to_all | solution.py:567
  139.1 1.1 gather.1.part_ref
  140.2 0.6 collective-permute-done.1.from_ref
  140.9 2.4 %finish.1 = f32[12,12,768]{2,1,0:T(8,128)} custom-call(f32[3,16,8,256]{3,2,1,0:T(8,128)S(1)} %gather.1.part_ref, f32[32,16,768]{2,1,0:T(8,128)S(1)} %fusion.factors, f32[16,24,256]{2,1,0:T(8,128)S(1)} %collective-permute-done.1.from_ref, bf16[2,512,768]{2,1,0:T(8,128)(2,1)S(1)} %copy-done.11), custom_call_target="tpu_custom_call" | custom-call | flops 1024 | bytes 1024 | tf_op jit(solution)/shard_map/finish/pallas_call | solution.py:413
  (45 shorter events, 0.1 us)
Async XLA Ops:
  1.3 7.4 %copy-start = (f32[1,96,6144]{2,1,0:T(8,128)S(1)}, f32[1,96,6144]{2,1,0:T(8,128)}, u32[]{:S(2)}) copy-start(f32[1,96,6144]{2,1,0:T(8,128)} %param.21) | copy-start | bytes 7077892
  1.3 7.4 %copy-start.15 = (f32[96,96]{1,0:T(8,128)S(1)}, f32[96,96]{1,0:T(8,128)}, u32[]{:S(2)}) copy-start(f32[96,96]{1,0:T(8,128)} %mixing_ref.3) | copy-start | bytes 110596
  1.3 7.4 %copy-start.16 = (s32[1,6144]{1,0:T(1,128)S(1)}, s32[1,6144]{1,0:T(1,128)}, u32[]{:S(2)}) copy-start(s32[1,6144]{1,0:T(1,128)} %col_ref.3) | copy-start | bytes 73732
  1.3 7.4 %copy-start.24 = (f32[96]{0:T(128)S(1)}, f32[96]{0:T(128)}, u32[]{:S(2)}) copy-start(f32[96]{0:T(128)} %param.25) | copy-start | bytes 1156
  1.3 7.4 %copy-start.25 = (f32[1,96]{1,0:T(1,128)S(1)}, f32[1,96]{1,0:T(1,128)}, u32[]{:S(2)}) copy-start(f32[1,96]{1,0:T(1,128)} %wind_ref.3) | copy-start | bytes 1156
  3.2 11.9 %copy-start.19 = (f32[128,96]{1,0:T(8,128)S(1)}, f32[128,96]{1,0:T(8,128)}, u32[]{:S(2)}) copy-start(f32[128,96]{1,0:T(8,128)} %constant.84.clone.back_ref) | copy-start | bytes 147460
  3.2 11.9 %copy-start.23 = (f32[96,128]{1,0:T(8,128)S(1)}, f32[96,128]{1,0:T(8,128)}, u32[]{:S(2)}) copy-start(f32[96,128]{1,0:T(8,128)} %constant.85.clone.perm_ref) | copy-start | bytes 147460
  3.2 11.9 %all-to-all-start = ((f32[8,24,128]{2,1,0:T(8,128)}), f32[8,24,128]{2,1,0:T(8,128)S(1)}, u32[]{:S(2)}, u32[]{:S(2)}) async-start(f32[8,24,128]{2,1,0:T(8,128)} %prepare.1), calls=%async_computation | async-start | bytes 196608 | tf_op jit(solution)/shard_map/all_to_all | solution.py:592
  8.7 20.5 %copy-start.9 = (f32[12,12,768]{2,1,0:T(8,128)S(1)}, f32[12,12,768]{2,1,0:T(8,128)}, u32[]{:S(2)}) copy-start(f32[12,12,768]{2,1,0:T(8,128)} %grid_ref) | copy-start | bytes 1327108
  11.2 1.4 copy-start.5
  15.1 1.7 %copy-start.6 = (f32[96,6144]{1,0:T(8,128)S(1)}, f32[96,6144]{1,0:T(8,128)}, u32[]{:S(2)}) copy-start(f32[96,6144]{1,0:T(8,128)} %copy-done.5) | copy-start | bytes 7077892
  24.3 1.4 copy-start.7
  25.7 12.0 %all-to-all-start.1 = ((f32[8,24,128]{2,1,0:T(8,128)}), f32[8,24,128]{2,1,0:T(8,128)S(1)}, u32[]{:S(2)}, u32[]{:S(2)}) async-start(f32[8,24,128]{2,1,0:T(8,128)} %get-tuple-element.28), calls=%async_computation.1 | async-start | bytes 196608 | tf_op jit(solution)/shard_map/all_to_all | solution.py:603
  29.2 1.4 copy-start.12
  30.7 7.0 %copy-start.1 = (bf16[2,1024,512]{2,1,0:T(8,128)(2,1)S(1)}, bf16[2,1024,512]{2,1,0:T(8,128)(2,1)}, u32[]{:S(2)}) copy-start(bf16[2,1024,512]{2,1,0:T(8,128)(2,1)} %constant.75.clone.table) | copy-start | bytes 6291460
  31.3 1.7 %copy-start.8 = (f32[96,6144]{1,0:T(8,128)S(1)}, f32[96,6144]{1,0:T(8,128)}, u32[]{:S(2)}) copy-start(f32[96,6144]{1,0:T(8,128)} %copy-done.7) | copy-start | bytes 7077892
  35.6 1.4 copy-start.3
  37.0 0.7 copy-start.20
  37.7 26.5 %copy-start.17 = (bf16[2,2,256,256]{3,2,1,0:T(8,128)(2,1)S(1)}, bf16[2,2,256,256]{3,2,1,0:T(8,128)(2,1)}, u32[]{:S(2)}) copy-start(bf16[2,2,256,256]{3,2,1,0:T(8,128)(2,1)} %constant.78.clone.from_spec) | copy-start | bytes 1572868
  62.4 1.7 %collective-permute-start = (f32[16,48,128]{2,1,0:T(8,128)S(1)}, f32[16,48,128]{2,1,0:T(8,128)S(1)}, u32[]{:S(2)}, u32[]{:S(2)}) collective-permute-start(f32[16,48,128]{2,1,0:T(8,128)S(1)} %all_to_all.35.mine_ref), channel_id=1, source_target_pairs={{0,8},{8,0},{16,24},{24,16},{32,40},{40,32},{48,56},{56,48},{64,72... | collective-permute-start | bytes 1179656 | tf_op jit(solution)/shard_map/ppermute | solution.py:571
  64.1 1.1 copy-start.13
  65.3 1.1 copy-start.14
  66.4 1.0 copy-start.18
  67.4 7.8 %copy-start.27 = (f32[384,256]{1,0:T(8,128)S(1)}, f32[384,256]{1,0:T(8,128)}, u32[]{:S(2)}) copy-start(f32[384,256]{1,0:T(8,128)} %constant.79.clone) | copy-start | bytes 1179652
  69.7 26.7 %copy-start.26 = (f32[256,768,1]{1,0,2:T(8,128)S(1)}, f32[256,768,1]{1,0,2:T(8,128)}, u32[]{:S(2)}) copy-start(f32[256,768,1]{1,0,2:T(8,128)} %constant.93) | copy-start | bytes 2359300
  69.7 19.2 %all-to-all-start.3 = ((f32[16,48,128]{2,1,0:T(8,128)}), f32[16,48,128]{2,1,0:T(8,128)S(1)}, u32[]{:S(2)}, u32[]{:S(2)}) async-start(f32[16,48,128]{2,1,0:T(8,128)} %settle.1), calls=%async_computation.3 | async-start | bytes 786432 | tf_op jit(solution)/shard_map/all_to_all | solution.py:567
  89.0 1.6 %copy-start.10 = (bf16[2,512,1024]{2,1,0:T(8,128)(2,1)S(1)}, bf16[2,512,1024]{2,1,0:T(8,128)(2,1)}, u32[]{:S(2)}) copy-start(bf16[2,512,1024]{2,1,0:T(8,128)(2,1)} %constant.76.clone.table) | copy-start | bytes 6291460
  90.6 12.2 %copy-start.21 = (f32[96,512]{1,0:T(8,128)S(1)}, f32[96,512]{1,0:T(8,128)}, u32[]{:S(2)}) copy-start(f32[96,512]{1,0:T(8,128)} %copy-done.20) | copy-start | bytes 589828
  90.6 12.2 %copy-start.22 = (f32[96,128]{1,0:T(8,128)S(1)}, f32[96,128]{1,0:T(8,128)}, u32[]{:S(2)}) copy-start(f32[96,128]{1,0:T(8,128)} %constant.83.clone.perm_ref) | copy-start | bytes 147460
  91.6 11.2 %all-to-all-start.4 = ((f32[8,16,128]{2,1,0:T(8,128)}), f32[8,16,128]{2,1,0:T(8,128)S(1)}, u32[]{:S(2)}, u32[]{:S(2)}) async-start(f32[8,16,128]{2,1,0:T(8,128)} %profile.1), calls=%async_computation.4 | async-start | bytes 131072 | tf_op jit(solution)/shard_map/all_to_all | solution.py:623
  102.8 18.8 %copy-start.2 = (bf16[2,1024,512]{2,1,0:T(8,128)(2,1)S(1)}, bf16[2,1024,512]{2,1,0:T(8,128)(2,1)}, u32[]{:S(2)}) copy-start(bf16[2,1024,512]{2,1,0:T(8,128)(2,1)} %constant.75.clone.table) | copy-start | bytes 6291460
  102.8 1.8 %copy-start.4 = (f32[96,6144]{1,0:T(8,128)S(1)}, f32[96,6144]{1,0:T(8,128)}, u32[]{:S(2)}) copy-start(f32[96,6144]{1,0:T(8,128)} %copy-done.3) | copy-start | bytes 7077892
  122.0 18.8 %copy-start.11 = (bf16[2,512,768]{2,1,0:T(8,128)(2,1)S(1)}, bf16[2,512,768]{2,1,0:T(8,128)(2,1)}, u32[]{:S(2)}) copy-start(bf16[2,512,768]{2,1,0:T(8,128)(2,1)} %constant.74.clone.table) | copy-start | bytes 4718596
  139.1 1.7 %collective-permute-start.1 = (f32[16,24,256]{2,1,0:T(8,128)S(1)}, f32[16,24,256]{2,1,0:T(8,128)S(1)}, u32[]{:S(2)}, u32[]{:S(2)}) collective-permute-start(f32[16,24,256]{2,1,0:T(8,128)S(1)} %all_to_all.37.from_ref), channel_id=1, source_target_pairs={{0,8},{8,0},{16,24},{24,16},{32,40},{40,32},{48,56},{56,48},{64,72... | collective-permute-start | bytes 1179656 | tf_op jit(solution)/shard_map/ppermute | solution.py:571

commit v4 on v3

--- a/solution.py
+++ b/solution.py
@@ -21,6 +21,8 @@
 SEGS = 8
 TILE = 256
 EXT = CELLS + 512
+CHUNK = 1024
+PIECES = CELLS // CHUNK
 RELAXATION = 0.5
 MIXING_RATE = 0.3
 DAMPING = 0.2
@@ -78,10 +80,9 @@
         inverse_seg=pair_of(inverse_seg.reshape(2 * M, SEGS * 128)),
         to_spec=pair_of(spread * weights[None, :, None]),
         from_spec=pair_of(np.transpose(spread, (0, 2, 1))),
-        basis=np.ascontiguousarray(basis.T).astype(f),
         once=np.ascontiguousarray(np.transpose(update.reshape(3, NT, 2, 128), (2, 0, 1, 3))).astype(f),
         twice=np.ascontiguousarray(np.transpose(twice.reshape(3, NT, 2, 128), (2, 0, 1, 3))).astype(f),
-        row_weights=row_weights.astype(f),
+        row_weights=pair_of(row_weights),
     )
 
 
@@ -153,8 +154,13 @@
     return padded.T[:8]
 
 
-def prepare_kernel(off_ref, row_ref, first_ref, last_ref, colf_ref, coll_ref, send_ref):
-    del off_ref
+def place(info):
+    lat = info[1]
+    return lax.rem(lat, 2), lax.div(lat, 2), info[2] - lat * LAT_DEV
+
+
+def prepare_kernel(info, row_ref, first_ref, last_ref, colf_ref, coll_ref, send_ref):
+    del info
     row = row_ref[0]
     lane = lanes_of((KD, 128))
     hit_first = jnp.where(colf_ref[...] == 0, 1.0, 0.0)
@@ -176,7 +182,7 @@
         send_ref[s, 16:24, :] = edge
 
 
-def prepare(offset, atmosphere, clouds, col):
+def prepare(info, atmosphere, clouds, col):
     last = CELLS // 128 - 1
     return pl.pallas_call(
         prepare_kernel,
@@ -184,7 +190,7 @@
             num_scalar_prefetch=1,
             grid=(1,),
             in_specs=[
-                pl.BlockSpec((1, KD, NLON), lambda i, off: (off[0], 0, 0)),
+                pl.BlockSpec((1, KD, NLON), lambda i, info: (place(info)[2], 0, 0)),
                 pl.BlockSpec((K, 128), lambda i, off: (0, 0)),
                 pl.BlockSpec((K, 128), lambda i, off: (0, last)),
                 pl.BlockSpec((1, 128), lambda i, off: (0, 0)),
@@ -194,7 +200,7 @@
         ),
         out_shape=jax.ShapeDtypeStruct((SEGS, 24, 128), F32),
         name="prepare",
-    )(offset, atmosphere, clouds, clouds, col, col)
+    )(info, atmosphere, clouds, clouds, col, col)
 
 
 def column_of(row):
@@ -203,24 +209,43 @@
     return jnp.sum(jnp.where(diagonal, row, 0.0), axis=1, keepdims=True)
 
 
+def pieces(source, target, sems, shift=0):
+    return [
+        pltpu.make_async_copy(
+            source.at[:, i * CHUNK : (i + 1) * CHUNK],
+            target.at[:, shift + i * CHUNK : shift + (i + 1) * CHUNK],
+            sems.at[i],
+        )
+        for i in range(PIECES)
+    ]
+
+
 def inner_kernel(with_mean, *refs):
     if with_mean:
-        c_ref, col_ref, diff_ref, wind_ref, mixing_ref, base_ref, ends_ref, mean_ref, inv_ref = refs
+        c_hbm, col_ref, diff_ref, wind_ref, mixing_ref, base_hbm, mean_ref, inv_ref = refs[:8]
     else:
-        c_ref, diff_ref, wind_ref, mixing_ref, base_ref, ends_ref = refs
+        c_hbm, diff_ref, wind_ref, mixing_ref, base_hbm = refs[:5]
+    c_ref, base_ref, in_sems, out_sems = refs[-4:]
+    reads = pieces(c_hbm, c_ref, in_sems)
+    writes = pieces(base_ref, base_hbm, out_sems)
+    for copy in reads:
+        copy.start()
     zeros = jnp.zeros((K, 128), F32)
     mix = mixing_block(mixing_ref[...])
     diffusivity, wind = column_of(diff_ref[...]), column_of(wind_ref[...])
-    ends_ref[:, 0:256] = c_ref[:, 0:256]
-    ends_ref[:, 256:512] = c_ref[:, CELLS - 256 :]
     total = jnp.zeros((2 * K + 16, 128), F32)
+    reads[0].wait()
     for start in range(0, CELLS, TILE):
+        if start % CHUNK == 0 and start // CHUNK + 1 < PIECES:
+            reads[start // CHUNK + 1].wait()
         window = c_ref[:, max(start - 128, 0) : min(start + TILE + 128, CELLS)]
         if start == 0:
             window = jnp.concatenate([zeros, window], axis=1)
         if start + TILE == CELLS:
             window = jnp.concatenate([window, zeros], axis=1)
         base_ref[:, start : start + TILE] = substep_tile(window, mix, diffusivity, wind)
+        if (start + TILE) % CHUNK == 0:
+            writes[start // CHUNK].start()
         if with_mean:
             hits = column_hits(col_ref[:, start : start + TILE])
             high, low = split(window[:, 128 : 128 + TILE])
@@ -233,32 +258,61 @@
         inv = jnp.where(counts > 0.0, 1.0 / jnp.maximum(counts, 1.0), 0.0)
         inv_ref[...] = inv
         mean_ref[...] = (total[:K] + total[K : 2 * K]) * inv[0:1]
+    for copy in writes:
+        copy.wait()
 
 
 VMEM_SPEC = pl.BlockSpec(memory_space=pltpu.VMEM)
+HBM_SPEC = pl.BlockSpec(memory_space=pltpu.HBM)
+
+
+def in_hbm(x):
+    return pltpu.with_memory_space_constraint(x, pltpu.HBM)
+
+
+STATE_SCRATCH = [
+    pltpu.VMEM((K, CELLS), F32),
+    pltpu.VMEM((K, CELLS), F32),
+    pltpu.SemaphoreType.DMA((PIECES,)),
+    pltpu.SemaphoreType.DMA((PIECES,)),
+]
 
 
 def inner(clouds, col, diffusivity, wind, mixing, with_mean):
-    args = [clouds] + ([col] if with_mean else []) + [diffusivity, wind, mixing]
-    shapes = [jax.ShapeDtypeStruct((K, CELLS), F32), jax.ShapeDtypeStruct((K, 512), F32)]
+    args = [in_hbm(clouds)] + ([col] if with_mean else []) + [diffusivity, wind, mixing]
+    shapes = [pltpu.HBM((K, CELLS), F32)]
     if with_mean:
         shapes += [jax.ShapeDtypeStruct((K, 128), F32), jax.ShapeDtypeStruct((8, 128), F32)]
     return pl.pallas_call(
         lambda *refs: inner_kernel(with_mean, *refs),
-        in_specs=[VMEM_SPEC] * len(args),
-        out_specs=[VMEM_SPEC] * len(shapes),
+        in_specs=[HBM_SPEC] + [VMEM_SPEC] * (len(args) - 1),
+        out_specs=[HBM_SPEC] + [VMEM_SPEC] * (len(shapes) - 1),
         out_shape=shapes,
+        scratch_shapes=STATE_SCRATCH,
         cost_estimate=pl.CostEstimate(flops=1 << 10, bytes_accessed=1 << 10, transcendentals=0),
-        compiler_params=pltpu.CompilerParams(vmem_limit_bytes=6 << 20),
+        compiler_params=pltpu.CompilerParams(vmem_limit_bytes=10 << 20),
         name="inner",
     )(*args)
 
 
 def outer_kernel(
-    info, base_ref, ends_ref, prof_ref, halo_ref, perm_ref, back_ref, mean_ref, inv_ref,
-    col_ref, diff_ref, wind_ref, mixing_ref, out_ref, end_ref, send_ref, ext1, ext2, force,
+    info, base_hbm, c_hbm, prof_ref, halo_ref, perm_ref, back_ref, mean_ref, inv_ref,
+    col_ref, diff_ref, wind_ref, mixing_ref, out_hbm, end_ref, send_ref, ext1, ext2, force, ends_ref, end_sems, out_ref,
+    in_sems, out_sems,
 ):
     seg = info[0]
+    reads = pieces(base_hbm, ext1, in_sems, 256)
+    ends = [
+        pltpu.make_async_copy(
+            c_hbm.at[:, at : at + 256], ends_ref.at[:, 256 * i : 256 * i + 256], end_sems.at[i]
+        )
+        for i, at in enumerate((0, CELLS - 256))
+    ]
+    for copy in ends:
+        copy.start()
+    writes = pieces(out_ref, out_hbm, out_sems)
+    for copy in reads:
+        copy.start()
     lane = lanes_of((K, 128))
     zeros = jnp.zeros((K, 128), F32)
     mix = mixing_block(mixing_ref[...])
@@ -294,16 +348,20 @@
     right_col = jnp.full((1, 128), COLS, jnp.int32)
     for at in range(128, EXT - 128, TILE):
         cell = at - 256
+        if (cell + 128) % CHUNK == 0 and (cell + 128) // CHUNK < PIECES:
+            reads[(cell + 128) // CHUNK].wait()
         if cell < 0:
+            ends[0].wait()
             window = jnp.concatenate([zeros, left_tile, ends_ref[:, 0:256]], axis=1)
             value = substep_tile(window, mix, diffusivity, wind)
             col = jnp.concatenate([left_col, col_ref[:, 0:128]], axis=1)
         elif cell + TILE > CELLS:
+            ends[1].wait()
             window = jnp.concatenate([ends_ref[:, 256:512], right_tile, zeros], axis=1)
             value = substep_tile(window, mix, diffusivity, wind)
             col = jnp.concatenate([col_ref[:, CELLS - 128 :], right_col], axis=1)
         else:
-            value = base_ref[:, cell : cell + TILE]
+            value = ext1[:, at : at + TILE]
             col = col_ref[:, cell : cell + TILE]
         hits = column_hits(col)
         forced = jnp.dot(
@@ -324,6 +382,8 @@
         window = ext2[:, at - 128 : at + TILE + 128]
         value = substep_tile(window, mix, diffusivity, wind) + force[:, at : at + TILE]
         out_ref[:, cell : cell + TILE] = value
+        if (cell + TILE) % CHUNK == 0:
+            writes[cell // CHUNK].start()
         hits = column_hits(col_ref[:, cell : cell + TILE])
         rows = jnp.concatenate(split(value), axis=0)
         total = total + lax.dot_general(
@@ -339,12 +399,17 @@
     for s in range(send_ref.shape[0]):
         send_ref[s, 0:16, :] = sent[16 * (s % SEGS) : 16 * (s % SEGS) + 16]
         send_ref[s, 16:24, :] = edge
-
-
-def outer(info, *args):
+    for copy in writes:
+        copy.wait()
+
+
+def outer(info, base, clouds, *args):
     return call(
-        outer_kernel, "outer", args, [shape(K, CELLS), shape(K, 128), shape(SEGS, 24, 128)],
-        scratch=[pltpu.VMEM((K, EXT), F32)] * 3, prefetch=info, limit=14,
+        outer_kernel, "outer", (in_hbm(base), in_hbm(clouds), *args), [pltpu.HBM((K, CELLS), F32), shape(K, 128), shape(SEGS, 24, 128)],
+        scratch=[pltpu.VMEM((K, EXT), F32)] * 3
+        + [pltpu.VMEM((K, 512), F32), pltpu.SemaphoreType.DMA((2,))]
+        + STATE_SCRATCH[1:],
+        prefetch=info, limit=16, hbm=True,
     )
 
 
@@ -400,8 +465,8 @@
     ]
 
 
-def call(kernel, name, args, shapes, scratch=(), prefetch=None, limit=8, specs=None):
-    specs = specs or [VMEM_SPEC] * len(args)
+def call(kernel, name, args, shapes, scratch=(), prefetch=None, limit=8, hbm=False):
+    specs = [VMEM_SPEC] * len(args)
     common = dict(
         out_shape=shapes,
         name=name,
@@ -409,6 +474,8 @@
         compiler_params=pltpu.CompilerParams(vmem_limit_bytes=limit << 20),
     )
     outs = [VMEM_SPEC] * len(shapes)
+    if hbm:
+        specs[0] = specs[1] = outs[0] = HBM_SPEC
     if prefetch is None:
         return pl.pallas_call(
             kernel, in_specs=specs, out_specs=outs, scratch_shapes=list(scratch), **common
@@ -444,20 +511,40 @@
 
 
 def spread_kernel(info, got_ref, table, rows_ref, send_ref, held):
+    offset = place(info)[2]
     forced = received_rows([got_ref[:, 0:16, :]], table)[0]
     for h in range(2):
         held[h] = rows_ref[:, :, :, 128 * h : 128 * h + 128].reshape(384, 128)
         for v in range(3):
-            at = pl.ds(pl.multiple_of((v * 16 + info[2]) * 8, 8), 8)
+            at = pl.ds(pl.multiple_of((v * 16 + offset) * 8, 8), 8)
             held[h, at, :] += forced[v][:, 128 * h : 128 * h + 128]
-        held[h, LAT_DEV * 8 : LAT_DEV * 8 + 8, :] = jnp.full((8, 128), info[2], jnp.int32).astype(F32)
+        held[h, LAT_DEV * 8 : LAT_DEV * 8 + 8, :] = jnp.full((8, 128), offset, jnp.int32).astype(F32)
     for u in range(8):
         for h in range(2):
             send_ref[2 * u + h] = held[h, pl.ds(u, 48, stride=8), :]
 
 
+def channel_basis(spec_ref, table):
+    offsets = spec_ref[:, LAT_DEV, :][:, 0:1].astype(jnp.int32)
+    wanted = 16 * lax.broadcasted_iota(jnp.int32, (16, 256), 0) + offsets
+    picks = jnp.where(lanes_of((16, 256)) == wanted, 1.0, 0.0).astype(BF16)
+    return [jnp.dot(picks, t, preferred_element_type=F32) for t in table]
+
+
+def weights_kernel(info, mine_ref, others_ref, from_spec, row_weights, out_ref):
+    core, chip, _ = place(info)
+    own = pl.ds(pl.multiple_of(chip * 16, 16), 16)
+    here = from_spec[0, core, own, :].astype(F32) + from_spec[1, core, own, :].astype(F32)
+    for half, ref, side in ((0, mine_ref, core), (16, others_ref, 1 - core)):
+        high, low = channel_basis(ref, [from_spec[0, side], from_spec[1, side]])
+        basis = high + low
+        products = jnp.concatenate([basis[c : c + 1] * here for c in range(16)], axis=0)
+        out_ref[half : half + 16] = dot3(products, row_weights).reshape(16, 16, 3 * M)
+
+
 def settle_kernel(info, mine_ref, others_ref, to_spec, from_spec, once, twice, out_ref):
-    core, half = info[1], info[3]
+    core, chip, _ = place(info)
+    half = lax.rem(chip, 2)
 
     def columns(ref):
         return jnp.concatenate(
@@ -474,11 +561,9 @@
     )
     table = [from_spec[0, core], from_spec[1, core]]
     back = dot3_left(table, update(twice, spec))
-    offsets = mine_ref[:, LAT_DEV, :][:, 0:1].astype(jnp.int32)
-    wanted = 16 * lax.broadcasted_iota(jnp.int32, (16, 256), 0) + offsets
-    picks = jnp.where(lanes_of((16, 256)) == wanted, 1.0, 0.0).astype(BF16)
-    picked = [jnp.dot(picks, t, preferred_element_type=F32).astype(BF16) for t in table]
-    channels = dot3_left(picked, update(once, spec))
+    channels = dot3_left(
+        [t.astype(BF16) for t in channel_basis(mine_ref, table)], update(once, spec)
+    )
     for v in range(3):
         out_ref[:, 16 * v : 16 * v + 16, :] = back[:, 128 * v : 128 * v + 128].reshape(16, 16, 128)
         for q in range(16):
@@ -576,10 +661,7 @@
     natural, grouped = permutations()
     lat = lax.axis_index("lat").astype(jnp.int32)
     seg = lax.axis_index("seg").astype(jnp.int32)
-    core = lat % 2
-    chip = lat // 2
-    offset = channel_lat - lat * LAT_DEV
-    info = jnp.stack((seg, core, offset[0], chip % 2))
+    info = jnp.stack((seg, lat, channel_lat[0]))
     clouds = cloud_state[0]
     col = cell_column
     wind = channel_wind
@@ -588,21 +670,22 @@
     gather_rows = jnp.asarray(grouped)
     scatter_rows = jnp.asarray(grouped.T.copy())
 
-    send = prepare(offset, atmosphere, clouds, col)
+    send = prepare(info, atmosphere, clouds, col)
     got = lax.all_to_all(send, "seg", 0, 0, tiled=True)
     grid, state, send = lax.optimization_barrier((atmosphere, clouds, send))
-    base, ends, mean, inv = inner(state, col, diff, wind, mixing, True)
+    base, mean, inv = inner(state, col, diff, wind, mixing, True)
     rows = call(
         rows_kernel, "rows", (grid, tab["forward"]), [shape(3, 16, 8, M)],
         scratch=[pltpu.VMEM((144, NLON), F32)],
     )[0]
+    rows, got = lax.optimization_barrier((rows, got))
     clouds, mean_1, send = outer(
-        info, base, ends, got, got, jnp.asarray(natural), scatter_rows,
+        info, base, state, got, got, jnp.asarray(natural), scatter_rows,
         mean, inv, col, diff, wind, mixing,
     )
     halo = lax.all_to_all(send, "seg", 0, 0, tiled=True)
-    base, ends = inner(clouds, col, diff, wind, mixing, False)
-    base, ends, halo = lax.optimization_barrier((base, ends, halo))
+    base = inner(clouds, col, diff, wind, mixing, False)[0]
+    base, halo = lax.optimization_barrier((base, halo))
 
     spread = call(
         spread_kernel, "spread", (halo, spread_table, rows), [shape(16, 48, 128)],
@@ -620,23 +703,17 @@
         profile_kernel, "profile", (settled, tab["inverse_seg"]), [shape(SEGS, 16, 128)],
         scratch=[pltpu.VMEM((24, M), F32)],
     )[0]
+    profile, spec_mine, spec_others = lax.optimization_barrier((profile, spec_mine, spec_others))
+    factors = call(
+        weights_kernel, "weights", (spec_mine, spec_others, tab["from_spec"], tab["row_weights"]),
+        [shape(32, 16, 3 * M)], prefetch=info,
+    )[0]
     profile = lax.all_to_all(profile, "seg", 0, 0, tiled=True)
 
-    numbers = jnp.arange(16, dtype=jnp.int32)
-    near = (2 * numbers + core) * LAT_DEV + spec_mine[:, LAT_DEV, 0].astype(jnp.int32)
-    far = (2 * numbers + 1 - core) * LAT_DEV + spec_others[:, LAT_DEV, 0].astype(jnp.int32)
-    wanted = jnp.concatenate((near, far))
-    picks = (wanted[:, None] == jnp.arange(NLAT, dtype=jnp.int32)[None, :]).astype(F32)
-    basis = jnp.dot(picks, tab["basis"], precision=HIGHEST)
-    here = lax.dynamic_slice_in_dim(tab["basis"], lat * LAT_DEV, LAT_DEV, axis=0)
-    here = jnp.pad(here, ((0, 4), (0, 0)))
-    products = (basis[:, None] * here[None]).reshape(32 * 16, NT)
-    factors = jnp.dot(products, tab["row_weights"], precision=HIGH).reshape(32, 16, 3 * M)
-
     factors, profile = lax.optimization_barrier((factors, profile))
 
     clouds, _, send = outer(
-        info, base, ends, profile, halo, gather_rows, scatter_rows,
+        info, base, clouds, profile, halo, gather_rows, scatter_rows,
         mean_1, inv, col, diff, wind, mixing,
     )
     got = lax.all_to_all(send, "seg", 0, 0, tiled=True)

time: 146 us -> 141 us (0.966)
  blocking collectives: 49.6 us -> 67.6 us
  waiting for transfers between devices: 22.6 us -> 8.68 us
  local copies, waits for them, and re-layouts: 17.1 us -> 3.42 us
  Pallas kernels: 31.5 us -> 42.1 us
  starting transfers between devices: 18.9 us -> 14.5 us
    all_to_all x2 -> x3, blocking collectives: 40.8 us -> 58.8 us  [rows_exchange(): lax.all_to_all(x, 'lat', 0, 0, axis_index_groups=ROW_GROUPS, tiled=True)]
    all_to_all x1 -> x0, waiting for transfers between devices: 13.4 us -> none  [rows_exchange(): lax.all_to_all(x, 'lat', 0, 0, axis_index_groups=ROW_GROUPS, tiled=True)]
    unnamed x56 -> x42, local copies, waits for them, and re-layouts: 16.4 us -> 3.42 us
    pallas_call x4 -> x5, Pallas kernels: 18.9 us -> 24.5 us  [call(): pl.pallas_call(kernel, grid_spec=pltpu.PrefetchScalarGridSpec(num_scalar_...]
    all_to_all x1 -> x0, starting transfers between devices: 5.05 us -> none  [rows_exchange(): lax.all_to_all(x, 'lat', 0, 0, axis_index_groups=ROW_GROUPS, tiled=True)]
    pallas_call x2, Pallas kernels: 5.1 us -> 9.47 us  [inner(): pl.pallas_call(lambda *refs: inner_kernel(with_mean, *refs), in_specs=[HB...]
    all_to_all x1, waiting for transfers between devices: 5.53 us -> 3.68 us  [shards(): profile = lax.all_to_all(profile, 'seg', 0, 0, tiled=True)]
    all_to_all x1, waiting for transfers between devices: 0.01 us -> 1.61 us  [shards(): halo = lax.all_to_all(send, 'seg', 0, 0, tiled=True)]
  transfers between devices with their start and end apart: 6 -> 5, of which waited for: 5 -> 5; matrix products, arithmetic and copies ran while one was open for 2% -> 0% of each run, Pallas kernels for 5% -> 9%
where the time goes in v4:
time: 141 us; the launch traced here: 139 us
  blocking collectives  67.6 us (48%)
  Pallas kernels  42.1 us (30%)
  starting transfers between devices  14.5 us (10%)
  waiting for transfers between devices  8.68 us (6%)
  local copies, waits for them, and re-layouts  3.42 us (2%)
  between operations  1.49 us (1%)
    all_to_all x3, blocking collectives, rows_exchange(): lax.all_to_all(x, 'lat', 0, 0, axis_index_groups=ROW_GROUPS, tiled=True)  58.8 us
    pallas_call x5, Pallas kernels, call(): pl.pallas_call(kernel, grid_spec=pltpu.PrefetchScalarGridSpec(num_scalar_...  24.5 us
    pallas_call x2, Pallas kernels, inner(): pl.pallas_call(lambda *refs: inner_kernel(with_mean, *refs), in_specs=[HB...  9.47 us
    all_to_all x1, blocking collectives, shards(): got = lax.all_to_all(send, 'seg', 0, 0, tiled=True)  8.86 us
    pallas_call x5, Pallas kernels, call(): pl.pallas_call(kernel, in_specs=specs, out_specs=outs, scratch_shapes=lis...  5.57 us
    all_to_all x1, starting transfers between devices, shards(): got = lax.all_to_all(send, 'seg', 0, 0, tiled=True)  5.46 us
    all_to_all x1, starting transfers between devices, shards(): halo = lax.all_to_all(send, 'seg', 0, 0, tiled=True)  4.7 us
    all_to_all x1, starting transfers between devices, shards(): profile = lax.all_to_all(profile, 'seg', 0, 0, tiled=True)  4.39 us
  transfers between devices with their start and end apart: 5, of which 5 were waited for; matrix products, arithmetic and copies ran while one was open for 0% of the time, Pallas kernels for 9%

profile of v4, /device:TPU:32, one launch (start us, length us, event | category | flops | bytes accessed | tf_op | source)
XLA Modules:
  0.0 138.5 jit_solution(10543150039537913212)
XLA Ops:
  1.3 0.7 pad_add_fusion.info
  2.0 2.5 %prepare.1 = f32[8,24,128]{2,1,0:T(8,128)} custom-call(s32[3]{0:T(128)} %pad_add_fusion.info, f32[12,12,768]{2,1,0:T(8,128)} %grid_ref, f32[96,6144]{1,0:T(8,128)} %bitcast.9, f32[96,6144]{1,0:T(8,128)} %bitcast.10, s32[1,6144]{1,0:T(1,128)} %col_ref.3, s32[1,6144]{1,0:T(1,128)} %col_ref.3), custom_call_target="tpu_custom_call" | custom-call | tf_op jit(solution)/shard_map/prepare/pallas_call | solution.py:187
  4.5 5.5 %all-to-all-start = ((f32[8,24,128]{2,1,0:T(8,128)}), f32[8,24,128]{2,1,0:T(8,128)S(1)}, u32[]{:S(2)}, u32[]{:S(2)}) async-start(f32[8,24,128]{2,1,0:T(8,128)} %prepare.1), calls=%async_computation | async-start | bytes 196608 | tf_op jit(solution)/shard_map/all_to_all | solution.py:674
  10.0 0.0 copy-done.2
  10.0 0.0 copy-done.6
  10.0 0.0 copy-start.13
  10.0 0.0 copy-start.17
  10.0 0.0 copy-start.18
  10.0 0.6 rows.1.rows_ref
  10.6 0.0 copy-done.7
  10.7 0.0 copy-done.11
  10.7 0.0 copy-done.19
  10.7 0.0 copy-done.20
  10.7 4.7 %inner.2 = (f32[96,6144]{1,0:T(8,128)}, f32[96,128]{1,0:T(8,128)S(1)}, f32[8,128]{1,0:T(8,128)S(1)}) custom-call(f32[96,6144]{1,0:T(8,128)} %bitcast.11, s32[1,6144]{1,0:T(1,128)S(1)} %copy-done.11, f32[1,96]{1,0:T(1,128)S(1)} %bitcast.5, f32[1,96]{1,0:T(1,128)S(1)} %copy-done.20, f32[96,96]{1,0:T(8,128)S(1)} %copy-done.7), custom_call_target="tpu_custom_call" | custom-call | flops 1024 | bytes 1024 | tf_op jit(solution)/shard_map/inner/pallas_call | solution.py:286
  15.4 1.0 all-to-all-done.prof_ref.halo_ref
  16.4 0.0 copy-done.13
  16.4 0.0 copy-done.17
  16.4 9.7 %outer.2 = (f32[96,6144]{1,0:T(8,128)}, f32[96,128]{1,0:T(8,128)S(1)}, f32[8,24,128]{2,1,0:T(8,128)}) custom-call(s32[3]{0:T(128)S(1)} %copy-done.18, f32[96,6144]{1,0:T(8,128)} %get-tuple-element.22.base_hbm, f32[96,6144]{1,0:T(8,128)} %bitcast.12, f32[8,24,128]{2,1,0:T(8,128)S(1)} %all-to-all-done.prof_ref.halo_ref, ...), custom_call_target="tpu_custom_call" | custom-call | flops 1024 | bytes 1024 | tf_op jit(solution)/shard_map/outer/pallas_call | solution.py:483
  26.1 0.0 copy-start.15
  26.1 0.6 copy-done.15
  26.8 4.7 %all-to-all-start.1 = ((f32[8,24,128]{2,1,0:T(8,128)}), f32[8,24,128]{2,1,0:T(8,128)S(1)}, u32[]{:S(2)}, u32[]{:S(2)}) async-start(f32[8,24,128]{2,1,0:T(8,128)} %get-tuple-element.28), calls=%async_computation.1 | async-start | bytes 196608 | tf_op jit(solution)/shard_map/all_to_all | solution.py:686
  31.5 4.8 %inner.3.base_hbm = f32[96,6144]{1,0:T(8,128)} custom-call(f32[96,6144]{1,0:T(8,128)} %get-tuple-element.27.refs_0_.c_hbm, f32[1,96]{1,0:T(1,128)S(1)} %bitcast.7, f32[1,96]{1,0:T(1,128)S(1)} %copy-done.20, f32[96,96]{1,0:T(8,128)S(1)} %copy-done.7), custom_call_target="tpu_custom_call" | custom-call | flops 1024 | bytes 1024 | tf_op jit(solution)/shard_map/inner/pallas_call | solution.py:286
  36.3 0.0 copy-start.4
  36.3 1.6 %all-to-all-done.1.got_ref.halo_ref = f32[8,24,128]{2,1,0:T(8,128)S(1)} async-done(((f32[8,24,128]{2,1,0:T(8,128)}), f32[8,24,128]{2,1,0:T(8,128)S(1)}, u32[]{:S(2)}, u32[]{:S(2)}) %all-to-all-start.1) | async-done | bytes 98336 | tf_op jit(solution)/shard_map/all_to_all | solution.py:686
  37.9 1.0 spread.1
  38.9 22.8 %all_to_all.35.mine_ref = f32[16,48,128]{2,1,0:T(8,128)S(1)} all-to-all(f32[16,48,128]{2,1,0:T(8,128)S(1)} %spread.1), channel_id=1, replica_groups={{0,16,32,48,64,80,96,112,128,144,160,176,192,208,224,240},{8,24,40,56,7..., dimensions={0} | all-to-all | bytes 786432 | tf_op jit(solution)/shard_map/all_to_all | solution.py:652
  61.8 0.0 collective-permute-start
  61.8 1.7 %collective-permute-done.others_ref = f32[16,48,128]{2,1,0:T(8,128)S(1)} collective-permute-done((f32[16,48,128]{2,1,0:T(8,128)S(1)}, f32[16,48,128]{2,1,0:T(8,128)S(1)}, u32[]{:S(2)}, u32[]{:S(2)}) %collective-permute-start) | collective-permute-done | bytes 393248 | tf_op jit(solution)/shard_map/ppermute | solution.py:656
  63.5 0.0 copy-done.4
  63.5 1.6 %settle.1 = f32[16,48,128]{2,1,0:T(8,128)S(1)} custom-call(s32[3]{0:T(128)S(1)} %copy-done.18, f32[16,48,128]{2,1,0:T(8,128)S(1)} %all_to_all.35.mine_ref, f32[16,48,128]{2,1,0:T(8,128)S(1)} %collective-permute-done.others_ref, bf16[2,2,256,256]{3,2,1,0:T(8,128)(2,1)S(1)} %copy-done.12, bf16[2,2,256,256]{3,2,1,0:T(8,128)(2,1)S(1)} %copy-done.4, ...), custom_call_target="tpu_custom_call" | custom-call | flops 1024 | bytes 1024 | tf_op jit(solution)/shard_map/settle/pallas_call | solution.py:483
  65.1 18.8 %all_to_all.36.got_ref = f32[16,48,128]{2,1,0:T(8,128)S(1)} all-to-all(f32[16,48,128]{2,1,0:T(8,128)S(1)} %settle.1), channel_id=1, replica_groups={{0,16,32,48,64,80,96,112,128,144,160,176,192,208,224,240},{8,24,40,56,7..., dimensions={0} | all-to-all | bytes 786432 | tf_op jit(solution)/shard_map/all_to_all | solution.py:652
  83.9 1.1 profile.1
  85.0 4.4 %all-to-all-start.4 = ((f32[8,16,128]{2,1,0:T(8,128)}), f32[8,16,128]{2,1,0:T(8,128)}, u32[]{:S(2)}, u32[]{:S(2)}) async-start(f32[8,16,128]{2,1,0:T(8,128)} %profile.1), calls=%async_computation.4 | async-start | bytes 131072 | tf_op jit(solution)/shard_map/all_to_all | solution.py:711
  89.4 1.1 copy-done.8
  90.5 1.6 %weights.1.factors = f32[32,16,768]{2,1,0:T(8,128)S(1)} custom-call(s32[3]{0:T(128)S(1)} %copy-done.18, f32[16,48,128]{2,1,0:T(8,128)S(1)} %all_to_all.35.mine_ref, f32[16,48,128]{2,1,0:T(8,128)S(1)} %collective-permute-done.others_ref, bf16[2,2,256,256]{3,2,1,0:T(8,128)(2,1)S(1)} %copy-done.4, bf16[2,256,768]{2,1,0:T(8,128)(2,1)S(1)} %copy-done.8), custom_call_target="tpu_custom_call" | custom-call | flops 1024 | bytes 1024 | tf_op jit(solution)/shard_map/weights/pallas_call | solution.py:483
  92.1 3.7 %all-to-all-done.4.prof_ref = f32[8,16,128]{2,1,0:T(8,128)} async-done(((f32[8,16,128]{2,1,0:T(8,128)}), f32[8,16,128]{2,1,0:T(8,128)}, u32[]{:S(2)}, u32[]{:S(2)}) %all-to-all-start.4) | async-done | bytes 65568 | tf_op jit(solution)/shard_map/all_to_all | solution.py:711
  95.8 0.8 copy-done.14
  96.6 0.8 copy-done.16
  97.4 10.6 %outer.3 = (f32[96,6144]{1,0:T(8,128)}, f32[96,128]{1,0:T(8,128)}, f32[8,24,128]{2,1,0:T(8,128)S(1)}) custom-call(s32[3]{0:T(128)S(1)} %copy-done.18, f32[96,6144]{1,0:T(8,128)} %inner.3.base_hbm, f32[96,6144]{1,0:T(8,128)} %get-tuple-element.27.refs_0_.c_hbm, f32[8,16,128]{2,1,0:T(8,128)} %all-to-all-done.4.prof_ref, ...), custom_call_target="tpu_custom_call" | custom-call | flops 1024 | bytes 1024 | tf_op jit(solution)/shard_map/outer/pallas_call | solution.py:483
  108.0 8.9 %all_to_all.37.got_ref = f32[8,24,128]{2,1,0:T(8,128)S(1)} all-to-all(f32[8,24,128]{2,1,0:T(8,128)S(1)} %get-tuple-element.38), channel_id=1, replica_groups=mesh['lat'=32,'seg'=8] {'seg'}, dimensions={0} | all-to-all | bytes 196608 | tf_op jit(solution)/shard_map/all_to_all | solution.py:719
  116.9 0.4 last.1
  117.3 0.0 copy-start.5
  117.3 17.1 %all_to_all.38.from_ref = f32[16,24,256]{2,1,0:T(8,128)S(1)} all-to-all(f32[16,24,256]{2,1,0:T(8,128)S(1)} %last.1), channel_id=1, replica_groups={{0,16,32,48,64,80,96,112,128,144,160,176,192,208,224,240},{8,24,40,56,7..., dimensions={0} | all-to-all | bytes 786432 | tf_op jit(solution)/shard_map/all_to_all | solution.py:652
  134.4 0.0 collective-permute-start.1
  134.4 1.1 gather.1.part_ref
  135.5 0.6 collective-permute-done.1.from_ref
  136.1 0.0 copy-done.5
  136.1 2.4 %finish.1 = f32[12,12,768]{2,1,0:T(8,128)} custom-call(f32[3,16,8,256]{3,2,1,0:T(8,128)S(1)} %gather.1.part_ref, f32[32,16,768]{2,1,0:T(8,128)S(1)} %weights.1.factors, f32[16,24,256]{2,1,0:T(8,128)S(1)} %collective-permute-done.1.from_ref, bf16[2,512,768]{2,1,0:T(8,128)(2,1)S(1)} %copy-done.5), custom_call_target="tpu_custom_call" | custom-call | flops 1024 | bytes 1024 | tf_op jit(solution)/shard_map/finish/pallas_call | solution.py:480
  (22 shorter events, 0.0 us)
Async XLA Ops:
  1.9 8.0 %copy-start.2 = (f32[12,12,768]{2,1,0:T(8,128)S(1)}, f32[12,12,768]{2,1,0:T(8,128)}, u32[]{:S(2)}) copy-start(f32[12,12,768]{2,1,0:T(8,128)} %grid_ref) | copy-start | bytes 1327108
  2.0 8.0 %copy-start.6 = (bf16[2,768,512]{2,1,0:T(8,128)(2,1)S(1)}, bf16[2,768,512]{2,1,0:T(8,128)(2,1)}, u32[]{:S(2)}) copy-start(bf16[2,768,512]{2,1,0:T(8,128)(2,1)} %constant.33.clone.table) | copy-start | bytes 4718596
  4.5 6.1 %copy-start.7 = (f32[96,96]{1,0:T(8,128)S(1)}, f32[96,96]{1,0:T(8,128)}, u32[]{:S(2)}) copy-start(f32[96,96]{1,0:T(8,128)} %mixing_ref.3) | copy-start | bytes 110596
  4.5 6.2 %copy-start.11 = (s32[1,6144]{1,0:T(1,128)S(1)}, s32[1,6144]{1,0:T(1,128)}, u32[]{:S(2)}) copy-start(s32[1,6144]{1,0:T(1,128)} %col_ref.3) | copy-start | bytes 73732
  4.5 6.2 %copy-start.19 = (f32[96]{0:T(128)S(1)}, f32[96]{0:T(128)}, u32[]{:S(2)}) copy-start(f32[96]{0:T(128)} %param.24) | copy-start | bytes 1156
  4.5 6.2 %copy-start.20 = (f32[1,96]{1,0:T(1,128)S(1)}, f32[1,96]{1,0:T(1,128)}, u32[]{:S(2)}) copy-start(f32[1,96]{1,0:T(1,128)} %wind_ref.3) | copy-start | bytes 1156
  4.5 11.9 %all-to-all-start = ((f32[8,24,128]{2,1,0:T(8,128)}), f32[8,24,128]{2,1,0:T(8,128)S(1)}, u32[]{:S(2)}, u32[]{:S(2)}) async-start(f32[8,24,128]{2,1,0:T(8,128)} %prepare.1), calls=%async_computation | async-start | bytes 196608 | tf_op jit(solution)/shard_map/all_to_all | solution.py:674
  10.0 6.4 %copy-start.13 = (f32[128,96]{1,0:T(8,128)S(1)}, f32[128,96]{1,0:T(8,128)}, u32[]{:S(2)}) copy-start(f32[128,96]{1,0:T(8,128)} %constant.43.clone.back_ref) | copy-start | bytes 147460
  10.0 6.4 %copy-start.17 = (f32[96,128]{1,0:T(8,128)S(1)}, f32[96,128]{1,0:T(8,128)}, u32[]{:S(2)}) copy-start(f32[96,128]{1,0:T(8,128)} %constant.44.clone.perm_ref) | copy-start | bytes 147460
  10.0 6.4 %copy-start.18 = (s32[3]{0:T(128)S(1)}, s32[3]{0:T(128)}, u32[]{:S(2)}) copy-start(s32[3]{0:T(128)} %pad_add_fusion.info) | copy-start | bytes 40
  26.1 0.6 copy-start.15
  26.8 11.1 %all-to-all-start.1 = ((f32[8,24,128]{2,1,0:T(8,128)}), f32[8,24,128]{2,1,0:T(8,128)S(1)}, u32[]{:S(2)}, u32[]{:S(2)}) async-start(f32[8,24,128]{2,1,0:T(8,128)} %get-tuple-element.28), calls=%async_computation.1 | async-start | bytes 196608 | tf_op jit(solution)/shard_map/all_to_all | solution.py:686
  31.4 6.4 %copy-start = (bf16[2,1024,512]{2,1,0:T(8,128)(2,1)S(1)}, bf16[2,1024,512]{2,1,0:T(8,128)(2,1)}, u32[]{:S(2)}) copy-start(bf16[2,1024,512]{2,1,0:T(8,128)(2,1)} %constant.35.clone.table) | copy-start | bytes 6291460
  36.3 27.2 %copy-start.4 = (bf16[2,2,256,256]{3,2,1,0:T(8,128)(2,1)S(1)}, bf16[2,2,256,256]{3,2,1,0:T(8,128)(2,1)}, u32[]{:S(2)}) copy-start(bf16[2,2,256,256]{3,2,1,0:T(8,128)(2,1)} %constant.38.clone.from_spec) | copy-start | bytes 1572868
  37.9 25.6 %copy-start.9 = (f32[2,3,256,128]{3,2,1,0:T(8,128)S(1)}, f32[2,3,256,128]{3,2,1,0:T(8,128)}, u32[]{:S(2)}) copy-start(f32[2,3,256,128]{3,2,1,0:T(8,128)} %constant.40.clone.twice) | copy-start | bytes 2359300
  37.9 25.6 %copy-start.10 = (f32[2,3,256,128]{3,2,1,0:T(8,128)S(1)}, f32[2,3,256,128]{3,2,1,0:T(8,128)}, u32[]{:S(2)}) copy-start(f32[2,3,256,128]{3,2,1,0:T(8,128)} %constant.39.clone.once) | copy-start | bytes 2359300
  37.9 25.6 %copy-start.12 = (bf16[2,2,256,256]{3,2,1,0:T(8,128)(2,1)S(1)}, bf16[2,2,256,256]{3,2,1,0:T(8,128)(2,1)}, u32[]{:S(2)}) copy-start(bf16[2,2,256,256]{3,2,1,0:T(8,128)(2,1)} %constant.37.clone.to_spec) | copy-start | bytes 1572868
  61.8 22.2 %copy-start.3 = (bf16[2,512,1024]{2,1,0:T(8,128)(2,1)S(1)}, bf16[2,512,1024]{2,1,0:T(8,128)(2,1)}, u32[]{:S(2)}) copy-start(bf16[2,512,1024]{2,1,0:T(8,128)(2,1)} %constant.36.clone.table) | copy-start | bytes 6291460
  61.8 1.7 %collective-permute-start = (f32[16,48,128]{2,1,0:T(8,128)S(1)}, f32[16,48,128]{2,1,0:T(8,128)S(1)}, u32[]{:S(2)}, u32[]{:S(2)}) collective-permute-start(f32[16,48,128]{2,1,0:T(8,128)S(1)} %all_to_all.35.mine_ref), channel_id=1, source_target_pairs={{0,8},{8,0},{16,24},{24,16},{32,40},{40,32},{48,56},{56,48},{64,72... | collective-permute-start | bytes 1179656 | tf_op jit(solution)/shard_map/ppermute | solution.py:656
  85.0 10.8 %all-to-all-start.4 = ((f32[8,16,128]{2,1,0:T(8,128)}), f32[8,16,128]{2,1,0:T(8,128)}, u32[]{:S(2)}, u32[]{:S(2)}) async-start(f32[8,16,128]{2,1,0:T(8,128)} %profile.1), calls=%async_computation.4 | async-start | bytes 131072 | tf_op jit(solution)/shard_map/all_to_all | solution.py:711
  89.4 1.1 copy-start.8
  95.8 0.8 copy-start.14
  96.6 0.8 copy-start.16
  97.4 19.4 %copy-start.1 = (bf16[2,1024,512]{2,1,0:T(8,128)(2,1)S(1)}, bf16[2,1024,512]{2,1,0:T(8,128)(2,1)}, u32[]{:S(2)}) copy-start(bf16[2,1024,512]{2,1,0:T(8,128)(2,1)} %constant.35.clone.table) | copy-start | bytes 6291460
  117.3 18.8 %copy-start.5 = (bf16[2,512,768]{2,1,0:T(8,128)(2,1)S(1)}, bf16[2,512,768]{2,1,0:T(8,128)(2,1)}, u32[]{:S(2)}) copy-start(bf16[2,512,768]{2,1,0:T(8,128)(2,1)} %constant.34.clone.table) | copy-start | bytes 4718596
  134.4 1.7 %collective-permute-start.1 = (f32[16,24,256]{2,1,0:T(8,128)S(1)}, f32[16,24,256]{2,1,0:T(8,128)S(1)}, u32[]{:S(2)}, u32[]{:S(2)}) collective-permute-start(f32[16,24,256]{2,1,0:T(8,128)S(1)} %all_to_all.38.from_ref), channel_id=1, source_target_pairs={{0,8},{8,0},{16,24},{24,16},{32,40},{40,32},{48,56},{56,48},{64,72... | collective-permute-start | bytes 1179656 | tf_op jit(solution)/shard_map/ppermute | solution.py:656

commit v5 on v4

--- a/solution.py
+++ b/solution.py
@@ -20,8 +20,11 @@
 LATS = 32
 SEGS = 8
 TILE = 256
+T2 = 1280
+T3 = 1536
+TI = 1536
 EXT = CELLS + 512
-CHUNK = 1024
+CHUNK = 1536
 PIECES = CELLS // CHUNK
 RELAXATION = 0.5
 MIXING_RATE = 0.3
@@ -29,8 +32,6 @@
 COUPLING = 2.0
 F32 = jnp.float32
 BF16 = jnp.bfloat16
-HIGHEST = lax.Precision.HIGHEST
-HIGH = lax.Precision.HIGH
 
 ROW_GROUPS = [[2 * q + b for q in range(16)] for b in range(2)]
 CORE_SWAP = [(i, i ^ 1) for i in range(LATS)]
@@ -93,16 +94,6 @@
     return np.stack((high, low))
 
 
-def permutations():
-    natural = np.zeros((K, SEGS * 16), np.float32)
-    grouped = np.zeros((K, SEGS * 16), np.float32)
-    for s in range(SEGS):
-        for i in range(KD):
-            natural[KD * s + i, 16 * s + i] = 1.0
-            grouped[KD * s + i, 16 * s + (i % 3) * 4 + i // 3] = 1.0
-    return natural, grouped
-
-
 def lanes_of(shape):
     return lax.broadcasted_iota(jnp.int32, shape, len(shape) - 1)
 
@@ -139,6 +130,25 @@
 def column_hits(col):
     ids = lax.broadcasted_iota(jnp.int32, (128, col.shape[1]), 0)
     return jnp.where(ids == col, 1.0, 0.0).astype(BF16)
+
+
+def row_order(grouped, transposed):
+    size = (SEGS * 16, K) if transposed else (K, SEGS * 16)
+    pair = lax.broadcasted_iota(jnp.int32, size, 1 if transposed else 0)
+    row = lax.broadcasted_iota(jnp.int32, size, 0 if transposed else 1)
+    owner = (pair * 43691) >> 19
+    within = pair - KD * owner
+    level = (within * 11) >> 5
+    place_in = (within - 3 * level) * 4 + level if grouped else within
+    return jnp.where(row == 16 * owner + place_in, 1.0, 0.0).astype(BF16)
+
+
+def reorder(matrix, x):
+    high, low = split(x)
+    rest = (x - high.astype(F32) - low.astype(F32)).astype(BF16)
+    width = x.shape[1]
+    out = jnp.dot(matrix, jnp.concatenate([high, low, rest], axis=1), preferred_element_type=F32)
+    return out[:, :width] + out[:, width : 2 * width] + out[:, 2 * width :]
 
 
 def edge_rows(first, last, mean_first, mean_last):
@@ -222,7 +232,8 @@
 
 def inner_kernel(with_mean, *refs):
     if with_mean:
-        c_hbm, col_ref, diff_ref, wind_ref, mixing_ref, base_hbm, mean_ref, inv_ref = refs[:8]
+        c_hbm, col_ref, diff_ref, wind_ref, mixing_ref, base_hbm, mean_hbm, inv_ref = refs[:8]
+        mean_ref, mean_sem = refs[8:10]
     else:
         c_hbm, diff_ref, wind_ref, mixing_ref, base_hbm = refs[:5]
     c_ref, base_ref, in_sems, out_sems = refs[-4:]
@@ -235,21 +246,21 @@
     diffusivity, wind = column_of(diff_ref[...]), column_of(wind_ref[...])
     total = jnp.zeros((2 * K + 16, 128), F32)
     reads[0].wait()
-    for start in range(0, CELLS, TILE):
+    for start in range(0, CELLS, TI):
         if start % CHUNK == 0 and start // CHUNK + 1 < PIECES:
             reads[start // CHUNK + 1].wait()
-        window = c_ref[:, max(start - 128, 0) : min(start + TILE + 128, CELLS)]
+        window = c_ref[:, max(start - 128, 0) : min(start + TI + 128, CELLS)]
         if start == 0:
             window = jnp.concatenate([zeros, window], axis=1)
-        if start + TILE == CELLS:
+        if start + TI == CELLS:
             window = jnp.concatenate([window, zeros], axis=1)
-        base_ref[:, start : start + TILE] = substep_tile(window, mix, diffusivity, wind)
-        if (start + TILE) % CHUNK == 0:
+        base_ref[:, start : start + TI] = substep_tile(window, mix, diffusivity, wind)
+        if (start + TI) % CHUNK == 0:
             writes[start // CHUNK].start()
         if with_mean:
-            hits = column_hits(col_ref[:, start : start + TILE])
-            high, low = split(window[:, 128 : 128 + TILE])
-            rows = jnp.concatenate([high, low, jnp.ones((16, TILE), BF16)], axis=0)
+            hits = column_hits(col_ref[:, start : start + TI])
+            high, low = split(window[:, 128 : 128 + TI])
+            rows = jnp.concatenate([high, low, jnp.ones((16, TI), BF16)], axis=0)
             total = total + lax.dot_general(
                 rows, hits, (((1,), (1,)), ((), ())), preferred_element_type=F32
             )
@@ -258,12 +269,16 @@
         inv = jnp.where(counts > 0.0, 1.0 / jnp.maximum(counts, 1.0), 0.0)
         inv_ref[...] = inv
         mean_ref[...] = (total[:K] + total[K : 2 * K]) * inv[0:1]
+        mean_write = pltpu.make_async_copy(mean_ref, mean_hbm, mean_sem)
+        mean_write.start()
+        mean_write.wait()
     for copy in writes:
         copy.wait()
 
 
 VMEM_SPEC = pl.BlockSpec(memory_space=pltpu.VMEM)
 HBM_SPEC = pl.BlockSpec(memory_space=pltpu.HBM)
+MEAN_SCRATCH = [pltpu.VMEM((K, 128), F32), pltpu.SemaphoreType.DMA]
 
 
 def in_hbm(x):
@@ -282,13 +297,13 @@
     args = [in_hbm(clouds)] + ([col] if with_mean else []) + [diffusivity, wind, mixing]
     shapes = [pltpu.HBM((K, CELLS), F32)]
     if with_mean:
-        shapes += [jax.ShapeDtypeStruct((K, 128), F32), jax.ShapeDtypeStruct((8, 128), F32)]
+        shapes += [pltpu.HBM((K, 128), F32), jax.ShapeDtypeStruct((8, 128), F32)]
     return pl.pallas_call(
         lambda *refs: inner_kernel(with_mean, *refs),
         in_specs=[HBM_SPEC] + [VMEM_SPEC] * (len(args) - 1),
-        out_specs=[HBM_SPEC] + [VMEM_SPEC] * (len(shapes) - 1),
+        out_specs=([HBM_SPEC, HBM_SPEC, VMEM_SPEC] if with_mean else [HBM_SPEC]),
         out_shape=shapes,
-        scratch_shapes=STATE_SCRATCH,
+        scratch_shapes=MEAN_SCRATCH * with_mean + STATE_SCRATCH,
         cost_estimate=pl.CostEstimate(flops=1 << 10, bytes_accessed=1 << 10, transcendentals=0),
         compiler_params=pltpu.CompilerParams(vmem_limit_bytes=10 << 20),
         name="inner",
@@ -296,18 +311,21 @@
 
 
 def outer_kernel(
-    info, base_hbm, c_hbm, prof_ref, halo_ref, perm_ref, back_ref, mean_ref, inv_ref,
-    col_ref, diff_ref, wind_ref, mixing_ref, out_hbm, end_ref, send_ref, ext1, ext2, force, ends_ref, end_sems, out_ref,
-    in_sems, out_sems,
+    grouped, info, base_hbm, c_hbm, mean_hbm, prof_ref, halo_ref, inv_ref, col_ref, diff_ref, wind_ref,
+    mixing_ref, out_hbm, end_hbm, send_ref, ext1, ext2, force, ends_ref, mean_ref, end_ref, small_sems,
+    out_ref, in_sems, out_sems,
 ):
     seg = info[0]
     reads = pieces(base_hbm, ext1, in_sems, 256)
     ends = [
         pltpu.make_async_copy(
-            c_hbm.at[:, at : at + 256], ends_ref.at[:, 256 * i : 256 * i + 256], end_sems.at[i]
+            c_hbm.at[:, at : at + 256], ends_ref.at[:, 256 * i : 256 * i + 256], small_sems.at[i]
         )
         for i, at in enumerate((0, CELLS - 256))
     ]
+    mean_read = pltpu.make_async_copy(mean_hbm, mean_ref, small_sems.at[2])
+    mean_read.start()
+    end_write = pltpu.make_async_copy(end_ref, end_hbm, small_sems.at[3])
     for copy in ends:
         copy.start()
     writes = pieces(out_ref, out_hbm, out_sems)
@@ -323,6 +341,7 @@
     edges = jnp.concatenate([from_left, from_right, jnp.zeros((112, 128), F32)], axis=0).T[:K]
     left_tile = jnp.where(lane >= 125, pltpu.roll(edges, 122, 1), 0.0)
     right_tile = jnp.where(lane < 3, pltpu.roll(edges, 120, 1), 0.0)
+    mean_read.wait()
     mean = mean_ref[...]
     mean_all = jnp.where(
         lane < COLS,
@@ -333,11 +352,8 @@
             jnp.where(lane == COLS + 1, pltpu.roll(edges, COLS + 1 - 7, 1), 0.0),
         ),
     )
-    profile = jnp.dot(
-        perm_ref[...],
-        prof_ref[:, 0:16, :].reshape(SEGS * 16, 128),
-        precision=HIGHEST,
-        preferred_element_type=F32,
+    profile = reorder(
+        row_order(grouped, False), prof_ref[:, 0:16, :].reshape(SEGS * 16, 128)
     )
     pulled = jnp.where(lane < COLS + 2, RELAXATION * (profile - mean_all), 0.0)
     pulled = jnp.concatenate(split(pulled), axis=1)
@@ -346,6 +362,19 @@
     ext1[:, EXT - 128 :] = zeros
     left_col = jnp.full((1, 128), COLS + 1, jnp.int32)
     right_col = jnp.full((1, 128), COLS, jnp.int32)
+    for at in range(128, EXT - 128, TILE):
+        cell = at - 256
+        if cell < 0:
+            col = jnp.concatenate([left_col, col_ref[:, 0:128]], axis=1)
+        elif cell + TILE > CELLS:
+            col = jnp.concatenate([col_ref[:, CELLS - 128 :], right_col], axis=1)
+        else:
+            col = col_ref[:, cell : cell + TILE]
+        hits = column_hits(col)
+        force[:, at : at + TILE] = jnp.dot(
+            pulled, jnp.concatenate([hits, hits], axis=0), preferred_element_type=F32
+        )
+
     for at in range(128, EXT - 128, TILE):
         cell = at - 256
         if (cell + 128) % CHUNK == 0 and (cell + 128) // CHUNK < PIECES:
@@ -354,62 +383,59 @@
             ends[0].wait()
             window = jnp.concatenate([zeros, left_tile, ends_ref[:, 0:256]], axis=1)
             value = substep_tile(window, mix, diffusivity, wind)
-            col = jnp.concatenate([left_col, col_ref[:, 0:128]], axis=1)
         elif cell + TILE > CELLS:
             ends[1].wait()
             window = jnp.concatenate([ends_ref[:, 256:512], right_tile, zeros], axis=1)
             value = substep_tile(window, mix, diffusivity, wind)
-            col = jnp.concatenate([col_ref[:, CELLS - 128 :], right_col], axis=1)
         else:
             value = ext1[:, at : at + TILE]
-            col = col_ref[:, cell : cell + TILE]
-        hits = column_hits(col)
-        forced = jnp.dot(
-            pulled, jnp.concatenate([hits, hits], axis=0), preferred_element_type=F32
+        ext1[:, at : at + TILE] = value + force[:, at : at + TILE]
+
+    for at in range(128, EXT - 128, T2):
+        window = ext1[:, at - 128 : at + T2 + 128]
+        ext2[:, at : at + T2] = (
+            substep_tile(window, mix, diffusivity, wind) + force[:, at : at + T2]
         )
-        force[:, at : at + TILE] = forced
-        ext1[:, at : at + TILE] = value + forced
-
-    for at in range(128, EXT - 128, TILE):
-        window = ext1[:, at - 128 : at + TILE + 128]
-        ext2[:, at : at + TILE] = (
-            substep_tile(window, mix, diffusivity, wind) + force[:, at : at + TILE]
-        )
 
     total = jnp.zeros((2 * K, 128), F32)
-    for cell in range(0, CELLS, TILE):
+    for cell in range(0, CELLS, T3):
         at = cell + 256
-        window = ext2[:, at - 128 : at + TILE + 128]
-        value = substep_tile(window, mix, diffusivity, wind) + force[:, at : at + TILE]
-        out_ref[:, cell : cell + TILE] = value
-        if (cell + TILE) % CHUNK == 0:
+        window = ext2[:, at - 128 : at + T3 + 128]
+        value = substep_tile(window, mix, diffusivity, wind) + force[:, at : at + T3]
+        out_ref[:, cell : cell + T3] = value
+        if (cell + T3) % CHUNK == 0:
             writes[cell // CHUNK].start()
-        hits = column_hits(col_ref[:, cell : cell + TILE])
+        hits = column_hits(col_ref[:, cell : cell + T3])
         rows = jnp.concatenate(split(value), axis=0)
         total = total + lax.dot_general(
             rows, hits, (((1,), (1,)), ((), ())), preferred_element_type=F32
         )
     end = (total[:K] + total[K:]) * inv_ref[0:1]
     end_ref[...] = end
+    end_write.start()
     tendency = jnp.where(lane < COLS, end - mean, 0.0)
-    sent = jnp.dot(back_ref[...], tendency, precision=HIGHEST, preferred_element_type=F32)
+    sent = reorder(row_order(True, True), tendency)
     edge = edge_rows(
         out_ref[:, 0:128], out_ref[:, CELLS - 128 :], end[:, 0:1], end[:, COLS - 1 : COLS]
     )
     for s in range(send_ref.shape[0]):
         send_ref[s, 0:16, :] = sent[16 * (s % SEGS) : 16 * (s % SEGS) + 16]
         send_ref[s, 16:24, :] = edge
+    end_write.wait()
     for copy in writes:
         copy.wait()
 
 
-def outer(info, base, clouds, *args):
+def outer(grouped, info, base, clouds, mean, *args):
     return call(
-        outer_kernel, "outer", (in_hbm(base), in_hbm(clouds), *args), [pltpu.HBM((K, CELLS), F32), shape(K, 128), shape(SEGS, 24, 128)],
+        lambda *refs: outer_kernel(grouped, *refs), "outer",
+        (in_hbm(base), in_hbm(clouds), in_hbm(mean), *args),
+        [pltpu.HBM((K, CELLS), F32), pltpu.HBM((K, 128), F32), shape(SEGS, 24, 128)],
         scratch=[pltpu.VMEM((K, EXT), F32)] * 3
-        + [pltpu.VMEM((K, 512), F32), pltpu.SemaphoreType.DMA((2,))]
+        + [pltpu.VMEM((K, 512), F32), pltpu.VMEM((K, 128), F32), pltpu.VMEM((K, 128), F32)]
+        + [pltpu.SemaphoreType.DMA((4,))]
         + STATE_SCRATCH[1:],
-        prefetch=info, limit=16, hbm=True,
+        prefetch=info, limit=16, hbm=(3, 2),
     )
 
 
@@ -465,7 +491,7 @@
     ]
 
 
-def call(kernel, name, args, shapes, scratch=(), prefetch=None, limit=8, hbm=False):
+def call(kernel, name, args, shapes, scratch=(), prefetch=None, limit=8, hbm=(0, 0)):
     specs = [VMEM_SPEC] * len(args)
     common = dict(
         out_shape=shapes,
@@ -474,8 +500,8 @@
         compiler_params=pltpu.CompilerParams(vmem_limit_bytes=limit << 20),
     )
     outs = [VMEM_SPEC] * len(shapes)
-    if hbm:
-        specs[0] = specs[1] = outs[0] = HBM_SPEC
+    specs[: hbm[0]] = [HBM_SPEC] * hbm[0]
+    outs[: hbm[1]] = [HBM_SPEC] * hbm[1]
     if prefetch is None:
         return pl.pallas_call(
             kernel, in_specs=specs, out_specs=outs, scratch_shapes=list(scratch), **common
@@ -658,7 +684,6 @@
 
 def shards(atmosphere, cloud_state, channel_lat, cell_column, channel_wind, diffusivity, mixing):
     tab = {name: jnp.asarray(value) for name, value in tables().items()}
-    natural, grouped = permutations()
     lat = lax.axis_index("lat").astype(jnp.int32)
     seg = lax.axis_index("seg").astype(jnp.int32)
     info = jnp.stack((seg, lat, channel_lat[0]))
@@ -667,8 +692,6 @@
     wind = channel_wind
     diff = diffusivity.reshape(1, K)
     spread_table = tab["forward_seg"]
-    gather_rows = jnp.asarray(grouped)
-    scatter_rows = jnp.asarray(grouped.T.copy())
 
     send = prepare(info, atmosphere, clouds, col)
     got = lax.all_to_all(send, "seg", 0, 0, tiled=True)
@@ -680,8 +703,7 @@
     )[0]
     rows, got = lax.optimization_barrier((rows, got))
     clouds, mean_1, send = outer(
-        info, base, state, got, got, jnp.asarray(natural), scatter_rows,
-        mean, inv, col, diff, wind, mixing,
+        False, info, base, state, mean, got, got, inv, col, diff, wind, mixing,
     )
     halo = lax.all_to_all(send, "seg", 0, 0, tiled=True)
     base = inner(clouds, col, diff, wind, mixing, False)[0]
@@ -713,8 +735,7 @@
     factors, profile = lax.optimization_barrier((factors, profile))
 
     clouds, _, send = outer(
-        info, base, clouds, profile, halo, gather_rows, scatter_rows,
-        mean_1, inv, col, diff, wind, mixing,
+        True, info, base, clouds, mean_1, profile, halo, inv, col, diff, wind, mixing,
     )
     got = lax.all_to_all(send, "seg", 0, 0, tiled=True)
     from_mine = rows_exchange(

time: 141 us -> 135 us (0.957)
  Pallas kernels: 42.1 us -> 38.6 us
  local copies, waits for them, and re-layouts: 3.42 us -> 1.19 us
    pallas_call x5, Pallas kernels: 24.5 us -> 21.2 us  [call(): pl.pallas_call(kernel, grid_spec=pltpu.PrefetchScalarGridSpec(num_scalar_...]
    unnamed x42 -> x32, local copies, waits for them, and re-layouts: 3.42 us -> 1.19 us
  transfers between devices with their start and end apart: 5 -> 5, of which waited for: 5 -> 5; matrix products, arithmetic and copies ran while one was open for 0% -> 0% of each run, Pallas kernels for 9% -> 10%
where the time goes in v5:
time: 135 us; the launch traced here: 133 us
  blocking collectives  67.6 us (50%)
  Pallas kernels  38.6 us (29%)
  starting transfers between devices  14.4 us (11%)
  waiting for transfers between devices  8.77 us (6%)
  between operations  1.46 us (1%)
    all_to_all x3, blocking collectives, rows_exchange(): lax.all_to_all(x, 'lat', 0, 0, axis_index_groups=ROW_GROUPS, tiled=True)  58.7 us
    pallas_call x5, Pallas kernels, call(): pl.pallas_call(kernel, grid_spec=pltpu.PrefetchScalarGridSpec(num_scalar_...  21.2 us
    pallas_call x2, Pallas kernels, inner(): pl.pallas_call(lambda *refs: inner_kernel(with_mean, *refs), in_specs=[HB...  9.29 us
    all_to_all x1, blocking collectives, shards(): got = lax.all_to_all(send, 'seg', 0, 0, tiled=True)  8.85 us
    pallas_call x5, Pallas kernels, call(): pl.pallas_call(kernel, in_specs=specs, out_specs=outs, scratch_shapes=lis...  5.58 us
    all_to_all x1, starting transfers between devices, shards(): got = lax.all_to_all(send, 'seg', 0, 0, tiled=True)  5.46 us
    all_to_all x1, starting transfers between devices, shards(): halo = lax.all_to_all(send, 'seg', 0, 0, tiled=True)  4.83 us
    all_to_all x1, starting transfers between devices, shards(): profile = lax.all_to_all(profile, 'seg', 0, 0, tiled=True)  4.07 us
  transfers between devices with their start and end apart: 5, of which 5 were waited for; matrix products, arithmetic and copies ran while one was open for 0% of the time, Pallas kernels for 10%

profile of v5, /device:TPU:32, one launch (start us, length us, event | category | flops | bytes accessed | tf_op | source)
XLA Modules:
  0.0 132.5 jit_solution(2109005957353535942)
XLA Ops:
  1.3 0.6 pad_add_fusion.info.refs_0_
  1.9 0.0 copy-start.2
  1.9 2.5 %prepare.1 = f32[8,24,128]{2,1,0:T(8,128)} custom-call(s32[3]{0:T(128)} %pad_add_fusion.info.refs_0_, f32[12,12,768]{2,1,0:T(8,128)} %grid_ref, f32[96,6144]{1,0:T(8,128)} %bitcast.9, f32[96,6144]{1,0:T(8,128)} %bitcast.10, s32[1,6144]{1,0:T(1,128)} %refs_7_.3, s32[1,6144]{1,0:T(1,128)} %refs_7_.3), custom_call_target="tpu_custom_call" | custom-call | tf_op jit(solution)/shard_map/prepare/pallas_call | solution.py:197
  4.4 5.5 %all-to-all-start = ((f32[8,24,128]{2,1,0:T(8,128)}), f32[8,24,128]{2,1,0:T(8,128)S(1)}, u32[]{:S(2)}, u32[]{:S(2)}) async-start(f32[8,24,128]{2,1,0:T(8,128)} %prepare.1), calls=%async_computation | async-start | bytes 196608 | tf_op jit(solution)/shard_map/all_to_all | solution.py:697
  9.9 0.0 copy-done.2
  9.9 0.0 copy-done.6
  9.9 0.0 copy-start.13
  9.9 0.6 rows.1.rows_ref
  10.5 0.0 copy-done.7
  10.6 0.0 copy-done.11
  10.6 0.0 copy-done.14
  10.6 0.0 copy-done.15
  10.6 4.8 %inner.2 = (f32[96,6144]{1,0:T(8,128)}, f32[96,128]{1,0:T(8,128)}, f32[8,128]{1,0:T(8,128)S(1)}) custom-call(f32[96,6144]{1,0:T(8,128)} %bitcast.11, s32[1,6144]{1,0:T(1,128)S(1)} %copy-done.11, f32[1,96]{1,0:T(1,128)S(1)} %bitcast.5, f32[1,96]{1,0:T(1,128)S(1)} %copy-done.15, f32[96,96]{1,0:T(8,128)S(1)} %copy-done.7), custom_call_target="tpu_custom_call" | custom-call | flops 1024 | bytes 1024 | tf_op jit(solution)/shard_map/inner/pallas_call | solution.py:301
  15.4 0.9 all-to-all-done.refs_4_.refs_5_
  16.3 0.0 copy-done.13
  16.3 8.8 %outer.2 = (f32[96,6144]{1,0:T(8,128)}, f32[96,128]{1,0:T(8,128)}, f32[8,24,128]{2,1,0:T(8,128)}) custom-call(s32[3]{0:T(128)S(1)} %copy-done.13, f32[96,6144]{1,0:T(8,128)} %get-tuple-element.22.refs_1_, f32[96,6144]{1,0:T(8,128)} %bitcast.12, f32[96,128]{1,0:T(8,128)} %get-tuple-element.23.refs_3_, f32[8,24,128]{2,1,0:T(8,128)S(1)} %all-to-all-done.refs_4_.refs_5_, ...), custom_call_target="tpu_custom_call" | custom-call | flops 1024 | bytes 1024 | tf_op jit(solution)/shard_map/outer/pallas_call | solution.py:509
  25.1 4.8 %all-to-all-start.1 = ((f32[8,24,128]{2,1,0:T(8,128)}), f32[8,24,128]{2,1,0:T(8,128)S(1)}, u32[]{:S(2)}, u32[]{:S(2)}) async-start(f32[8,24,128]{2,1,0:T(8,128)} %get-tuple-element.28), calls=%async_computation.1 | async-start | bytes 196608 | tf_op jit(solution)/shard_map/all_to_all | solution.py:708
  29.9 4.5 %inner.3.refs_1_ = f32[96,6144]{1,0:T(8,128)} custom-call(f32[96,6144]{1,0:T(8,128)} %get-tuple-element.27.refs_0_.refs_2_, f32[1,96]{1,0:T(1,128)S(1)} %bitcast.7, f32[1,96]{1,0:T(1,128)S(1)} %copy-done.15, f32[96,96]{1,0:T(8,128)S(1)} %copy-done.7), custom_call_target="tpu_custom_call" | custom-call | flops 1024 | bytes 1024 | tf_op jit(solution)/shard_map/inner/pallas_call | solution.py:301
  34.4 0.0 copy-start.4
  34.4 2.0 %all-to-all-done.1.got_ref.refs_5_ = f32[8,24,128]{2,1,0:T(8,128)S(1)} async-done(((f32[8,24,128]{2,1,0:T(8,128)}), f32[8,24,128]{2,1,0:T(8,128)S(1)}, u32[]{:S(2)}, u32[]{:S(2)}) %all-to-all-start.1) | async-done | bytes 98336 | tf_op jit(solution)/shard_map/all_to_all | solution.py:708
  36.4 0.0 copy-done
  36.4 1.0 spread.1
  37.4 22.8 %all_to_all.35.mine_ref = f32[16,48,128]{2,1,0:T(8,128)S(1)} all-to-all(f32[16,48,128]{2,1,0:T(8,128)S(1)} %spread.1), channel_id=1, replica_groups={{0,16,32,48,64,80,96,112,128,144,160,176,192,208,224,240},{8,24,40,56,7..., dimensions={0} | all-to-all | bytes 786432 | tf_op jit(solution)/shard_map/all_to_all | solution.py:678
  60.3 0.0 collective-permute-start
  60.3 1.7 %collective-permute-done.others_ref = f32[16,48,128]{2,1,0:T(8,128)S(1)} collective-permute-done((f32[16,48,128]{2,1,0:T(8,128)S(1)}, f32[16,48,128]{2,1,0:T(8,128)S(1)}, u32[]{:S(2)}, u32[]{:S(2)}) %collective-permute-start) | collective-permute-done | bytes 393248 | tf_op jit(solution)/shard_map/ppermute | solution.py:682
  62.0 0.0 copy-done.4
  62.0 0.0 copy-done.9
  62.0 0.0 copy-done.10
  62.0 0.0 copy-done.12
  62.0 1.6 %settle.1 = f32[16,48,128]{2,1,0:T(8,128)S(1)} custom-call(s32[3]{0:T(128)S(1)} %copy-done.13, f32[16,48,128]{2,1,0:T(8,128)S(1)} %all_to_all.35.mine_ref, f32[16,48,128]{2,1,0:T(8,128)S(1)} %collective-permute-done.others_ref, bf16[2,2,256,256]{3,2,1,0:T(8,128)(2,1)S(1)} %copy-done.12, bf16[2,2,256,256]{3,2,1,0:T(8,128)(2,1)S(1)} %copy-done.4, ...), custom_call_target="tpu_custom_call" | custom-call | flops 1024 | bytes 1024 | tf_op jit(solution)/shard_map/settle/pallas_call | solution.py:509
  63.6 18.8 %all_to_all.36.got_ref = f32[16,48,128]{2,1,0:T(8,128)S(1)} all-to-all(f32[16,48,128]{2,1,0:T(8,128)S(1)} %settle.1), channel_id=1, replica_groups={{0,16,32,48,64,80,96,112,128,144,160,176,192,208,224,240},{8,24,40,56,7..., dimensions={0} | all-to-all | bytes 786432 | tf_op jit(solution)/shard_map/all_to_all | solution.py:678
  82.4 0.0 copy-done.3
  82.4 1.1 profile.1
  83.5 4.1 %all-to-all-start.4 = ((f32[8,16,128]{2,1,0:T(8,128)}), f32[8,16,128]{2,1,0:T(8,128)S(1)}, u32[]{:S(2)}, u32[]{:S(2)}) async-start(f32[8,16,128]{2,1,0:T(8,128)} %profile.1), calls=%async_computation.4 | async-start | bytes 131072 | tf_op jit(solution)/shard_map/all_to_all | solution.py:733
  87.6 1.1 copy-done.8
  88.7 1.6 %weights.1.factors = f32[32,16,768]{2,1,0:T(8,128)S(1)} custom-call(s32[3]{0:T(128)S(1)} %copy-done.13, f32[16,48,128]{2,1,0:T(8,128)S(1)} %all_to_all.35.mine_ref, f32[16,48,128]{2,1,0:T(8,128)S(1)} %collective-permute-done.others_ref, bf16[2,2,256,256]{3,2,1,0:T(8,128)(2,1)S(1)} %copy-done.4, bf16[2,256,768]{2,1,0:T(8,128)(2,1)S(1)} %copy-done.8), custom_call_target="tpu_custom_call" | custom-call | flops 1024 | bytes 1024 | tf_op jit(solution)/shard_map/weights/pallas_call | solution.py:509
  90.3 3.6 %all-to-all-done.4.refs_4_ = f32[8,16,128]{2,1,0:T(8,128)S(1)} async-done(((f32[8,16,128]{2,1,0:T(8,128)}), f32[8,16,128]{2,1,0:T(8,128)S(1)}, u32[]{:S(2)}, u32[]{:S(2)}) %all-to-all-start.4) | async-done | bytes 65568 | tf_op jit(solution)/shard_map/all_to_all | solution.py:733
  93.9 8.2 %outer.3 = (f32[96,6144]{1,0:T(8,128)}, f32[96,128]{1,0:T(8,128)}, f32[8,24,128]{2,1,0:T(8,128)S(1)}) custom-call(s32[3]{0:T(128)S(1)} %copy-done.13, f32[96,6144]{1,0:T(8,128)} %inner.3.refs_1_, f32[96,6144]{1,0:T(8,128)} %get-tuple-element.27.refs_0_.refs_2_, f32[96,128]{1,0:T(8,128)} %get-tuple-element.36.refs_3_, ...), custom_call_target="tpu_custom_call" | custom-call | flops 1024 | bytes 1024 | tf_op jit(solution)/shard_map/outer/pallas_call | solution.py:509
  102.1 8.8 %all_to_all.37.got_ref = f32[8,24,128]{2,1,0:T(8,128)S(1)} all-to-all(f32[8,24,128]{2,1,0:T(8,128)S(1)} %get-tuple-element.38), channel_id=1, replica_groups=mesh['lat'=32,'seg'=8] {'seg'}, dimensions={0} | all-to-all | bytes 196608 | tf_op jit(solution)/shard_map/all_to_all | solution.py:740
  110.9 0.0 copy-done.1
  110.9 0.4 last.1
  111.4 0.0 copy-start.5
  111.4 17.0 %all_to_all.38.from_ref = f32[16,24,256]{2,1,0:T(8,128)S(1)} all-to-all(f32[16,24,256]{2,1,0:T(8,128)S(1)} %last.1), channel_id=1, replica_groups={{0,16,32,48,64,80,96,112,128,144,160,176,192,208,224,240},{8,24,40,56,7..., dimensions={0} | all-to-all | bytes 786432 | tf_op jit(solution)/shard_map/all_to_all | solution.py:678
  128.4 0.0 collective-permute-start.1
  128.4 1.1 gather.1.part_ref
  129.5 0.6 collective-permute-done.1.from_ref
  130.1 0.0 copy-done.5
  130.1 2.4 %finish.1 = f32[12,12,768]{2,1,0:T(8,128)} custom-call(f32[3,16,8,256]{3,2,1,0:T(8,128)S(1)} %gather.1.part_ref, f32[32,16,768]{2,1,0:T(8,128)S(1)} %weights.1.factors, f32[16,24,256]{2,1,0:T(8,128)S(1)} %collective-permute-done.1.from_ref, bf16[2,512,768]{2,1,0:T(8,128)(2,1)S(1)} %copy-done.5), custom_call_target="tpu_custom_call" | custom-call | flops 1024 | bytes 1024 | tf_op jit(solution)/shard_map/finish/pallas_call | solution.py:506
  (12 shorter events, 0.0 us)
Async XLA Ops:
  1.9 8.0 %copy-start.2 = (f32[12,12,768]{2,1,0:T(8,128)S(1)}, f32[12,12,768]{2,1,0:T(8,128)}, u32[]{:S(2)}) copy-start(f32[12,12,768]{2,1,0:T(8,128)} %grid_ref) | copy-start | bytes 1327108
  1.9 8.0 %copy-start.6 = (bf16[2,768,512]{2,1,0:T(8,128)(2,1)S(1)}, bf16[2,768,512]{2,1,0:T(8,128)(2,1)}, u32[]{:S(2)}) copy-start(bf16[2,768,512]{2,1,0:T(8,128)(2,1)} %constant.27.clone.table) | copy-start | bytes 4718596
  4.4 6.1 %copy-start.7 = (f32[96,96]{1,0:T(8,128)S(1)}, f32[96,96]{1,0:T(8,128)}, u32[]{:S(2)}) copy-start(f32[96,96]{1,0:T(8,128)} %refs_10_.3) | copy-start | bytes 110596
  4.4 6.1 %copy-start.11 = (s32[1,6144]{1,0:T(1,128)S(1)}, s32[1,6144]{1,0:T(1,128)}, u32[]{:S(2)}) copy-start(s32[1,6144]{1,0:T(1,128)} %refs_7_.3) | copy-start | bytes 73732
  4.4 6.1 %copy-start.14 = (f32[96]{0:T(128)S(1)}, f32[96]{0:T(128)}, u32[]{:S(2)}) copy-start(f32[96]{0:T(128)} %param.21) | copy-start | bytes 1156
  4.4 6.2 %copy-start.15 = (f32[1,96]{1,0:T(1,128)S(1)}, f32[1,96]{1,0:T(1,128)}, u32[]{:S(2)}) copy-start(f32[1,96]{1,0:T(1,128)} %refs_9_.3) | copy-start | bytes 1156
  4.4 11.9 %all-to-all-start = ((f32[8,24,128]{2,1,0:T(8,128)}), f32[8,24,128]{2,1,0:T(8,128)S(1)}, u32[]{:S(2)}, u32[]{:S(2)}) async-start(f32[8,24,128]{2,1,0:T(8,128)} %prepare.1), calls=%async_computation | async-start | bytes 196608 | tf_op jit(solution)/shard_map/all_to_all | solution.py:697
  9.9 6.4 %copy-start.13 = (s32[3]{0:T(128)S(1)}, s32[3]{0:T(128)}, u32[]{:S(2)}) copy-start(s32[3]{0:T(128)} %pad_add_fusion.info.refs_0_) | copy-start | bytes 40
  25.1 11.3 %all-to-all-start.1 = ((f32[8,24,128]{2,1,0:T(8,128)}), f32[8,24,128]{2,1,0:T(8,128)S(1)}, u32[]{:S(2)}, u32[]{:S(2)}) async-start(f32[8,24,128]{2,1,0:T(8,128)} %get-tuple-element.28), calls=%async_computation.1 | async-start | bytes 196608 | tf_op jit(solution)/shard_map/all_to_all | solution.py:708
  29.9 6.4 %copy-start = (bf16[2,1024,512]{2,1,0:T(8,128)(2,1)S(1)}, bf16[2,1024,512]{2,1,0:T(8,128)(2,1)}, u32[]{:S(2)}) copy-start(bf16[2,1024,512]{2,1,0:T(8,128)(2,1)} %constant.29.clone.table) | copy-start | bytes 6291460
  34.4 27.6 %copy-start.4 = (bf16[2,2,256,256]{3,2,1,0:T(8,128)(2,1)S(1)}, bf16[2,2,256,256]{3,2,1,0:T(8,128)(2,1)}, u32[]{:S(2)}) copy-start(bf16[2,2,256,256]{3,2,1,0:T(8,128)(2,1)} %constant.32.clone.from_spec) | copy-start | bytes 1572868
  36.4 25.6 %copy-start.9 = (f32[2,3,256,128]{3,2,1,0:T(8,128)S(1)}, f32[2,3,256,128]{3,2,1,0:T(8,128)}, u32[]{:S(2)}) copy-start(f32[2,3,256,128]{3,2,1,0:T(8,128)} %constant.34.clone.twice) | copy-start | bytes 2359300
  36.4 25.6 %copy-start.10 = (f32[2,3,256,128]{3,2,1,0:T(8,128)S(1)}, f32[2,3,256,128]{3,2,1,0:T(8,128)}, u32[]{:S(2)}) copy-start(f32[2,3,256,128]{3,2,1,0:T(8,128)} %constant.33.clone.once) | copy-start | bytes 2359300
  36.4 25.6 %copy-start.12 = (bf16[2,2,256,256]{3,2,1,0:T(8,128)(2,1)S(1)}, bf16[2,2,256,256]{3,2,1,0:T(8,128)(2,1)}, u32[]{:S(2)}) copy-start(bf16[2,2,256,256]{3,2,1,0:T(8,128)(2,1)} %constant.31.clone.to_spec) | copy-start | bytes 1572868
  60.3 22.2 %copy-start.3 = (bf16[2,512,1024]{2,1,0:T(8,128)(2,1)S(1)}, bf16[2,512,1024]{2,1,0:T(8,128)(2,1)}, u32[]{:S(2)}) copy-start(bf16[2,512,1024]{2,1,0:T(8,128)(2,1)} %constant.30.clone.table) | copy-start | bytes 6291460
  60.3 1.7 %collective-permute-start = (f32[16,48,128]{2,1,0:T(8,128)S(1)}, f32[16,48,128]{2,1,0:T(8,128)S(1)}, u32[]{:S(2)}, u32[]{:S(2)}) collective-permute-start(f32[16,48,128]{2,1,0:T(8,128)S(1)} %all_to_all.35.mine_ref), channel_id=1, source_target_pairs={{0,8},{8,0},{16,24},{24,16},{32,40},{40,32},{48,56},{56,48},{64,72... | collective-permute-start | bytes 1179656 | tf_op jit(solution)/shard_map/ppermute | solution.py:682
  83.5 10.4 %all-to-all-start.4 = ((f32[8,16,128]{2,1,0:T(8,128)}), f32[8,16,128]{2,1,0:T(8,128)S(1)}, u32[]{:S(2)}, u32[]{:S(2)}) async-start(f32[8,16,128]{2,1,0:T(8,128)} %profile.1), calls=%async_computation.4 | async-start | bytes 131072 | tf_op jit(solution)/shard_map/all_to_all | solution.py:733
  87.5 1.1 copy-start.8
  93.9 17.0 %copy-start.1 = (bf16[2,1024,512]{2,1,0:T(8,128)(2,1)S(1)}, bf16[2,1024,512]{2,1,0:T(8,128)(2,1)}, u32[]{:S(2)}) copy-start(bf16[2,1024,512]{2,1,0:T(8,128)(2,1)} %constant.29.clone.table) | copy-start | bytes 6291460
  111.4 18.8 %copy-start.5 = (bf16[2,512,768]{2,1,0:T(8,128)(2,1)S(1)}, bf16[2,512,768]{2,1,0:T(8,128)(2,1)}, u32[]{:S(2)}) copy-start(bf16[2,512,768]{2,1,0:T(8,128)(2,1)} %constant.28.clone.table) | copy-start | bytes 4718596
  128.4 1.7 %collective-permute-start.1 = (f32[16,24,256]{2,1,0:T(8,128)S(1)}, f32[16,24,256]{2,1,0:T(8,128)S(1)}, u32[]{:S(2)}, u32[]{:S(2)}) collective-permute-start(f32[16,24,256]{2,1,0:T(8,128)S(1)} %all_to_all.38.from_ref), channel_id=1, source_target_pairs={{0,8},{8,0},{16,24},{24,16},{32,40},{40,32},{48,56},{56,48},{64,72... | collective-permute-start | bytes 1179656 | tf_op jit(solution)/shard_map/ppermute | solution.py:682

commit v6 on v5

--- a/solution.py
+++ b/solution.py
@@ -165,8 +165,8 @@
 
 
 def place(info):
-    lat = info[1]
-    return lax.rem(lat, 2), lax.div(lat, 2), info[2] - lat * LAT_DEV
+    lat = lax.axis_index("lat")
+    return lax.rem(lat, 2), lax.div(lat, 2), info[0]
 
 
 def prepare_kernel(info, row_ref, first_ref, last_ref, colf_ref, coll_ref, send_ref):
@@ -200,7 +200,7 @@
             num_scalar_prefetch=1,
             grid=(1,),
             in_specs=[
-                pl.BlockSpec((1, KD, NLON), lambda i, info: (place(info)[2], 0, 0)),
+                pl.BlockSpec((1, KD, NLON), lambda i, info: (info[0], 0, 0)),
                 pl.BlockSpec((K, 128), lambda i, off: (0, 0)),
                 pl.BlockSpec((K, 128), lambda i, off: (0, last)),
                 pl.BlockSpec((1, 128), lambda i, off: (0, 0)),
@@ -315,7 +315,7 @@
     mixing_ref, out_hbm, end_hbm, send_ref, ext1, ext2, force, ends_ref, mean_ref, end_ref, small_sems,
     out_ref, in_sems, out_sems,
 ):
-    seg = info[0]
+    seg = lax.axis_index("seg")
     reads = pieces(base_hbm, ext1, in_sems, 256)
     ends = [
         pltpu.make_async_copy(
@@ -685,8 +685,7 @@
 def shards(atmosphere, cloud_state, channel_lat, cell_column, channel_wind, diffusivity, mixing):
     tab = {name: jnp.asarray(value) for name, value in tables().items()}
     lat = lax.axis_index("lat").astype(jnp.int32)
-    seg = lax.axis_index("seg").astype(jnp.int32)
-    info = jnp.stack((seg, lat, channel_lat[0]))
+    info = channel_lat - lat * LAT_DEV
     clouds = cloud_state[0]
     col = cell_column
     wind = channel_wind

time: 135 us -> 131 us (0.970)
  Pallas kernels: 38.6 us -> 35.3 us
    pallas_call x5, Pallas kernels: 21.2 us -> 18.5 us  [call(): pl.pallas_call(kernel, grid_spec=pltpu.PrefetchScalarGridSpec(num_scalar_...]
  transfers between devices with their start and end apart: 5 -> 5, of which waited for: 5 -> 5; matrix products, arithmetic and copies ran while one was open for 0% -> 0% of each run, Pallas kernels for 10% -> 9%
where the time goes in v6:
time: 131 us; the launch traced here: 129 us
  blocking collectives  67.8 us (52%)
  Pallas kernels  35.3 us (27%)
  starting transfers between devices  14.3 us (11%)
  waiting for transfers between devices  9.33 us (7%)
  between operations  1.47 us (1%)
    all_to_all x3, blocking collectives, rows_exchange(): lax.all_to_all(x, 'lat', 0, 0, axis_index_groups=ROW_GROUPS, tiled=True)  58.9 us
    pallas_call x5, Pallas kernels, call(): pl.pallas_call(kernel, grid_spec=pltpu.PrefetchScalarGridSpec(num_scalar_...  18.5 us
    pallas_call x2, Pallas kernels, inner(): pl.pallas_call(lambda *refs: inner_kernel(with_mean, *refs), in_specs=[HB...  9.29 us
    all_to_all x1, blocking collectives, shards(): got = lax.all_to_all(send, 'seg', 0, 0, tiled=True)  8.85 us
    pallas_call x5, Pallas kernels, call(): pl.pallas_call(kernel, in_specs=specs, out_specs=outs, scratch_shapes=lis...  5.57 us
    all_to_all x1, starting transfers between devices, shards(): got = lax.all_to_all(send, 'seg', 0, 0, tiled=True)  5.46 us
    all_to_all x1, starting transfers between devices, shards(): halo = lax.all_to_all(send, 'seg', 0, 0, tiled=True)  4.79 us
    all_to_all x1, waiting for transfers between devices, shards(): profile = lax.all_to_all(profile, 'seg', 0, 0, tiled=True)  4.12 us
  transfers between devices with their start and end apart: 5, of which 5 were waited for; matrix products, arithmetic and copies ran while one was open for 0% of the time, Pallas kernels for 9%

profile of v6, /device:TPU:32, one launch (start us, length us, event | category | flops | bytes accessed | tf_op | source)
XLA Modules:
  0.0 129.4 jit_solution(11056714455477920001)
XLA Ops:
  1.3 0.0 copy-start.2
  1.3 0.0 copy-start.6
  1.3 1.9 %prepare.1 = f32[8,24,128]{2,1,0:T(8,128)} custom-call(s32[1]{0:T(128)S(6)} %sub.7.info.refs_0_, f32[12,12,768]{2,1,0:T(8,128)} %grid_ref, f32[96,6144]{1,0:T(8,128)} %bitcast.8, f32[96,6144]{1,0:T(8,128)} %bitcast.9, s32[1,6144]{1,0:T(1,128)} %refs_7_.3, s32[1,6144]{1,0:T(1,128)} %refs_7_.3), custom_call_target="tpu_custom_call" | custom-call | tf_op jit(solution)/shard_map/prepare/pallas_call | solution.py:197
  3.2 0.0 copy-start.7
  3.2 0.0 copy-start.11
  3.2 5.5 %all-to-all-start = ((f32[8,24,128]{2,1,0:T(8,128)}), f32[8,24,128]{2,1,0:T(8,128)S(1)}, u32[]{:S(2)}, u32[]{:S(2)}) async-start(f32[8,24,128]{2,1,0:T(8,128)} %prepare.1), calls=%async_computation | async-start | bytes 196608 | tf_op jit(solution)/shard_map/all_to_all | solution.py:696
  8.7 0.0 copy-done.2
  8.7 0.0 copy-done.6
  8.7 0.6 rows.1.rows_ref
  9.3 0.0 copy-done.7
  9.3 0.0 copy-done.11
  9.3 0.0 copy-done.13
  9.4 0.0 copy-done.14
  9.4 4.8 %inner.2 = (f32[96,6144]{1,0:T(8,128)}, f32[96,128]{1,0:T(8,128)}, f32[8,128]{1,0:T(8,128)S(1)}) custom-call(f32[96,6144]{1,0:T(8,128)} %bitcast.10, s32[1,6144]{1,0:T(1,128)S(1)} %copy-done.11, f32[1,96]{1,0:T(1,128)S(1)} %bitcast.4, f32[1,96]{1,0:T(1,128)S(1)} %copy-done.14, f32[96,96]{1,0:T(8,128)S(1)} %copy-done.7), custom_call_target="tpu_custom_call" | custom-call | flops 1024 | bytes 1024 | tf_op jit(solution)/shard_map/inner/pallas_call | solution.py:301
  14.2 0.9 all-to-all-done.refs_4_.refs_5_
  15.1 8.2 %outer.2 = (f32[96,6144]{1,0:T(8,128)}, f32[96,128]{1,0:T(8,128)}, f32[8,24,128]{2,1,0:T(8,128)}) custom-call(s32[1]{0:T(128)S(6)} %sub.7.info.refs_0_, f32[96,6144]{1,0:T(8,128)} %get-tuple-element.22.refs_1_, f32[96,6144]{1,0:T(8,128)} %bitcast.11, f32[96,128]{1,0:T(8,128)} %get-tuple-element.23.refs_3_, f32[8,24,128]{2,1,0:T(8,128)S(1)} %all-to-all-done.refs_4_.refs_5_, ...), custom_call_target="tpu_custom_call" | custom-call | flops 1024 | bytes 1024 | tf_op jit(solution)/shard_map/outer/pallas_call | solution.py:509
  23.4 4.8 %all-to-all-start.1 = ((f32[8,24,128]{2,1,0:T(8,128)}), f32[8,24,128]{2,1,0:T(8,128)S(1)}, u32[]{:S(2)}, u32[]{:S(2)}) async-start(f32[8,24,128]{2,1,0:T(8,128)} %get-tuple-element.28), calls=%async_computation.1 | async-start | bytes 196608 | tf_op jit(solution)/shard_map/all_to_all | solution.py:707
  28.2 4.5 %inner.3.refs_1_ = f32[96,6144]{1,0:T(8,128)} custom-call(f32[96,6144]{1,0:T(8,128)} %get-tuple-element.27.refs_0_.refs_2_, f32[1,96]{1,0:T(1,128)S(1)} %bitcast.6, f32[1,96]{1,0:T(1,128)S(1)} %copy-done.14, f32[96,96]{1,0:T(8,128)S(1)} %copy-done.7), custom_call_target="tpu_custom_call" | custom-call | flops 1024 | bytes 1024 | tf_op jit(solution)/shard_map/inner/pallas_call | solution.py:301
  32.6 0.0 copy-start.4
  32.6 1.9 %all-to-all-done.1.got_ref.refs_5_ = f32[8,24,128]{2,1,0:T(8,128)S(1)} async-done(((f32[8,24,128]{2,1,0:T(8,128)}), f32[8,24,128]{2,1,0:T(8,128)S(1)}, u32[]{:S(2)}, u32[]{:S(2)}) %all-to-all-start.1) | async-done | bytes 98336 | tf_op jit(solution)/shard_map/all_to_all | solution.py:707
  34.6 0.0 copy-done
  34.6 0.5 spread.1
  35.1 23.0 %all_to_all.35.mine_ref = f32[16,48,128]{2,1,0:T(8,128)S(1)} all-to-all(f32[16,48,128]{2,1,0:T(8,128)S(1)} %spread.1), channel_id=1, replica_groups={{0,16,32,48,64,80,96,112,128,144,160,176,192,208,224,240},{8,24,40,56,7..., dimensions={0} | all-to-all | bytes 786432 | tf_op jit(solution)/shard_map/all_to_all | solution.py:678
  58.1 0.0 collective-permute-start
  58.1 1.7 %collective-permute-done.others_ref = f32[16,48,128]{2,1,0:T(8,128)S(1)} collective-permute-done((f32[16,48,128]{2,1,0:T(8,128)S(1)}, f32[16,48,128]{2,1,0:T(8,128)S(1)}, u32[]{:S(2)}, u32[]{:S(2)}) %collective-permute-start) | collective-permute-done | bytes 393248 | tf_op jit(solution)/shard_map/ppermute | solution.py:682
  59.8 0.0 copy-done.4
  59.8 0.0 copy-done.9
  59.8 0.0 copy-done.10
  59.8 0.0 copy-done.12
  59.8 1.0 settle.1
  60.9 18.8 %all_to_all.36.got_ref = f32[16,48,128]{2,1,0:T(8,128)S(1)} all-to-all(f32[16,48,128]{2,1,0:T(8,128)S(1)} %settle.1), channel_id=1, replica_groups={{0,16,32,48,64,80,96,112,128,144,160,176,192,208,224,240},{8,24,40,56,7..., dimensions={0} | all-to-all | bytes 786432 | tf_op jit(solution)/shard_map/all_to_all | solution.py:678
  79.7 0.0 copy-done.3
  79.7 1.1 profile.1
  80.8 4.1 %all-to-all-start.4 = ((f32[8,16,128]{2,1,0:T(8,128)}), f32[8,16,128]{2,1,0:T(8,128)S(1)}, u32[]{:S(2)}, u32[]{:S(2)}) async-start(f32[8,16,128]{2,1,0:T(8,128)} %profile.1), calls=%async_computation.4 | async-start | bytes 131072 | tf_op jit(solution)/shard_map/all_to_all | solution.py:732
  84.8 1.1 copy-done.8
  85.9 1.1 weights.1.factors
  87.0 4.1 %all-to-all-done.4.refs_4_ = f32[8,16,128]{2,1,0:T(8,128)S(1)} async-done(((f32[8,16,128]{2,1,0:T(8,128)}), f32[8,16,128]{2,1,0:T(8,128)S(1)}, u32[]{:S(2)}, u32[]{:S(2)}) %all-to-all-start.4) | async-done | bytes 65568 | tf_op jit(solution)/shard_map/all_to_all | solution.py:732
  91.2 7.7 %outer.3 = (f32[96,6144]{1,0:T(8,128)}, f32[96,128]{1,0:T(8,128)}, f32[8,24,128]{2,1,0:T(8,128)S(1)}) custom-call(s32[1]{0:T(128)S(6)} %sub.7.info.refs_0_, f32[96,6144]{1,0:T(8,128)} %inner.3.refs_1_, f32[96,6144]{1,0:T(8,128)} %get-tuple-element.27.refs_0_.refs_2_, f32[96,128]{1,0:T(8,128)} %get-tuple-element.36.refs_3_, ...), custom_call_target="tpu_custom_call" | custom-call | flops 1024 | bytes 1024 | tf_op jit(solution)/shard_map/outer/pallas_call | solution.py:509
  98.8 8.8 %all_to_all.37.got_ref = f32[8,24,128]{2,1,0:T(8,128)S(1)} all-to-all(f32[8,24,128]{2,1,0:T(8,128)S(1)} %get-tuple-element.38), channel_id=1, replica_groups=mesh['lat'=32,'seg'=8] {'seg'}, dimensions={0} | all-to-all | bytes 196608 | tf_op jit(solution)/shard_map/all_to_all | solution.py:739
  107.7 0.0 copy-done.1
  107.7 0.4 last.1
  108.1 0.0 copy-start.5
  108.2 17.1 %all_to_all.38.from_ref = f32[16,24,256]{2,1,0:T(8,128)S(1)} all-to-all(f32[16,24,256]{2,1,0:T(8,128)S(1)} %last.1), channel_id=1, replica_groups={{0,16,32,48,64,80,96,112,128,144,160,176,192,208,224,240},{8,24,40,56,7..., dimensions={0} | all-to-all | bytes 786432 | tf_op jit(solution)/shard_map/all_to_all | solution.py:678
  125.3 0.0 collective-permute-start.1
  125.3 1.1 gather.1.part_ref
  126.4 0.6 collective-permute-done.1.from_ref
  127.0 0.0 copy-done.5
  127.0 2.4 %finish.1 = f32[12,12,768]{2,1,0:T(8,128)} custom-call(f32[3,16,8,256]{3,2,1,0:T(8,128)S(1)} %gather.1.part_ref, f32[32,16,768]{2,1,0:T(8,128)S(1)} %weights.1.factors, f32[16,24,256]{2,1,0:T(8,128)S(1)} %collective-permute-done.1.from_ref, bf16[2,512,768]{2,1,0:T(8,128)(2,1)S(1)} %copy-done.5), custom_call_target="tpu_custom_call" | custom-call | flops 1024 | bytes 1024 | tf_op jit(solution)/shard_map/finish/pallas_call | solution.py:506
  (9 shorter events, 0.0 us)
Async XLA Ops:
  1.3 7.4 %copy-start.2 = (f32[12,12,768]{2,1,0:T(8,128)S(1)}, f32[12,12,768]{2,1,0:T(8,128)}, u32[]{:S(2)}) copy-start(f32[12,12,768]{2,1,0:T(8,128)} %grid_ref) | copy-start | bytes 1327108
  1.3 7.4 %copy-start.6 = (bf16[2,768,512]{2,1,0:T(8,128)(2,1)S(1)}, bf16[2,768,512]{2,1,0:T(8,128)(2,1)}, u32[]{:S(2)}) copy-start(bf16[2,768,512]{2,1,0:T(8,128)(2,1)} %constant.26.clone.table) | copy-start | bytes 4718596
  3.2 6.1 %copy-start.7 = (f32[96,96]{1,0:T(8,128)S(1)}, f32[96,96]{1,0:T(8,128)}, u32[]{:S(2)}) copy-start(f32[96,96]{1,0:T(8,128)} %refs_10_.3) | copy-start | bytes 110596
  3.2 6.1 %copy-start.11 = (s32[1,6144]{1,0:T(1,128)S(1)}, s32[1,6144]{1,0:T(1,128)}, u32[]{:S(2)}) copy-start(s32[1,6144]{1,0:T(1,128)} %refs_7_.3) | copy-start | bytes 73732
  3.2 6.1 %copy-start.13 = (f32[96]{0:T(128)S(1)}, f32[96]{0:T(128)}, u32[]{:S(2)}) copy-start(f32[96]{0:T(128)} %param.21) | copy-start | bytes 1156
  3.2 6.1 %copy-start.14 = (f32[1,96]{1,0:T(1,128)S(1)}, f32[1,96]{1,0:T(1,128)}, u32[]{:S(2)}) copy-start(f32[1,96]{1,0:T(1,128)} %refs_9_.3) | copy-start | bytes 1156
  3.2 11.9 %all-to-all-start = ((f32[8,24,128]{2,1,0:T(8,128)}), f32[8,24,128]{2,1,0:T(8,128)S(1)}, u32[]{:S(2)}, u32[]{:S(2)}) async-start(f32[8,24,128]{2,1,0:T(8,128)} %prepare.1), calls=%async_computation | async-start | bytes 196608 | tf_op jit(solution)/shard_map/all_to_all | solution.py:696
  23.4 11.2 %all-to-all-start.1 = ((f32[8,24,128]{2,1,0:T(8,128)}), f32[8,24,128]{2,1,0:T(8,128)S(1)}, u32[]{:S(2)}, u32[]{:S(2)}) async-start(f32[8,24,128]{2,1,0:T(8,128)} %get-tuple-element.28), calls=%async_computation.1 | async-start | bytes 196608 | tf_op jit(solution)/shard_map/all_to_all | solution.py:707
  28.2 6.4 %copy-start = (bf16[2,1024,512]{2,1,0:T(8,128)(2,1)S(1)}, bf16[2,1024,512]{2,1,0:T(8,128)(2,1)}, u32[]{:S(2)}) copy-start(bf16[2,1024,512]{2,1,0:T(8,128)(2,1)} %constant.28.clone.table) | copy-start | bytes 6291460
  32.6 27.2 %copy-start.4 = (bf16[2,2,256,256]{3,2,1,0:T(8,128)(2,1)S(1)}, bf16[2,2,256,256]{3,2,1,0:T(8,128)(2,1)}, u32[]{:S(2)}) copy-start(bf16[2,2,256,256]{3,2,1,0:T(8,128)(2,1)} %constant.31.clone.from_spec) | copy-start | bytes 1572868
  34.6 25.2 %copy-start.9 = (f32[2,3,256,128]{3,2,1,0:T(8,128)S(1)}, f32[2,3,256,128]{3,2,1,0:T(8,128)}, u32[]{:S(2)}) copy-start(f32[2,3,256,128]{3,2,1,0:T(8,128)} %constant.33.clone.twice) | copy-start | bytes 2359300
  34.6 25.2 %copy-start.10 = (f32[2,3,256,128]{3,2,1,0:T(8,128)S(1)}, f32[2,3,256,128]{3,2,1,0:T(8,128)}, u32[]{:S(2)}) copy-start(f32[2,3,256,128]{3,2,1,0:T(8,128)} %constant.32.clone.once) | copy-start | bytes 2359300
  34.6 25.2 %copy-start.12 = (bf16[2,2,256,256]{3,2,1,0:T(8,128)(2,1)S(1)}, bf16[2,2,256,256]{3,2,1,0:T(8,128)(2,1)}, u32[]{:S(2)}) copy-start(bf16[2,2,256,256]{3,2,1,0:T(8,128)(2,1)} %constant.30.clone.to_spec) | copy-start | bytes 1572868
  58.1 21.6 %copy-start.3 = (bf16[2,512,1024]{2,1,0:T(8,128)(2,1)S(1)}, bf16[2,512,1024]{2,1,0:T(8,128)(2,1)}, u32[]{:S(2)}) copy-start(bf16[2,512,1024]{2,1,0:T(8,128)(2,1)} %constant.29.clone.table) | copy-start | bytes 6291460
  58.1 1.7 %collective-permute-start = (f32[16,48,128]{2,1,0:T(8,128)S(1)}, f32[16,48,128]{2,1,0:T(8,128)S(1)}, u32[]{:S(2)}, u32[]{:S(2)}) collective-permute-start(f32[16,48,128]{2,1,0:T(8,128)S(1)} %all_to_all.35.mine_ref), channel_id=1, source_target_pairs={{0,8},{8,0},{16,24},{24,16},{32,40},{40,32},{48,56},{56,48},{64,72... | collective-permute-start | bytes 1179656 | tf_op jit(solution)/shard_map/ppermute | solution.py:682
  80.8 10.4 %all-to-all-start.4 = ((f32[8,16,128]{2,1,0:T(8,128)}), f32[8,16,128]{2,1,0:T(8,128)S(1)}, u32[]{:S(2)}, u32[]{:S(2)}) async-start(f32[8,16,128]{2,1,0:T(8,128)} %profile.1), calls=%async_computation.4 | async-start | bytes 131072 | tf_op jit(solution)/shard_map/all_to_all | solution.py:732
  84.8 1.1 copy-start.8
  91.2 16.5 %copy-start.1 = (bf16[2,1024,512]{2,1,0:T(8,128)(2,1)S(1)}, bf16[2,1024,512]{2,1,0:T(8,128)(2,1)}, u32[]{:S(2)}) copy-start(bf16[2,1024,512]{2,1,0:T(8,128)(2,1)} %constant.28.clone.table) | copy-start | bytes 6291460
  108.1 18.9 %copy-start.5 = (bf16[2,512,768]{2,1,0:T(8,128)(2,1)S(1)}, bf16[2,512,768]{2,1,0:T(8,128)(2,1)}, u32[]{:S(2)}) copy-start(bf16[2,512,768]{2,1,0:T(8,128)(2,1)} %constant.27.clone.table) | copy-start | bytes 4718596
  125.3 1.7 %collective-permute-start.1 = (f32[16,24,256]{2,1,0:T(8,128)S(1)}, f32[16,24,256]{2,1,0:T(8,128)S(1)}, u32[]{:S(2)}, u32[]{:S(2)}) collective-permute-start(f32[16,24,256]{2,1,0:T(8,128)S(1)} %all_to_all.38.from_ref), channel_id=1, source_target_pairs={{0,8},{8,0},{16,24},{24,16},{32,40},{40,32},{48,56},{56,48},{64,72... | collective-permute-start | bytes 1179656 | tf_op jit(solution)/shard_map/ppermute | solution.py:682

commit v7 on v6

--- a/solution.py
+++ b/solution.py
@@ -21,10 +21,10 @@
 SEGS = 8
 TILE = 256
 T2 = 1280
-T3 = 1536
-TI = 1536
+T3 = 2048
+TI = 2048
 EXT = CELLS + 512
-CHUNK = 1536
+CHUNK = 2048
 PIECES = CELLS // CHUNK
 RELAXATION = 0.5
 MIXING_RATE = 0.3

time: 131 us -> 131 us (level)
  no operation moved by 1% of the time
where the time goes in v7:
time: 131 us; the launch traced here: 129 us
  blocking collectives  67.9 us (52%)
  Pallas kernels  35 us (27%)
  starting transfers between devices  14.4 us (11%)
  waiting for transfers between devices  9.28 us (7%)
  between operations  1.47 us (1%)
    all_to_all x3, blocking collectives, rows_exchange(): lax.all_to_all(x, 'lat', 0, 0, axis_index_groups=ROW_GROUPS, tiled=True)  59.1 us
    pallas_call x5, Pallas kernels, call(): pl.pallas_call(kernel, grid_spec=pltpu.PrefetchScalarGridSpec(num_scalar_...  18.2 us
    pallas_call x2, Pallas kernels, inner(): pl.pallas_call(lambda *refs: inner_kernel(with_mean, *refs), in_specs=[HB...  9.35 us
    all_to_all x1, blocking collectives, shards(): got = lax.all_to_all(send, 'seg', 0, 0, tiled=True)  8.84 us
    pallas_call x5, Pallas kernels, call(): pl.pallas_call(kernel, in_specs=specs, out_specs=outs, scratch_shapes=lis...  5.57 us
    all_to_all x1, starting transfers between devices, shards(): got = lax.all_to_all(send, 'seg', 0, 0, tiled=True)  5.46 us
    all_to_all x1, starting transfers between devices, shards(): halo = lax.all_to_all(send, 'seg', 0, 0, tiled=True)  4.84 us
    all_to_all x1, waiting for transfers between devices, shards(): profile = lax.all_to_all(profile, 'seg', 0, 0, tiled=True)  4.12 us
  transfers between devices with their start and end apart: 5, of which 5 were waited for; matrix products, arithmetic and copies ran while one was open for 0% of the time, Pallas kernels for 9%

profile of v7, /device:TPU:32, one launch (start us, length us, event | category | flops | bytes accessed | tf_op | source)
XLA Modules:
  0.0 129.2 jit_solution(14664742729795383754)
XLA Ops:
  1.3 0.0 copy-start.2
  1.3 0.0 copy-start.6
  1.3 1.9 %prepare.1 = f32[8,24,128]{2,1,0:T(8,128)} custom-call(s32[1]{0:T(128)S(6)} %sub.7.info.refs_0_, f32[12,12,768]{2,1,0:T(8,128)} %grid_ref, f32[96,6144]{1,0:T(8,128)} %bitcast.8, f32[96,6144]{1,0:T(8,128)} %bitcast.9, s32[1,6144]{1,0:T(1,128)} %refs_7_.3, s32[1,6144]{1,0:T(1,128)} %refs_7_.3), custom_call_target="tpu_custom_call" | custom-call | tf_op jit(solution)/shard_map/prepare/pallas_call | solution.py:197
  3.2 0.0 copy-start.7
  3.2 0.0 copy-start.11
  3.2 5.5 %all-to-all-start = ((f32[8,24,128]{2,1,0:T(8,128)}), f32[8,24,128]{2,1,0:T(8,128)S(1)}, u32[]{:S(2)}, u32[]{:S(2)}) async-start(f32[8,24,128]{2,1,0:T(8,128)} %prepare.1), calls=%async_computation | async-start | bytes 196608 | tf_op jit(solution)/shard_map/all_to_all | solution.py:696
  8.7 0.0 copy-done.2
  8.7 0.0 copy-done.6
  8.7 0.6 rows.1.rows_ref
  9.3 0.0 copy-done.7
  9.3 0.0 copy-done.11
  9.3 0.0 copy-done.13
  9.4 0.0 copy-done.14
  9.4 4.9 %inner.2 = (f32[96,6144]{1,0:T(8,128)}, f32[96,128]{1,0:T(8,128)}, f32[8,128]{1,0:T(8,128)S(1)}) custom-call(f32[96,6144]{1,0:T(8,128)} %bitcast.10, s32[1,6144]{1,0:T(1,128)S(1)} %copy-done.11, f32[1,96]{1,0:T(1,128)S(1)} %bitcast.4, f32[1,96]{1,0:T(1,128)S(1)} %copy-done.14, f32[96,96]{1,0:T(8,128)S(1)} %copy-done.7), custom_call_target="tpu_custom_call" | custom-call | flops 1024 | bytes 1024 | tf_op jit(solution)/shard_map/inner/pallas_call | solution.py:301
  14.2 0.9 all-to-all-done.refs_4_.refs_5_
  15.1 8.0 %outer.2 = (f32[96,6144]{1,0:T(8,128)}, f32[96,128]{1,0:T(8,128)}, f32[8,24,128]{2,1,0:T(8,128)}) custom-call(s32[1]{0:T(128)S(6)} %sub.7.info.refs_0_, f32[96,6144]{1,0:T(8,128)} %get-tuple-element.22.refs_1_, f32[96,6144]{1,0:T(8,128)} %bitcast.11, f32[96,128]{1,0:T(8,128)} %get-tuple-element.23.refs_3_, f32[8,24,128]{2,1,0:T(8,128)S(1)} %all-to-all-done.refs_4_.refs_5_, ...), custom_call_target="tpu_custom_call" | custom-call | flops 1024 | bytes 1024 | tf_op jit(solution)/shard_map/outer/pallas_call | solution.py:509
  23.1 4.8 %all-to-all-start.1 = ((f32[8,24,128]{2,1,0:T(8,128)}), f32[8,24,128]{2,1,0:T(8,128)S(1)}, u32[]{:S(2)}, u32[]{:S(2)}) async-start(f32[8,24,128]{2,1,0:T(8,128)} %get-tuple-element.28), calls=%async_computation.1 | async-start | bytes 196608 | tf_op jit(solution)/shard_map/all_to_all | solution.py:707
  28.0 4.5 %inner.3.refs_1_ = f32[96,6144]{1,0:T(8,128)} custom-call(f32[96,6144]{1,0:T(8,128)} %get-tuple-element.27.refs_0_.refs_2_, f32[1,96]{1,0:T(1,128)S(1)} %bitcast.6, f32[1,96]{1,0:T(1,128)S(1)} %copy-done.14, f32[96,96]{1,0:T(8,128)S(1)} %copy-done.7), custom_call_target="tpu_custom_call" | custom-call | flops 1024 | bytes 1024 | tf_op jit(solution)/shard_map/inner/pallas_call | solution.py:301
  32.5 0.0 copy-start.4
  32.5 1.9 %all-to-all-done.1.got_ref.refs_5_ = f32[8,24,128]{2,1,0:T(8,128)S(1)} async-done(((f32[8,24,128]{2,1,0:T(8,128)}), f32[8,24,128]{2,1,0:T(8,128)S(1)}, u32[]{:S(2)}, u32[]{:S(2)}) %all-to-all-start.1) | async-done | bytes 98336 | tf_op jit(solution)/shard_map/all_to_all | solution.py:707
  34.4 0.0 copy-done
  34.4 0.5 spread.1
  34.9 23.1 %all_to_all.35.mine_ref = f32[16,48,128]{2,1,0:T(8,128)S(1)} all-to-all(f32[16,48,128]{2,1,0:T(8,128)S(1)} %spread.1), channel_id=1, replica_groups={{0,16,32,48,64,80,96,112,128,144,160,176,192,208,224,240},{8,24,40,56,7..., dimensions={0} | all-to-all | bytes 786432 | tf_op jit(solution)/shard_map/all_to_all | solution.py:678
  58.1 0.0 collective-permute-start
  58.1 1.7 %collective-permute-done.others_ref = f32[16,48,128]{2,1,0:T(8,128)S(1)} collective-permute-done((f32[16,48,128]{2,1,0:T(8,128)S(1)}, f32[16,48,128]{2,1,0:T(8,128)S(1)}, u32[]{:S(2)}, u32[]{:S(2)}) %collective-permute-start) | collective-permute-done | bytes 393248 | tf_op jit(solution)/shard_map/ppermute | solution.py:682
  59.8 0.0 copy-done.4
  59.8 0.0 copy-done.9
  59.8 0.0 copy-done.10
  59.8 0.0 copy-done.12
  59.8 1.0 settle.1
  60.9 18.8 %all_to_all.36.got_ref = f32[16,48,128]{2,1,0:T(8,128)S(1)} all-to-all(f32[16,48,128]{2,1,0:T(8,128)S(1)} %settle.1), channel_id=1, replica_groups={{0,16,32,48,64,80,96,112,128,144,160,176,192,208,224,240},{8,24,40,56,7..., dimensions={0} | all-to-all | bytes 786432 | tf_op jit(solution)/shard_map/all_to_all | solution.py:678
  79.7 0.0 copy-done.3
  79.7 1.1 profile.1
  80.8 4.1 %all-to-all-start.4 = ((f32[8,16,128]{2,1,0:T(8,128)}), f32[8,16,128]{2,1,0:T(8,128)S(1)}, u32[]{:S(2)}, u32[]{:S(2)}) async-start(f32[8,16,128]{2,1,0:T(8,128)} %profile.1), calls=%async_computation.4 | async-start | bytes 131072 | tf_op jit(solution)/shard_map/all_to_all | solution.py:732
  84.8 1.1 copy-done.8
  86.0 1.1 weights.1.factors
  87.1 4.1 %all-to-all-done.4.refs_4_ = f32[8,16,128]{2,1,0:T(8,128)S(1)} async-done(((f32[8,16,128]{2,1,0:T(8,128)}), f32[8,16,128]{2,1,0:T(8,128)S(1)}, u32[]{:S(2)}, u32[]{:S(2)}) %all-to-all-start.4) | async-done | bytes 65568 | tf_op jit(solution)/shard_map/all_to_all | solution.py:732
  91.2 7.5 %outer.3 = (f32[96,6144]{1,0:T(8,128)}, f32[96,128]{1,0:T(8,128)}, f32[8,24,128]{2,1,0:T(8,128)S(1)}) custom-call(s32[1]{0:T(128)S(6)} %sub.7.info.refs_0_, f32[96,6144]{1,0:T(8,128)} %inner.3.refs_1_, f32[96,6144]{1,0:T(8,128)} %get-tuple-element.27.refs_0_.refs_2_, f32[96,128]{1,0:T(8,128)} %get-tuple-element.36.refs_3_, ...), custom_call_target="tpu_custom_call" | custom-call | flops 1024 | bytes 1024 | tf_op jit(solution)/shard_map/outer/pallas_call | solution.py:509
  98.7 8.8 %all_to_all.37.got_ref = f32[8,24,128]{2,1,0:T(8,128)S(1)} all-to-all(f32[8,24,128]{2,1,0:T(8,128)S(1)} %get-tuple-element.38), channel_id=1, replica_groups=mesh['lat'=32,'seg'=8] {'seg'}, dimensions={0} | all-to-all | bytes 196608 | tf_op jit(solution)/shard_map/all_to_all | solution.py:739
  107.6 0.0 copy-done.1
  107.6 0.4 last.1
  108.0 0.0 copy-start.5
  108.0 17.1 %all_to_all.38.from_ref = f32[16,24,256]{2,1,0:T(8,128)S(1)} all-to-all(f32[16,24,256]{2,1,0:T(8,128)S(1)} %last.1), channel_id=1, replica_groups={{0,16,32,48,64,80,96,112,128,144,160,176,192,208,224,240},{8,24,40,56,7..., dimensions={0} | all-to-all | bytes 786432 | tf_op jit(solution)/shard_map/all_to_all | solution.py:678
  125.1 0.0 collective-permute-start.1
  125.1 1.1 gather.1.part_ref
  126.2 0.6 collective-permute-done.1.from_ref
  126.8 0.0 copy-done.5
  126.9 2.4 %finish.1 = f32[12,12,768]{2,1,0:T(8,128)} custom-call(f32[3,16,8,256]{3,2,1,0:T(8,128)S(1)} %gather.1.part_ref, f32[32,16,768]{2,1,0:T(8,128)S(1)} %weights.1.factors, f32[16,24,256]{2,1,0:T(8,128)S(1)} %collective-permute-done.1.from_ref, bf16[2,512,768]{2,1,0:T(8,128)(2,1)S(1)} %copy-done.5), custom_call_target="tpu_custom_call" | custom-call | flops 1024 | bytes 1024 | tf_op jit(solution)/shard_map/finish/pallas_call | solution.py:506
  (9 shorter events, 0.0 us)
Async XLA Ops:
  1.3 7.4 %copy-start.2 = (f32[12,12,768]{2,1,0:T(8,128)S(1)}, f32[12,12,768]{2,1,0:T(8,128)}, u32[]{:S(2)}) copy-start(f32[12,12,768]{2,1,0:T(8,128)} %grid_ref) | copy-start | bytes 1327108
  1.3 7.4 %copy-start.6 = (bf16[2,768,512]{2,1,0:T(8,128)(2,1)S(1)}, bf16[2,768,512]{2,1,0:T(8,128)(2,1)}, u32[]{:S(2)}) copy-start(bf16[2,768,512]{2,1,0:T(8,128)(2,1)} %constant.26.clone.table) | copy-start | bytes 4718596
  3.2 6.1 %copy-start.7 = (f32[96,96]{1,0:T(8,128)S(1)}, f32[96,96]{1,0:T(8,128)}, u32[]{:S(2)}) copy-start(f32[96,96]{1,0:T(8,128)} %refs_10_.3) | copy-start | bytes 110596
  3.2 6.1 %copy-start.11 = (s32[1,6144]{1,0:T(1,128)S(1)}, s32[1,6144]{1,0:T(1,128)}, u32[]{:S(2)}) copy-start(s32[1,6144]{1,0:T(1,128)} %refs_7_.3) | copy-start | bytes 73732
  3.2 6.1 %copy-start.13 = (f32[96]{0:T(128)S(1)}, f32[96]{0:T(128)}, u32[]{:S(2)}) copy-start(f32[96]{0:T(128)} %param.21) | copy-start | bytes 1156
  3.2 6.1 %copy-start.14 = (f32[1,96]{1,0:T(1,128)S(1)}, f32[1,96]{1,0:T(1,128)}, u32[]{:S(2)}) copy-start(f32[1,96]{1,0:T(1,128)} %refs_9_.3) | copy-start | bytes 1156
  3.2 11.9 %all-to-all-start = ((f32[8,24,128]{2,1,0:T(8,128)}), f32[8,24,128]{2,1,0:T(8,128)S(1)}, u32[]{:S(2)}, u32[]{:S(2)}) async-start(f32[8,24,128]{2,1,0:T(8,128)} %prepare.1), calls=%async_computation | async-start | bytes 196608 | tf_op jit(solution)/shard_map/all_to_all | solution.py:696
  23.1 11.3 %all-to-all-start.1 = ((f32[8,24,128]{2,1,0:T(8,128)}), f32[8,24,128]{2,1,0:T(8,128)S(1)}, u32[]{:S(2)}, u32[]{:S(2)}) async-start(f32[8,24,128]{2,1,0:T(8,128)} %get-tuple-element.28), calls=%async_computation.1 | async-start | bytes 196608 | tf_op jit(solution)/shard_map/all_to_all | solution.py:707
  28.0 6.4 %copy-start = (bf16[2,1024,512]{2,1,0:T(8,128)(2,1)S(1)}, bf16[2,1024,512]{2,1,0:T(8,128)(2,1)}, u32[]{:S(2)}) copy-start(bf16[2,1024,512]{2,1,0:T(8,128)(2,1)} %constant.28.clone.table) | copy-start | bytes 6291460
  32.5 27.3 %copy-start.4 = (bf16[2,2,256,256]{3,2,1,0:T(8,128)(2,1)S(1)}, bf16[2,2,256,256]{3,2,1,0:T(8,128)(2,1)}, u32[]{:S(2)}) copy-start(bf16[2,2,256,256]{3,2,1,0:T(8,128)(2,1)} %constant.31.clone.from_spec) | copy-start | bytes 1572868
  34.4 25.4 %copy-start.9 = (f32[2,3,256,128]{3,2,1,0:T(8,128)S(1)}, f32[2,3,256,128]{3,2,1,0:T(8,128)}, u32[]{:S(2)}) copy-start(f32[2,3,256,128]{3,2,1,0:T(8,128)} %constant.33.clone.twice) | copy-start | bytes 2359300
  34.4 25.4 %copy-start.10 = (f32[2,3,256,128]{3,2,1,0:T(8,128)S(1)}, f32[2,3,256,128]{3,2,1,0:T(8,128)}, u32[]{:S(2)}) copy-start(f32[2,3,256,128]{3,2,1,0:T(8,128)} %constant.32.clone.once) | copy-start | bytes 2359300
  34.4 25.4 %copy-start.12 = (bf16[2,2,256,256]{3,2,1,0:T(8,128)(2,1)S(1)}, bf16[2,2,256,256]{3,2,1,0:T(8,128)(2,1)}, u32[]{:S(2)}) copy-start(bf16[2,2,256,256]{3,2,1,0:T(8,128)(2,1)} %constant.30.clone.to_spec) | copy-start | bytes 1572868
  58.1 21.6 %copy-start.3 = (bf16[2,512,1024]{2,1,0:T(8,128)(2,1)S(1)}, bf16[2,512,1024]{2,1,0:T(8,128)(2,1)}, u32[]{:S(2)}) copy-start(bf16[2,512,1024]{2,1,0:T(8,128)(2,1)} %constant.29.clone.table) | copy-start | bytes 6291460
  58.1 1.7 %collective-permute-start = (f32[16,48,128]{2,1,0:T(8,128)S(1)}, f32[16,48,128]{2,1,0:T(8,128)S(1)}, u32[]{:S(2)}, u32[]{:S(2)}) collective-permute-start(f32[16,48,128]{2,1,0:T(8,128)S(1)} %all_to_all.35.mine_ref), channel_id=1, source_target_pairs={{0,8},{8,0},{16,24},{24,16},{32,40},{40,32},{48,56},{56,48},{64,72... | collective-permute-start | bytes 1179656 | tf_op jit(solution)/shard_map/ppermute | solution.py:682
  80.8 10.4 %all-to-all-start.4 = ((f32[8,16,128]{2,1,0:T(8,128)}), f32[8,16,128]{2,1,0:T(8,128)S(1)}, u32[]{:S(2)}, u32[]{:S(2)}) async-start(f32[8,16,128]{2,1,0:T(8,128)} %profile.1), calls=%async_computation.4 | async-start | bytes 131072 | tf_op jit(solution)/shard_map/all_to_all | solution.py:732
  84.8 1.1 copy-start.8
  91.2 16.4 %copy-start.1 = (bf16[2,1024,512]{2,1,0:T(8,128)(2,1)S(1)}, bf16[2,1024,512]{2,1,0:T(8,128)(2,1)}, u32[]{:S(2)}) copy-start(bf16[2,1024,512]{2,1,0:T(8,128)(2,1)} %constant.28.clone.table) | copy-start | bytes 6291460
  108.0 18.8 %copy-start.5 = (bf16[2,512,768]{2,1,0:T(8,128)(2,1)S(1)}, bf16[2,512,768]{2,1,0:T(8,128)(2,1)}, u32[]{:S(2)}) copy-start(bf16[2,512,768]{2,1,0:T(8,128)(2,1)} %constant.27.clone.table) | copy-start | bytes 4718596
  125.1 1.7 %collective-permute-start.1 = (f32[16,24,256]{2,1,0:T(8,128)S(1)}, f32[16,24,256]{2,1,0:T(8,128)S(1)}, u32[]{:S(2)}, u32[]{:S(2)}) collective-permute-start(f32[16,24,256]{2,1,0:T(8,128)S(1)} %all_to_all.38.from_ref), channel_id=1, source_target_pairs={{0,8},{8,0},{16,24},{24,16},{32,40},{40,32},{48,56},{56,48},{64,72... | collective-permute-start | bytes 1179656 | tf_op jit(solution)/shard_map/ppermute | solution.py:682
